TPU v7x, 256 devices: a whole 4x4x8 slice. The times are simulated.
256 devices in a mesh: tile: 16 (over y, z_hi, core), band: 16 (over z_lo, x).
Axes of the slice: x: 4, y: 4, z: 8 (z_hi: 2, z_lo: 4; z = z_hi * 4 + z_lo), core: 2. Of those that a mesh axis runs over, the one named last changes fastest.
Arguments:
- features: bfloat16 [1024, 96, 512], P(('tile', 'band')), may hold values from -6 to 6
- occupancy: int32 [1024, 512], P(('tile', 'band')), may hold values 0 or 1
- weights: bfloat16 [27, 96, 96], replicated, may hold values from -0.125 to 0.125
- grad_out: bfloat16 [1024, 96, 512], P(('tile', 'band')), may hold values from -6 to 6
- lat_src: int32 [1024, 4], P(('tile', 'band')), may hold values from -1 to 23, as said below
- down_src: int32 [1024], P(('tile', 'band')), may hold values from -1 to 3, as said below
- up_src: int32 [1024], P(('tile', 'band')), may hold values from -1 to 3, as said below
- send_faces: int32 [256, 4, 2], P(('tile', 'band')), may hold values from 0 to 15, as said below
Outputs:
- layer_out: bfloat16 [1024, 96, 512], P(('tile', 'band'))
- input_grad: bfloat16 [1024, 96, 512], P(('tile', 'band'))
- weight_grad: float32 [27, 96, 96], replicated
Inputs may be any that keep to these rules, and one draw needn't show every extreme that they name: `lat_src`: neighbour relations are mutual: a block's side slab comes from the block whose opposite side takes this block's face. A cross-tile neighbour of a block in tile t lies in tile t XOR 2^k for some round k, and in round k every device sends exactly 2 faces to that tile, the ones that tile's entries name. `send_faces`: entries are codes f * 4 + j of face f < 4 of local block j. `down_src`: mutual with up_src; -1 in the lowest band. `up_src`: mutual with down_src; -1 in the highest band.
All inputs are finite; a program needn't handle non-finite values. No bound on the sum of `occupancy` on one device may be relied on, other than what follows from the above.
Results may differ from a plain program's by a relative error of at most 0.0029.
Values may be sent and summed in bfloat16 or wider, within the bound.
No kernel may reach another device: no remote copies, remote signals or barrier semaphores. Data moves between devices by JAX's collectives and lax.ppermute only.
A program may use at most 128 MiB of HBM per device.

v0:
```python
import math

import jax
import jax.numpy as jnp
import numpy as np
from jax import lax
from jax.sharding import PartitionSpec as P

margin_cells = 111


def swapped(value, axis, distance):
    mask = 2**distance
    pairs = [(source, source ^ mask) for source in range(lax.axis_size(axis))]
    return lax.ppermute(value, axis, pairs)


def extended_2(block, sides, width):
    for axis, dim in sides:
        count = lax.axis_size(axis)
        forward = [(i, i + 1) for i in range(count - 1)]
        backward = [(target, source) for source, target in forward]
        low = lax.ppermute(
            lax.slice_in_dim(block, block.shape[dim] - width, None, axis=dim), axis, forward
        )
        high = lax.ppermute(lax.slice_in_dim(block, 0, width, axis=dim), axis, backward)
        block = jnp.concatenate([low, block, high], axis=dim)
    return block


def face_table():
    table = []
    for face_index in range(6):
        for first in range(8):
            for second in range(8):
                if face_index < 2:
                    table.append(448 * face_index + 8 * first + second)
                elif face_index < 4:
                    table.append(64 * first + 56 * (face_index - 2) + second)
                else:
                    table.append(64 * first + 8 * second + 7 * (face_index - 4))
    return np.array(table, np.int32)


def extended_table():
    zero_slot = 896
    table = np.full(1000 + 2 * margin_cells, zero_slot, np.int32)
    for place in range(1000):
        pos_x, pos_y, pos_z = (place // 100, place // 10 % 10, place % 10)
        in_x, in_y, in_z = (1 <= pos_x <= 8, 1 <= pos_y <= 8, 1 <= pos_z <= 8)
        value = zero_slot
        if in_x and in_y and in_z:
            value = 64 * (pos_x - 1) + 8 * (pos_y - 1) + (pos_z - 1)
        elif in_y and in_z and (not in_x):
            value = 512 + (0 if pos_x == 0 else 64) + 8 * (pos_y - 1) + (pos_z - 1)
        elif in_x and in_z and (not in_y):
            value = 512 + (128 if pos_y == 0 else 192) + 8 * (pos_x - 1) + (pos_z - 1)
        elif in_x and in_y and (not in_z):
            value = 512 + (256 if pos_z == 0 else 320) + 8 * (pos_x - 1) + (pos_y - 1)
        table[place + margin_cells] = value
    return table


def interior_table():
    return np.array(
        [100 * (v // 64 + 1) + 10 * (v // 8 % 8 + 1) + (v % 8 + 1) for v in range(512)], np.int32
    )


def spread_table():
    table = np.full(1000, 512, np.int32)
    table[interior_table()] = np.arange(512, dtype=np.int32)
    return table


def tap_offset(tap_index):
    return 100 * (tap_index // 9) + 10 * (tap_index // 3 % 3) + tap_index % 3


def build_extended(flat_data, slabs):
    num_blocks, channels = (flat_data.shape[0], flat_data.shape[1])
    side_rows = slabs.transpose(1, 2, 0, 3).reshape(num_blocks, channels, 384)
    source = jnp.concatenate(
        [flat_data, side_rows, jnp.zeros((num_blocks, channels, 1), flat_data.dtype)], axis=2
    )
    return jnp.take(source, jnp.asarray(extended_table()), axis=2)


def convolve(extended, weights):
    total = None
    for tap_index in range(27):
        offset = tap_offset(tap_index)
        term = jnp.einsum(
            "bcp,co->bop",
            extended[:, :, offset : offset + 1000],
            weights[tap_index],
            preferred_element_type=jnp.float32,
        )
        total = term if total is None else total + term
    return jnp.take(total, jnp.asarray(interior_table()), axis=2)


def group_term(extended, delta_spread, group_index):
    terms = []
    for tap_index in range(3 * group_index, 3 * group_index + 3):
        offset = tap_offset(tap_index)
        terms.append(
            jnp.einsum(
                "bcp,bop->co",
                extended[:, :, offset : offset + 1000],
                delta_spread,
                preferred_element_type=jnp.float32,
            )
        )
    return jnp.stack(terms)


def gather_slabs(flat_data, lat_src, down_src, up_src, send_faces):
    num_blocks, channels = (flat_data.shape[0], flat_data.shape[1])
    face_set = (
        jnp.take(flat_data, jnp.asarray(face_table()), axis=2)
        .reshape(num_blocks, channels, 6, 64)
        .transpose(2, 0, 1, 3)
    )
    rounds = lax.axis_size("tile").bit_length() - 1
    link_count = send_faces.shape[2]
    own_faces = face_set[0:4].reshape(4 * num_blocks, channels, 64)
    outgoing = (
        own_faces[send_faces[0]].transpose(0, 2, 1, 3).reshape(rounds, channels, link_count * 64)
    )
    arrived = jnp.stack(
        [swapped(outgoing[bit_index], "tile", bit_index) for bit_index in range(rounds)]
    )
    received = (
        arrived.reshape(rounds, channels, link_count, 64)
        .transpose(0, 2, 1, 3)
        .reshape(rounds * link_count, channels, 64)
    )
    empty_row = jnp.zeros((1, channels, 64), face_set.dtype)
    face_pool = jnp.concatenate([own_faces, received, empty_row])
    lateral = face_pool[jnp.where(lat_src < 0, face_pool.shape[0] - 1, lat_src)]
    stacked = (
        jnp.stack([face_set[4], face_set[5]])
        .transpose(0, 2, 1, 3)
        .reshape(2, channels, num_blocks * 64)
    )
    extended = extended_2(stacked, (("band", 0),), 1)
    lower_tops = jnp.concatenate(
        [extended[0].reshape(channels, num_blocks, 64).transpose(1, 0, 2), empty_row]
    )
    upper_bottoms = jnp.concatenate(
        [extended[3].reshape(channels, num_blocks, 64).transpose(1, 0, 2), empty_row]
    )
    down_slab = lower_tops[jnp.where(down_src < 0, num_blocks, down_src)]
    up_slab = upper_bottoms[jnp.where(up_src < 0, num_blocks, up_src)]
    return jnp.concatenate([lateral.transpose(1, 0, 2, 3), down_slab[None], up_slab[None]])


def on_device(features, occupancy, weights, grad_out, lat_src, down_src, up_src, send_faces):
    num_blocks, channels, voxels = features.shape
    mask_float = occupancy.astype(jnp.float32)[:, None, :]
    masked = features * occupancy.astype(jnp.bfloat16)[:, None, :]
    extended = build_extended(masked, gather_slabs(masked, lat_src, down_src, up_src, send_faces))
    preact = convolve(extended, weights)
    sigmoid_value = jax.nn.sigmoid(preact)
    layer_out = (features.astype(jnp.float32) + mask_float * (preact * sigmoid_value)).astype(
        jnp.bfloat16
    )
    delta_grad = (
        grad_out.astype(jnp.float32)
        * mask_float
        * (sigmoid_value * (1.0 + preact * (1.0 - sigmoid_value)))
    ).astype(jnp.bfloat16)
    delta_extended = build_extended(
        delta_grad, gather_slabs(delta_grad, lat_src, down_src, up_src, send_faces)
    )
    delta_spread = jnp.take(
        jnp.concatenate(
            [delta_grad, jnp.zeros((num_blocks, channels, 1), delta_grad.dtype)], axis=2
        ),
        jnp.asarray(spread_table()),
        axis=2,
    )
    flipped = jnp.flip(weights, 0).transpose(0, 2, 1)
    back_term = convolve(delta_extended, flipped)
    local_terms = jnp.concatenate(
        [group_term(extended, delta_spread, group_index) for group_index in range(9)]
    )
    weight_total = lax.psum(local_terms, ("tile", "band"))
    input_grad = (grad_out.astype(jnp.float32) + mask_float * back_term).astype(jnp.bfloat16)
    scale = 1.0 / math.sqrt(num_blocks * voxels * lax.axis_size("tile") * lax.axis_size("band"))
    weight_grad = weight_total * scale
    return (layer_out, input_grad, weight_grad)


def solution(mesh):
    return jax.shard_map(
        on_device,
        mesh=mesh,
        in_specs=(
            P(("tile", "band"), None, None),
            P(("tile", "band"), None),
            P(),
            P(("tile", "band"), None, None),
            P(("tile", "band"), None),
            P(("tile", "band")),
            P(("tile", "band")),
            P(("tile", "band"), None, None),
        ),
        out_specs=(P(("tile", "band"), None, None), P(("tile", "band"), None, None), P()),
        check_vma=False,
    )
```

profile of v0, /device:TPU:1, one launch (start us, length us, event | category | flops | bytes accessed | tf_op | source)
XLA Modules:
  0.0 425.7 jit_solution(10019813312716341625)
XLA Ops:
  10.9 2.0 gather_fusion.9
  15.5 3.8 collective-permute-start.3
  20.7 6.9 %collective-permute-start.1 = (bf16[96,128]{0,1:T(8,128)(2,1)S(1)}, bf16[96,128]{0,1:T(8,128)(2,1)S(1)}, u32[]{:S(2)}, u32[]{:S(2)}) collective-permute-start(bf16[96,128]{0,1:T(8,128)(2,1)S(1)} %bitcast.725), channel_id=1, source_target_pairs={{0,32},{16,48},{32,0},{48,16},{64,96},{80,112},{96,64},{112,80},{1... | collective-permute-start | bytes 73736 | tf_op jit(solution)/shard_map/ppermute | solution.py:15
  28.7 4.3 %collective-permute-start.4 = (bf16[1,96,256]{1,2,0:T(8,128)(2,1)S(1)}, bf16[1,96,256]{1,2,0:T(8,128)(2,1)S(1)}, u32[]{:S(2)}, u32[]{:S(2)}) collective-permute-start(bf16[1,96,256]{1,2,0:T(8,128)(2,1)S(1)} %bitcast.715), channel_id=1, source_target_pairs={{0,1},{1,2},{2,3},{3,4},{4,5},{5,6},{6,7},{7,8},{8,9},{9,10},{10,1... | collective-permute-start | bytes 147464 | tf_op jit(solution)/shard_map/ppermute | solution.py:23
  35.9 9.2 %maximum_maximum_fusion = bf16[4,96,897]{1,0,2:T(4,128)(2,1)S(1)} fusion(bf16[4,96,384]{1,0,2:T(4,128)(2,1)S(1)} %copy.219, bf16[4,96,512]{1,0,2:T(4,128)(2,1)S(1)} %broadcast_multiply_fusion.1, bf16[897]{0:T(1024)(128)(2,1)S(1)} %pad.22.clone), kind=kLoop, calls=%fused_computation.91 | loop fusion | flops 688896 | bytes 1378818 | tf_op jit(solution)/shard_map/concatenate | solution.py:83
  45.1 4.4 %gather_fusion.10 = bf16[1222,4,96]{2,1,0:T(4,128)(2,1)S(1)} fusion(bf16[4,96,897]{1,0,2:T(4,128)(2,1)S(1)} %maximum_maximum_fusion, s32[2048]{0:T(1024)S(1)} %pad_clamp_fusion), kind=kCustom, calls=%fused_computation.1.clone | custom fusion | bytes 1881880 | tf_op jit(solution)/shard_map/jit(_take)/gather | solution.py:86
  49.4 1.8 copy.221
  54.1 1.7 fusion.112
  55.8 1.6 fusion.115
  57.4 1.7 fusion.118
  59.1 1.7 fusion.121
  60.8 1.6 fusion.124
  62.4 1.7 fusion.127
  64.2 1.6 fusion.130
  65.8 1.7 fusion.133
  67.5 1.6 fusion.136
  69.1 1.7 fusion.139
  70.8 1.6 fusion.142
  72.4 1.7 fusion.145
  74.1 1.6 fusion.148
  75.7 1.7 fusion.151
  77.4 1.7 fusion.154
  79.1 1.7 fusion.157
  80.8 1.7 fusion.160
  82.5 1.6 fusion.163
  84.1 1.6 fusion.166
  85.8 2.0 fusion.169
  87.8 11.7 %bitcast_add_fusion.10 = f32[4,96,1000]{2,1,0:T(8,128)S(1)} fusion(f32[4,1000,96]{1,2,0:T(8,128)S(1)} %fusion.94, f32[4,1000,96]{1,2,0:T(8,128)S(1)} %fusion.97, f32[4,1000,96]{1,2,0:T(8,128)S(1)} %fusion.100, f32[4,1000,96]{1,2,0:T(8,128)S(1)} %fusion.103, f32[4,1000,96]{1,2,0:T(8,128)S(1)} %fusion.106, f32[4,1000,96]{1,2,0:T(8,128)S(1)} %fusion.109, ...), kind=kOutput, calls=%fused_computation.25 | convolution fusion | flops 83712000 | bytes 42504192 | tf_op jit(solution)/shard_map/bcp,co->bop/dot_general | solution.py:93
  99.5 1.8 copy.249
  101.3 3.1 gather_fusion.11
  104.8 2.2 fusion.28
  107.3 2.0 gather_fusion.12
  111.7 1.6 collective-permute-start.9
  113.3 1.7 collective-permute-start.6
  115.0 1.9 collective-permute-start.7
  116.9 7.7 %gather_fusion.8 = bf16[1000,4,96]{2,1,0:T(4,128)(2,1)} fusion(bf16[4,96,513]{1,0,2:T(4,128)(2,1)S(1)} %concatenate.54.clone, s32[1024]{0:T(1024)S(1)} %get-tuple-element.32), kind=kCustom, calls=%fused_computation.14 | custom fusion | bytes 1540000 | tf_op jit(solution)/shard_map/jit(_take)/gather | solution.py:177
  154.6 4.6 %collective-permute-start.10 = (bf16[1,96,256]{1,2,0:T(8,128)(2,1)S(1)}, bf16[1,96,256]{1,2,0:T(8,128)(2,1)S(1)}, u32[]{:S(2)}, u32[]{:S(2)}) collective-permute-start(bf16[1,96,256]{1,2,0:T(8,128)(2,1)S(1)} %bitcast.713), channel_id=1, source_target_pairs={{0,1},{1,2},{2,3},{3,4},{4,5},{5,6},{6,7},{7,8},{8,9},{9,10},{10,1... | collective-permute-start | bytes 147464 | tf_op jit(solution)/shard_map/ppermute | solution.py:23
  163.2 4.4 %gather_fusion.13 = bf16[1222,4,96]{2,1,0:T(4,128)(2,1)S(1)} fusion(bf16[4,96,897]{1,0,2:T(4,128)(2,1)S(1)} %copy.259, s32[2048]{0:T(1024)S(1)} %pad_clamp_fusion), kind=kCustom, calls=%fused_computation.4.clone | custom fusion | bytes 1881880 | tf_op jit(solution)/shard_map/jit(_take)/gather | solution.py:86
  167.5 1.8 copy.260
  172.1 1.7 fusion.43
  173.8 1.6 fusion.45
  175.4 1.6 fusion.47
  177.1 1.7 fusion.49
  178.8 1.6 fusion.51
  180.4 1.7 fusion.53
  182.1 1.6 fusion.55
  183.7 1.7 fusion.57
  185.4 1.6 fusion.59
  187.0 1.6 fusion.61
  188.6 1.6 fusion.63
  190.3 1.7 fusion.65
  191.9 1.6 fusion.67
  193.5 1.7 fusion.69
  195.2 1.7 fusion.71
  196.9 1.7 fusion.73
  198.6 1.7 fusion.75
  200.2 1.6 fusion.77
  201.9 1.6 fusion.79
  203.5 1.8 fusion.81
  205.3 11.7 %bitcast_add_fusion = f32[4,96,1000]{2,1,0:T(8,128)S(1)} fusion(f32[4,1000,96]{1,2,0:T(8,128)S(1)} %fusion.31, f32[4,1000,96]{1,2,0:T(8,128)S(1)} %fusion.33, f32[4,1000,96]{1,2,0:T(8,128)S(1)} %fusion.35, f32[4,1000,96]{1,2,0:T(8,128)S(1)} %fusion.37, f32[4,1000,96]{1,2,0:T(8,128)S(1)} %fusion.39, f32[4,1000,96]{1,2,0:T(8,128)S(1)} %fusion.41, ...), kind=kOutput, calls=%fused_computation.15 | convolution fusion | flops 83712000 | bytes 42504192 | tf_op jit(solution)/shard_map/bcp,co->bop/dot_general | solution.py:93
  217.0 1.8 copy.261
  218.8 3.1 gather_fusion.14
  223.2 192.8 %all-reduce.7.cloned.1.call-done = f32[27,96,96]{2,1,0:T(8,128)} async-done(((f32[27,96,96]{2,1,0:T(8,128)}), f32[27,96,96]{2,1,0:T(8,128)}) %all-reduce.7.cloned.1.call-update) | async-done | bytes 995344 | tf_op jit(solution)/shard_map/psum | solution.py:189
  415.9 2.5 broadcast_multiply_fusion
  (150 shorter events, 54.9 us)
Async XLA Ops:
  7.2 408.8 %all-reduce.7.cloned.1.call-start = ((), (), s32[]{:S(2)}) async-start(), calls=%async_computation | async-start | bytes 2654208 | tf_op jit(solution)/shard_map/psum | solution.py:189
  10.2 4.4 %copy-start.8 = (s32[1,4,2]{1,2,0:T(2,128)S(1)}, s32[1,4,2]{1,2,0:T(2,128)}, u32[]{:S(2)}) copy-start(s32[1,4,2]{1,2,0:T(2,128)} %param.28) | copy-start | bytes 100
  10.2 4.6 %copy-start.7 = (s32[4,4]{1,0:T(4,128)S(1)}, s32[4,4]{1,0:T(4,128)}, u32[]{:S(2)}) copy-start(s32[4,4]{1,0:T(4,128)} %param.25) | copy-start | bytes 196
  13.0 14.7 %copy-start.9 = (s32[4]{0:T(128)S(1)}, s32[4]{0:T(128)}, u32[]{:S(2)}) copy-start(s32[4]{0:T(128)} %param.26) | copy-start | bytes 52
  13.0 14.7 %copy-start.10 = (s32[4]{0:T(128)S(1)}, s32[4]{0:T(128)}, u32[]{:S(2)}) copy-start(s32[4]{0:T(128)} %param.27) | copy-start | bytes 52
  13.0 14.7 %copy-start.4 = (s32[1222]{0:T(1024)S(1)}, s32[1222]{0:T(1024)}, u32[]{:S(2)}) copy-start(s32[1222]{0:T(1024)} %constant.159) | copy-start | bytes 14668
  13.0 14.7 %copy-start = (bf16[27,96,96]{2,1,0:T(8,128)(2,1)S(1)}, bf16[27,96,96]{2,1,0:T(8,128)(2,1)}, u32[]{:S(2)}) copy-start(bf16[27,96,96]{2,1,0:T(8,128)(2,1)} %param.23) | copy-start | bytes 1492996
  13.1 15.5 %copy-start.5 = (s32[1000]{0:T(1024)S(1)}, s32[1000]{0:T(1024)}, u32[]{:S(2)}) copy-start(s32[1000]{0:T(1024)} %constant.151) | copy-start | bytes 12004
  13.1 15.5 %copy-start.6 = (s32[512]{0:T(512)S(1)}, s32[512]{0:T(512)}, u32[]{:S(2)}) copy-start(s32[512]{0:T(512)} %constant.160) | copy-start | bytes 6148
  13.1 21.1 %collective-permute-start.5 = (bf16[1,96,256]{1,2,0:T(8,128)(2,1)S(1)}, bf16[1,96,256]{1,2,0:T(8,128)(2,1)S(1)}, u32[]{:S(2)}, u32[]{:S(2)}) collective-permute-start(bf16[1,96,256]{1,2,0:T(8,128)(2,1)S(1)} %bitcast.716), channel_id=1, source_target_pairs={{1,0},{2,1},{3,2},{4,3},{5,4},{6,5},{7,6},{8,7},{9,8},{10,9},{11,1... | collective-permute-start | bytes 147464 | tf_op jit(solution)/shard_map/ppermute | solution.py:26
  15.5 13.2 %collective-permute-start.3 = (bf16[96,128]{0,1:T(8,128)(2,1)S(1)}, bf16[96,128]{0,1:T(8,128)(2,1)S(1)}, u32[]{:S(2)}, u32[]{:S(2)}) collective-permute-start(bf16[96,128]{0,1:T(8,128)(2,1)S(1)} %bitcast.732), channel_id=1, source_target_pairs={{0,128},{16,144},{32,160},{48,176},{64,192},{80,208},{96,224},{112... | collective-permute-start | bytes 73736 | tf_op jit(solution)/shard_map/ppermute | solution.py:15
  19.4 13.7 %collective-permute-start = (bf16[96,128]{0,1:T(8,128)(2,1)S(1)}, bf16[96,128]{0,1:T(8,128)(2,1)S(1)}, u32[]{:S(2)}, u32[]{:S(2)}) collective-permute-start(bf16[96,128]{0,1:T(8,128)(2,1)S(1)} %bitcast.729), channel_id=1, source_target_pairs={{0,16},{16,0},{32,48},{48,32},{64,80},{80,64},{96,112},{112,96},{1... | collective-permute-start | bytes 73736 | tf_op jit(solution)/shard_map/ppermute | solution.py:15
  20.3 12.7 %collective-permute-start.2 = (bf16[96,128]{0,1:T(8,128)(2,1)S(1)}, bf16[96,128]{0,1:T(8,128)(2,1)S(1)}, u32[]{:S(2)}, u32[]{:S(2)}) collective-permute-start(bf16[96,128]{0,1:T(8,128)(2,1)S(1)} %bitcast.727), channel_id=1, source_target_pairs={{0,64},{16,80},{32,96},{48,112},{64,0},{80,16},{96,32},{112,48},{1... | collective-permute-start | bytes 73736 | tf_op jit(solution)/shard_map/ppermute | solution.py:15
  20.7 12.3 %collective-permute-start.1 = (bf16[96,128]{0,1:T(8,128)(2,1)S(1)}, bf16[96,128]{0,1:T(8,128)(2,1)S(1)}, u32[]{:S(2)}, u32[]{:S(2)}) collective-permute-start(bf16[96,128]{0,1:T(8,128)(2,1)S(1)} %bitcast.725), channel_id=1, source_target_pairs={{0,32},{16,48},{32,0},{48,16},{64,96},{80,112},{96,64},{112,80},{1... | collective-permute-start | bytes 73736 | tf_op jit(solution)/shard_map/ppermute | solution.py:15
  28.7 5.6 %collective-permute-start.4 = (bf16[1,96,256]{1,2,0:T(8,128)(2,1)S(1)}, bf16[1,96,256]{1,2,0:T(8,128)(2,1)S(1)}, u32[]{:S(2)}, u32[]{:S(2)}) collective-permute-start(bf16[1,96,256]{1,2,0:T(8,128)(2,1)S(1)} %bitcast.715), channel_id=1, source_target_pairs={{0,1},{1,2},{2,3},{3,4},{4,5},{5,6},{6,7},{7,8},{8,9},{9,10},{10,1... | collective-permute-start | bytes 147464 | tf_op jit(solution)/shard_map/ppermute | solution.py:23
  101.3 3.5 copy-start.2
  109.8 50.7 %collective-permute-start.11 = (bf16[1,96,256]{1,2,0:T(8,128)(2,1)S(1)}, bf16[1,96,256]{1,2,0:T(8,128)(2,1)S(1)}, u32[]{:S(2)}, u32[]{:S(2)}) collective-permute-start(bf16[1,96,256]{1,2,0:T(8,128)(2,1)S(1)} %bitcast.714), channel_id=1, source_target_pairs={{1,0},{2,1},{3,2},{4,3},{5,4},{6,5},{7,6},{8,7},{9,8},{10,9},{11,1... | collective-permute-start | bytes 147464 | tf_op jit(solution)/shard_map/ppermute | solution.py:26
  111.7 42.9 %collective-permute-start.9 = (bf16[96,128]{0,1:T(8,128)(2,1)S(1)}, bf16[96,128]{0,1:T(8,128)(2,1)S(1)}, u32[]{:S(2)}, u32[]{:S(2)}) collective-permute-start(bf16[96,128]{0,1:T(8,128)(2,1)S(1)} %bitcast.724), channel_id=1, source_target_pairs={{0,128},{16,144},{32,160},{48,176},{64,192},{80,208},{96,224},{112... | collective-permute-start | bytes 73736 | tf_op jit(solution)/shard_map/ppermute | solution.py:15
  113.3 45.9 %collective-permute-start.6 = (bf16[96,128]{0,1:T(8,128)(2,1)S(1)}, bf16[96,128]{0,1:T(8,128)(2,1)S(1)}, u32[]{:S(2)}, u32[]{:S(2)}) collective-permute-start(bf16[96,128]{0,1:T(8,128)(2,1)S(1)} %bitcast.721), channel_id=1, source_target_pairs={{0,16},{16,0},{32,48},{48,32},{64,80},{80,64},{96,112},{112,96},{1... | collective-permute-start | bytes 73736 | tf_op jit(solution)/shard_map/ppermute | solution.py:15
  115.0 44.2 %collective-permute-start.8 = (bf16[96,128]{0,1:T(8,128)(2,1)S(1)}, bf16[96,128]{0,1:T(8,128)(2,1)S(1)}, u32[]{:S(2)}, u32[]{:S(2)}) collective-permute-start(bf16[96,128]{0,1:T(8,128)(2,1)S(1)} %bitcast.719), channel_id=1, source_target_pairs={{0,64},{16,80},{32,96},{48,112},{64,0},{80,16},{96,32},{112,48},{1... | collective-permute-start | bytes 73736 | tf_op jit(solution)/shard_map/ppermute | solution.py:15
  115.0 44.2 %collective-permute-start.7 = (bf16[96,128]{0,1:T(8,128)(2,1)S(1)}, bf16[96,128]{0,1:T(8,128)(2,1)S(1)}, u32[]{:S(2)}, u32[]{:S(2)}) collective-permute-start(bf16[96,128]{0,1:T(8,128)(2,1)S(1)} %bitcast.717), channel_id=1, source_target_pairs={{0,32},{16,48},{32,0},{48,16},{64,96},{80,112},{96,64},{112,80},{1... | collective-permute-start | bytes 73736 | tf_op jit(solution)/shard_map/ppermute | solution.py:15
  154.6 6.4 %collective-permute-start.10 = (bf16[1,96,256]{1,2,0:T(8,128)(2,1)S(1)}, bf16[1,96,256]{1,2,0:T(8,128)(2,1)S(1)}, u32[]{:S(2)}, u32[]{:S(2)}) collective-permute-start(bf16[1,96,256]{1,2,0:T(8,128)(2,1)S(1)} %bitcast.713), channel_id=1, source_target_pairs={{0,1},{1,2},{2,3},{3,4},{4,5},{5,6},{6,7},{7,8},{8,9},{9,10},{10,1... | collective-permute-start | bytes 147464 | tf_op jit(solution)/shard_map/ppermute | solution.py:23
  167.5 1.8 copy-start.1
  218.8 3.5 copy-start.3
Sparse Core Ops, SparseCore 0:
  154.7 261.1 all-reduce.6
where the time goes:
time: 433 us; the launch traced here: 426 us
  waiting for transfers between devices  193 us (45%)
  matrix products  124 us (29%)
  local copies, waits for them, and re-layouts  46.6 us (11%)
  starting transfers between devices  29 us (7%)
  other arithmetic  17.8 us (4%)
  between operations  15.3 us (4%)
    psum x1, waiting for transfers between devices, on_device(): weight_total = lax.psum(local_terms, ('tile', 'band'))  193 us
    dot_general x54, matrix products, convolve(): jnp.einsum('bcp,co->bop', extended[:, :, offset:offset + 1000], weights[t...  95.8 us
    dot_general x27, matrix products, group_term(): jnp.einsum('bcp,bop->co', extended[:, :, offset:offset + 1000], delta_spr...  28.4 us
    ppermute x8, starting transfers between devices, swapped(): return lax.ppermute(value, axis, pairs)  17.3 us
    gather x4, local copies, waits for them, and re-layouts, build_extended(): return jnp.take(source, jnp.asarray(extended_table()), axis=2)  12.3 us
    concatenate x2, other arithmetic, build_extended(): jnp.concatenate([flat_data, side_rows, jnp.zeros((num_blocks, channels, 1...  9.32 us
    gather x2, local copies, waits for them, and re-layouts, on_device(): jnp.take(jnp.concatenate([delta_grad, jnp.zeros((num_blocks, channels, 1)...  9.28 us
    ppermute x2, starting transfers between devices, extended_2(): lax.ppermute(lax.slice_in_dim(block, block.shape[dim] - width, None, axis...  8.89 us
  transfers between devices with their start and end apart: 13, of which 2 were waited for; matrix products, arithmetic and copies ran while one was open for 25% of the time, Pallas kernels for 0%

commit v1 on v0

v1 whole, which is shorter than its diff:
```python
import functools
import math

import jax
import jax.numpy as jnp
import numpy as np
from jax import lax
from jax.experimental import pallas as pl
from jax.experimental.pallas import tpu as pltpu
from jax.sharding import Mesh
from jax.sharding import PartitionSpec as P

NB, C, V, TAPS = 4, 96, 512, 27
BF16, F32 = jnp.bfloat16, jnp.float32
TILE = ("y", "zh", "c")
BAND = ("zl", "x")
EVERY = TILE + BAND
PLANE = ("y", "x")
COLUMN = ("zh", "zl")
ROWS, HALF = 2048, 1024
SCALE = 1.0 / math.sqrt(1024 * 512)
SHIFTS = [(dy, dz) for dy in range(3) for dz in range(3)]
VMEM_LIMIT = 56 * 1024 * 1024


def face_matrix():
    table = np.zeros((V, 6 * 128), np.float32)
    for f in range(6):
        for a in range(8):
            for b in range(8):
                if f < 2:
                    v = 448 * f + 8 * a + b
                elif f < 4:
                    v = 64 * a + 56 * (f - 2) + b
                else:
                    v = 64 * a + 8 * b + 7 * (f - 4)
                table[v, 128 * f + 8 * a + b] = 1
                table[v, 128 * f + 64 + 8 * a + b] = 1
    return table


def halo_matrix():
    table = np.zeros((256, 9, V), np.float32)
    for t, (dy, dz) in enumerate(SHIFTS):
        for v in range(V):
            x, y, z = v // 64, v // 8 % 8 + dy - 1, v % 8 + dz - 1
            in_y, in_z = 0 <= y < 8, 0 <= z < 8
            if in_z and not in_y:
                table[(0 if y < 0 else 64) + 8 * x + z, t, v] = 1
            elif in_y and not in_z:
                table[(128 if z < 0 else 192) + 8 * x + y, t, v] = 1
    return table.reshape(256, 9 * V)


def lane_low(rows):
    return lax.broadcasted_iota(jnp.int32, (rows, 128), 1) < 64


def write_faces(data, pf, send_ref, own_ref, lat_ref, zf_ref):
    flat = data.reshape(NB * C, V)
    faces = jnp.dot(flat, pf, preferred_element_type=F32).astype(BF16)
    low = lane_low(C)
    for f in range(4):
        for b in range(NB):
            own_ref[NB * f + b] = faces[C * b : C * (b + 1), 128 * f : 128 * (f + 1)]
    for d in range(2):
        for h in range(2):
            cols = slice(128 * (4 + d), 128 * (5 + d))
            first = faces[C * 2 * h : C * (2 * h + 1), cols]
            second = faces[C * (2 * h + 1) : C * (2 * h + 2), cols]
            zf_ref[d, h] = jnp.where(low, first, second)
    for k in range(4):
        lat_ref[k] = jnp.where(low, own_ref[send_ref[0, k, 0]], own_ref[send_ref[0, k, 1]])


def fill_pool(own_ref, recv_ref, down_ref, up_ref, pool):
    low = lane_low(C)

    def spread(pair, at):
        turned = pltpu.roll(pair, 64, 1)
        pool[at] = jnp.where(low, pair, turned)
        pool[at + 1] = jnp.where(low, turned, pair)

    zero = jnp.zeros((C, 128), BF16)
    for i in range(16):
        pool[i] = own_ref[i]
    for k in range(4):
        spread(recv_ref[k], 16 + 2 * k)
    pool[24] = zero
    for h in range(2):
        spread(down_ref[h], 25 + 2 * h)
        spread(up_ref[h], 30 + 2 * h)
    pool[29] = zero
    pool[34] = zero


def build_taps(data, pool, src_ref, down_ref, up_ref, e_ref, slabs, halo, x_ref):
    low = lane_low(C)
    side_x = []
    for b in range(NB):
        lat = [pool[jnp.where(src_ref[b, i] < 0, 24, src_ref[b, i])] for i in range(4)]
        below = pool[jnp.where(down_ref[b] < 0, 29, 25 + down_ref[b])]
        above = pool[jnp.where(up_ref[b] < 0, 34, 30 + up_ref[b])]
        side_x.append(jnp.where(low, lat[0], lat[1]))
        slabs[C * b : C * (b + 1), 0:128] = jnp.where(low, lat[2], lat[3])
        slabs[C * b : C * (b + 1), 128:256] = jnp.where(low, below, above)
    lanes = lax.broadcasted_iota(jnp.int32, (C, V), 1)
    lane_y, lane_z = (lanes >> 3) & 7, lanes & 7
    for t, (dy, dz) in enumerate(SHIFTS):
        step = 8 * (dy - 1) + dz - 1
        if step:
            halo[...] = jnp.dot(
                slabs[...], e_ref[:, V * t : V * (t + 1)], preferred_element_type=F32
            ).astype(BF16)
            at_y, at_z = lane_y + (dy - 1), lane_z + (dz - 1)
            inside = (at_y >= 0) & (at_y < 8) & (at_z >= 0) & (at_z < 8)
        for b in range(NB):
            if step:
                shifted = pltpu.roll(data[b], (-step) % V, 1)
                shifted = jnp.where(inside, shifted, halo[C * b : C * (b + 1), :])
                edge = pltpu.roll(side_x[b], (-step) % 128, 1)
                edge = jnp.where(inside[:, :128], edge, jnp.zeros_like(edge))
            else:
                shifted, edge = data[b], side_x[b]
            turned = [pltpu.roll(shifted[:, 128 * i : 128 * (i + 1)], 64, 1) for i in range(4)]
            between = [jnp.where(low, turned[i], turned[i + 1]) for i in range(3)]
            columns = [jnp.where(low, edge, turned[0])] + between + [jnp.where(low, turned[3], edge)]
            at = [C * (9 * dx + t) for dx in range(3)]
            x_ref[at[1] : at[1] + C, V * b : V * (b + 1)] = shifted
            for i in range(4):
                place = slice(V * b + 128 * i, V * b + 128 * (i + 1))
                x_ref[at[0] : at[0] + C, place] = columns[i]
                x_ref[at[2] : at[2] + C, place] = columns[i + 1]


def masked_of(feat_ref, occ_ref):
    return feat_ref[...] * occ_ref[...].astype(F32).astype(BF16)


def faces_kernel(feat_ref, occ_ref, pf_ref, send_ref, own_ref, lat_ref, zf_ref):
    write_faces(masked_of(feat_ref, occ_ref), pf_ref[...], send_ref, own_ref, lat_ref, zf_ref)


def forward_kernel(
    feat_ref, occ_ref, grad_ref, w_ref, pf_ref, e_ref, own_ref, recv_ref, below_ref, above_ref,
    src_ref, down_ref, up_ref, send_ref, core_ref,
    out_ref, delta_ref, keep_ref, give_ref, down_own_ref, lat_ref, zf_ref,
    pool, slabs, halo, taps, terms_ref,
):
    fill_pool(own_ref, recv_ref, below_ref, above_ref, pool)
    masked = masked_of(feat_ref, occ_ref)
    build_taps(masked, pool, src_ref, down_ref, up_ref, e_ref, slabs, halo, taps)
    for b in range(NB):
        pre = jnp.dot(w_ref[...], taps[:, V * b : V * (b + 1)], preferred_element_type=F32)
        mask = occ_ref[b].astype(F32)
        sig = jax.nn.sigmoid(pre)
        out_ref[b] = (feat_ref[b].astype(F32) + mask * (pre * sig)).astype(BF16)
        delta = grad_ref[b].astype(F32) * mask * (sig * (1.0 + pre * (1.0 - sig)))
        delta_ref[b] = delta.astype(BF16)
    write_faces(delta_ref[...], pf_ref[...], send_ref, down_own_ref, lat_ref, zf_ref)
    delta = jnp.concatenate([delta_ref[b] for b in range(NB)], axis=1)
    quarter = TAPS * C // 4
    for q in range(4):
        term = lax.dot_general(
            taps[quarter * q : quarter * (q + 1), :], delta, (((1,), (1,)), ((), ())),
            preferred_element_type=F32,
        )
        if q < 3:
            terms_ref[quarter * q : quarter * (q + 1), 0:C] = term
        else:
            for i in range(3):
                terms_ref[quarter * i : quarter * (i + 1), C:128] = term[:, 32 * i : 32 * (i + 1)]
    terms_ref[3 * quarter : ROWS, :] = jnp.zeros((ROWS - 3 * quarter, 128), F32)
    core = core_ref[0]
    keep_ref[...] = terms_ref[pl.ds(pl.multiple_of(core * HALF, HALF), HALF), :]
    give_ref[...] = terms_ref[pl.ds(pl.multiple_of((1 - core) * HALF, HALF), HALF), :]


def backward_kernel(
    delta_in_ref, occ_ref, grad_ref, w_ref, e_ref, own_ref, recv_ref, below_ref, above_ref,
    src_ref, down_ref, up_ref,
    out_ref,
    pool, slabs, halo, taps,
):
    fill_pool(own_ref, recv_ref, below_ref, above_ref, pool)
    build_taps(delta_in_ref[...], pool, src_ref, down_ref, up_ref, e_ref, slabs, halo, taps)
    for b in range(NB):
        back = jnp.dot(w_ref[...], taps[:, V * b : V * (b + 1)], preferred_element_type=F32)
        out_ref[b] = (grad_ref[b].astype(F32) + occ_ref[b].astype(F32) * back).astype(BF16)


def unpack_kernel(mine_ref, other_ref, core_ref, out_ref, packed_ref):
    core = core_ref[0]
    packed_ref[pl.ds(pl.multiple_of(core * HALF, HALF), HALF), :] = mine_ref[...].astype(F32)
    packed_ref[pl.ds(pl.multiple_of((1 - core) * HALF, HALF), HALF), :] = other_ref[...].astype(F32)
    quarter = TAPS * C // 4
    for q in range(3):
        rows = slice(quarter * q, quarter * (q + 1))
        out_ref[rows, :] = packed_ref[rows, 0:C] * SCALE
        out_ref[3 * quarter :, 32 * q : 32 * (q + 1)] = packed_ref[rows, C:128] * SCALE


VM = pl.BlockSpec(memory_space=pltpu.VMEM)
SM = pl.BlockSpec(memory_space=pltpu.SMEM)


def call(kernel, ins, outs, scratch=(), flops=0, moved=0, **kw):
    return pl.pallas_call(
        kernel,
        in_specs=ins,
        out_specs=[VM] * len(outs),
        out_shape=[jax.ShapeDtypeStruct(*o) for o in outs],
        scratch_shapes=list(scratch),
        compiler_params=pltpu.CompilerParams(vmem_limit_bytes=VMEM_LIMIT),
        cost_estimate=pl.CostEstimate(flops=flops, bytes_accessed=moved, transcendentals=0),
        **kw,
    )


FACE_OUTS = [((16, C, 128), BF16), ((4, C, 128), BF16), ((2, 2, C, 128), BF16)]
SCRATCH = [
    pltpu.VMEM((35, C, 128), BF16),
    pltpu.VMEM((NB * C, 256), BF16),
    pltpu.VMEM((NB * C, V), BF16),
    pltpu.VMEM((TAPS * C, NB * V), BF16),
]


def exchange(lat, zf):
    flip2 = [(0, 1), (1, 0)]
    got = [
        lax.ppermute(lat[0], "c", flip2),
        lax.ppermute(lat[1], "zh", flip2),
        lax.ppermute(lat[2], "y", [(i, i ^ 1) for i in range(4)]),
        lax.ppermute(lat[3], "y", [(i, i ^ 2) for i in range(4)]),
    ]
    below = lax.ppermute(zf[1], BAND, [(i, i + 1) for i in range(15)])
    above = lax.ppermute(zf[0], BAND, [(i + 1, i) for i in range(15)])
    return jnp.stack(got), below, above


def exchanged(pieces, axes):
    return lax.all_to_all(pieces, axes, 0, 0, tiled=True)


def repeated(value, count):
    return jnp.broadcast_to(value[None], (count,) + value.shape)


def on_device(features, occupancy, weights, grad_out, lat_src, down_src, up_src, send_faces):
    occ = occupancy[:, None, :]
    core = lax.axis_index("c").reshape(1)
    pf = jnp.asarray(face_matrix(), BF16)
    e = jnp.asarray(halo_matrix(), BF16)
    w_fwd = weights.reshape(TAPS * C, C).T
    w_bwd = jnp.flip(weights, 0).transpose(1, 0, 2).reshape(C, TAPS * C)
    own, lat, zf = call(faces_kernel, [VM, VM, VM, SM], FACE_OUTS)(features, occ, pf, send_faces)
    recv, below, above = exchange(lat, zf)
    layer_out, delta, keep, give, down_own, lat, zf = call(
        forward_kernel,
        [VM] * 10 + [SM] * 5,
        [((NB, C, V), BF16), ((NB, C, V), BF16), ((HALF, 128), F32), ((HALF, 128), F32)] + FACE_OUTS,
        SCRATCH + [pltpu.VMEM((ROWS, 128), F32)],
    )(
        features, occ, grad_out, w_fwd, pf, e, own, recv, below, above,
        lat_src, down_src, up_src, send_faces, core,
    )
    recv, below, above = exchange(lat, zf)
    (input_grad,) = call(
        backward_kernel, [VM] * 9 + [SM] * 3, [((NB, C, V), BF16)], SCRATCH,
        flops=2 * 10**9, moved=4 * 10**6,
    )(delta, occ, grad_out, w_bwd, e, down_own, recv, below, above, lat_src, down_src, up_src)
    part = keep + lax.ppermute(give, "c", [(0, 1), (1, 0)])
    part = exchanged(part.reshape(16, HALF // 16, 128), PLANE).sum(0)
    part = exchanged(repeated(part, 8), COLUMN).sum(0)
    mine = exchanged(repeated(part.astype(BF16), 16), PLANE).reshape(HALF, 128)
    other = lax.ppermute(mine, "c", [(0, 1), (1, 0)])
    (weight_grad,) = call(
        unpack_kernel, [VM, VM, SM], [((TAPS * C, C), F32)], [pltpu.VMEM((ROWS, 128), F32)]
    )(mine, other, core)
    return layer_out, input_grad, weight_grad.reshape(TAPS, C, C)


def solution(mesh):
    fine = Mesh(mesh.devices.reshape(4, 2, 2, 4, 4), EVERY)
    split = P(EVERY)
    return jax.shard_map(
        on_device,
        mesh=fine,
        in_specs=(split, split, P(), split, split, split, split, split),
        out_specs=(split, split, P()),
        check_vma=False,
    )
```

time: 433 us -> 110 us (0.25)
  the two profiles are of different devices: /device:TPU:1 before, /device:TPU:6 now
where the time goes in v1:
time: 110 us; the launch traced here: 109 us
  starting transfers between devices  37.3 us (34%)
  Pallas kernels  21.9 us (20%)
  waiting for transfers between devices  20.3 us (18%)
  blocking collectives  14.8 us (13%)
  local copies, waits for them, and re-layouts  11.3 us (10%)
  other arithmetic  2.47 us (2%)
    all_to_all x1, blocking collectives, exchanged(): return lax.all_to_all(pieces, axes, 0, 0, tiled=True)  14.8 us
    pallas_call x1, Pallas kernels, on_device(): call(forward_kernel, [VM] * 10 + [SM] * 5, [((NB, C, V), BF16), ((NB, C,...  10.6 us
    all_to_all x2, starting transfers between devices, exchanged(): return lax.all_to_all(pieces, axes, 0, 0, tiled=True)  10.1 us
    all_to_all x2, waiting for transfers between devices, exchanged(): return lax.all_to_all(pieces, axes, 0, 0, tiled=True)  9.15 us
    ppermute x2, starting transfers between devices, exchange(): lax.ppermute(lat[1], 'zh', flip2)  7.75 us
    ppermute x2, waiting for transfers between devices, exchange(): above = lax.ppermute(zf[0], BAND, [(i + 1, i) for i in range(15)])  7.74 us
    ppermute x2, starting transfers between devices, exchange(): lax.ppermute(lat[3], 'y', [(i, i ^ 2) for i in range(4)])  6.33 us
    pallas_call x1, Pallas kernels, on_device(): call(backward_kernel, [VM] * 9 + [SM] * 3, [((NB, C, V), BF16)], SCRATCH,...  6.27 us
  transfers between devices with their start and end apart: 16, of which 5 were waited for; matrix products, arithmetic and copies ran while one was open for 5% of the time, Pallas kernels for 6%

profile of v1, /device:TPU:6, one launch (start us, length us, event | category | flops | bytes accessed | tf_op | source)
XLA Modules:
  0.0 108.9 jit_solution(4838374880971215024)
XLA Ops:
  0.6 1.3 %broadcast_in_dim.6.occ_ref = s32[4,1,512]{2,1,0:T(1,128)} reshape(s32[4,512]{1,0:T(4,128)} %param.11) | data formatting | bytes 16384 | tf_op jit(solution)/shard_map/broadcast_in_dim | solution.py:251
  1.9 1.4 %copy.23.send_ref = s32[1,4,2]{2,1,0:T(4,128)} copy(s32[1,4,2]{1,2,0:T(2,128)} %param.17) | data formatting | bytes 64 | tf_op args[7]
  3.3 2.6 %shard_map.121 = (bf16[16,96,128]{2,1,0:T(8,128)(2,1)}, bf16[4,96,128]{2,1,0:T(8,128)(2,1)}, bf16[2,2,96,128]{3,2,1,0:T(8,128)(2,1)}) custom-call(bf16[4,96,512]{2,1,0:T(8,128)(2,1)} %feat_ref.3, s32[4,1,512]{2,1,0:T(1,128)} %broadcast_in_dim.6.occ_ref, bf16[512,768]{1,0:T(8,128)(2,1)} %constant.12.clone.pf_ref, s32[1,4,2]{2,1,0:T(4,128)} %copy.23.send_ref), custom_call_target="tpu_custom_call" | custom-call | tf_op jit(solution)/shard_map/pallas_call | solution.py:257
  5.8 0.8 slice_bitcast_fusion.11
  6.6 3.3 %collective-permute-start.3 = (bf16[96,128]{1,0:T(8,128)(2,1)S(1)}, bf16[96,128]{1,0:T(8,128)(2,1)S(1)}, u32[]{:S(2)}, u32[]{:S(2)}) collective-permute-start(bf16[96,128]{1,0:T(8,128)(2,1)S(1)} %get-tuple-element.32), channel_id=1, source_target_pairs={{0,128},{64,192},{128,0},{192,64},{1,129},{65,193},{129,1},{193,65... | collective-permute-start | bytes 73736 | tf_op jit(solution)/shard_map/ppermute | solution.py:235
  9.9 0.7 collective-permute-start.2
  10.6 7.2 %collective-permute-start.1 = (bf16[96,128]{1,0:T(8,128)(2,1)S(1)}, bf16[96,128]{1,0:T(8,128)(2,1)S(1)}, u32[]{:S(2)}, u32[]{:S(2)}) collective-permute-start(bf16[96,128]{1,0:T(8,128)(2,1)S(1)} %get-tuple-element.34), channel_id=1, source_target_pairs={{0,32},{32,0},{1,33},{33,1},{2,34},{34,2},{3,35},{35,3},{4,36},{36... | collective-permute-start | bytes 73736 | tf_op jit(solution)/shard_map/ppermute | solution.py:233
  17.8 0.0 collective-permute-start
  17.8 0.8 slice_bitcast_fusion.2
  18.6 2.8 %collective-permute-start.4 = (bf16[2,96,128]{2,1,0:T(8,128)(2,1)S(1)}, bf16[2,96,128]{2,1,0:T(8,128)(2,1)S(1)}, u32[]{:S(2)}, u32[]{:S(2)}) collective-permute-start(bf16[2,96,128]{2,1,0:T(8,128)(2,1)S(1)} %get-tuple-element.30), channel_id=1, source_target_pairs={{0,1},{1,2},{2,3},{3,4},{4,5},{5,6},{6,7},{7,8},{8,9},{9,10},{10,1... | collective-permute-start | bytes 147464 | tf_op jit(solution)/shard_map/ppermute | solution.py:237
  21.5 2.2 %copy.22 = bf16[2592,96]{0,1:T(8,128)(2,1)} copy(bf16[2592,96]{1,0:T(8,128)(2,1)} %bitcast.41) | data formatting | bytes 995328 | tf_op jit(solution)/shard_map/reshape | solution.py:255
  23.6 0.0 collective-permute-done.3
  23.6 3.0 %collective-permute-start.5 = (bf16[2,96,128]{2,1,0:T(8,128)(2,1)S(1)}, bf16[2,96,128]{2,1,0:T(8,128)(2,1)S(1)}, u32[]{:S(2)}, u32[]{:S(2)}) collective-permute-start(bf16[2,96,128]{2,1,0:T(8,128)(2,1)S(1)} %get-tuple-element.29), channel_id=1, source_target_pairs={{1,0},{2,1},{3,2},{4,3},{5,4},{6,5},{7,6},{8,7},{9,8},{10,9},{11,1... | collective-permute-start | bytes 147464 | tf_op jit(solution)/shard_map/ppermute | solution.py:238
  26.6 0.0 collective-permute-done.2
  26.6 0.0 collective-permute-done.1
  26.6 0.0 collective-permute-done
  26.6 0.7 pad_maximum_fusion.recv_ref
  27.3 0.0 collective-permute-done.4.below_ref
  27.3 0.0 copy-start.5
  27.3 4.4 %collective-permute-done.5.above_ref = bf16[2,96,128]{2,1,0:T(8,128)(2,1)S(1)} collective-permute-done((bf16[2,96,128]{2,1,0:T(8,128)(2,1)S(1)}, bf16[2,96,128]{2,1,0:T(8,128)(2,1)S(1)}, u32[]{:S(2)}, u32[]{:S(2)}) %collective-permute-start.5) | collective-permute-done | bytes 49184 | tf_op jit(solution)/shard_map/ppermute | solution.py:238
  31.7 0.0 copy-done.5
  31.7 0.6 copy-done.6
  32.3 10.6 %shard_map.122 = (bf16[4,96,512]{2,1,0:T(8,128)(2,1)}, bf16[4,96,512]{2,1,0:T(8,128)(2,1)}, f32[1024,128]{1,0:T(8,128)}, f32[1024,128]{1,0:T(8,128)}, bf16[16,96...) custom-call(bf16[4,96,512]{2,1,0:T(8,128)(2,1)} %feat_ref.3, ...), custom_call_target="tpu_custom_call" | custom-call | tf_op jit(solution)/shard_map/pallas_call | solution.py:259
  42.9 0.0 copy-start
  42.9 0.1 collective-permute-start.12
  43.0 2.1 %collective-permute-done.12 = f32[1024,128]{1,0:T(8,128)S(1)} collective-permute-done((f32[1024,128]{1,0:T(8,128)}, f32[1024,128]{1,0:T(8,128)S(1)}, u32[]{:S(2)}, u32[]{:S(2)}) %collective-permute-start.12) | collective-permute-done | bytes 524320 | tf_op jit(solution)/shard_map/ppermute | solution.py:273
  45.1 1.1 %add.3 = f32[1024,128]{1,0:T(8,128)S(1)} add(f32[1024,128]{1,0:T(8,128)} %get-tuple-element.21, f32[1024,128]{1,0:T(8,128)S(1)} %collective-permute-done.12) | non-fusion elementwise | flops 131072 | bytes 1572864 | tf_op jit(solution)/shard_map/add | solution.py:273
  46.2 14.8 %all_to_all.15 = f32[16,64,128]{2,1,0:T(8,128)S(1)} all-to-all(f32[16,64,128]{2,1,0:T(8,128)S(1)} %bitcast.43), channel_id=1, replica_groups=mesh['y'=4,'zh'=2,'c'=2,'zl'=4,'x'=4] {'y','x'}, dimensions={0} | all-to-all | bytes 1048576 | tf_op jit(solution)/shard_map/all_to_all | solution.py:243
  61.1 0.7 broadcast_in_dim.7
  61.8 3.4 %all-to-all-start.1 = ((f32[8,64,128]{2,1,0:T(8,128)}), f32[8,64,128]{2,1,0:T(8,128)S(1)}, u32[]{:S(2)}, u32[]{:S(2)}) async-start(f32[8,64,128]{2,1,0:T(8,128)} %broadcast_in_dim.7), calls=%async_computation.1 | async-start | bytes 524288 | tf_op jit(solution)/shard_map/all_to_all | solution.py:243
  65.2 0.0 copy-done
  65.2 0.0 copy-start.4
  65.3 0.0 copy-start.3
  65.3 0.3 copy.25
  65.6 1.1 copy.26.w_ref
  66.7 9.1 %all-to-all-done.1 = f32[8,64,128]{2,1,0:T(8,128)S(1)} async-done(((f32[8,64,128]{2,1,0:T(8,128)}), f32[8,64,128]{2,1,0:T(8,128)S(1)}, u32[]{:S(2)}, u32[]{:S(2)}) %all-to-all-start.1) | async-done | bytes 262176 | tf_op jit(solution)/shard_map/all_to_all | solution.py:243
  75.9 0.8 broadcast_in_dim.8
  76.6 6.7 %all-to-all-start.2 = ((bf16[16,64,128]{2,1,0:T(8,128)(2,1)}), bf16[16,64,128]{2,1,0:T(8,128)(2,1)S(1)}, u32[]{:S(2)}, u32[]{:S(2)}) async-start(bf16[16,64,128]{2,1,0:T(8,128)(2,1)} %broadcast_in_dim.8), calls=%async_computation.2 | async-start | bytes 524288 | tf_op jit(solution)/shard_map/all_to_all | solution.py:243
  83.4 0.0 copy-done.4
  83.4 3.1 %collective-permute-start.9 = (bf16[96,128]{1,0:T(8,128)(2,1)S(1)}, bf16[96,128]{1,0:T(8,128)(2,1)S(1)}, u32[]{:S(2)}, u32[]{:S(2)}) collective-permute-start(bf16[96,128]{1,0:T(8,128)(2,1)S(1)} %get-tuple-element.26), channel_id=1, source_target_pairs={{0,128},{64,192},{128,0},{192,64},{1,129},{65,193},{129,1},{193,65... | collective-permute-start | bytes 73736 | tf_op jit(solution)/shard_map/ppermute | solution.py:235
  86.4 0.6 collective-permute-start.8
  87.0 0.6 collective-permute-start.7
  87.6 0.0 collective-permute-start.6
  87.6 0.0 copy-done.3
  87.6 3.1 %collective-permute-start.10 = (bf16[2,96,128]{2,1,0:T(8,128)(2,1)S(1)}, bf16[2,96,128]{2,1,0:T(8,128)(2,1)S(1)}, u32[]{:S(2)}, u32[]{:S(2)}) collective-permute-start(bf16[2,96,128]{2,1,0:T(8,128)(2,1)S(1)} %get-tuple-element.24), channel_id=1, source_target_pairs={{0,1},{1,2},{2,3},{3,4},{4,5},{5,6},{6,7},{7,8},{8,9},{9,10},{10,1... | collective-permute-start | bytes 147464 | tf_op jit(solution)/shard_map/ppermute | solution.py:237
  90.7 0.0 collective-permute-done.9
  90.7 2.7 %collective-permute-start.11 = (bf16[2,96,128]{2,1,0:T(8,128)(2,1)S(1)}, bf16[2,96,128]{2,1,0:T(8,128)(2,1)S(1)}, u32[]{:S(2)}, u32[]{:S(2)}) collective-permute-start(bf16[2,96,128]{2,1,0:T(8,128)(2,1)S(1)} %get-tuple-element.23), channel_id=1, source_target_pairs={{1,0},{2,1},{3,2},{4,3},{5,4},{6,5},{7,6},{8,7},{9,8},{10,9},{11,1... | collective-permute-start | bytes 147464 | tf_op jit(solution)/shard_map/ppermute | solution.py:238
  93.4 0.0 collective-permute-done.8
  93.5 0.0 all-to-all-done.2
  93.5 0.0 copy-start.1
  93.5 0.1 collective-permute-start.13
  93.6 1.3 %collective-permute-done.7 = bf16[96,128]{1,0:T(8,128)(2,1)S(1)} collective-permute-done((bf16[96,128]{1,0:T(8,128)(2,1)S(1)}, bf16[96,128]{1,0:T(8,128)(2,1)S(1)}, u32[]{:S(2)}, u32[]{:S(2)}) %collective-permute-start.7) | collective-permute-done | bytes 24608 | tf_op jit(solution)/shard_map/ppermute | solution.py:233
  94.8 0.0 collective-permute-done.6
  94.8 0.6 pad_maximum_fusion.1.recv_ref
  95.5 0.0 collective-permute-done.10.below_ref
  95.5 3.3 %collective-permute-done.11.above_ref = bf16[2,96,128]{2,1,0:T(8,128)(2,1)S(1)} collective-permute-done((bf16[2,96,128]{2,1,0:T(8,128)(2,1)S(1)}, bf16[2,96,128]{2,1,0:T(8,128)(2,1)S(1)}, u32[]{:S(2)}, u32[]{:S(2)}) %collective-permute-start.11) | collective-permute-done | bytes 49184 | tf_op jit(solution)/shard_map/ppermute | solution.py:238
  98.8 0.0 copy-done.7
  98.8 0.6 copy-done.8
  99.5 6.3 %shard_map.123 = bf16[4,96,512]{2,1,0:T(8,128)(2,1)} custom-call(bf16[4,96,512]{2,1,0:T(8,128)(2,1)} %get-tuple-element.17.delta_in_ref, s32[4,1,512]{2,1,0:T(1,128)} %broadcast_in_dim.6.occ_ref, bf16[4,96,512]{2,1,0:T(8,128)(2,1)} %grad_ref.3, bf16[96,2592]{1,0:T(8,128)(2,1)} %copy.26.w_ref, bf16[256,4608]{1,0:T(8,128)(2,1)} %constant.13.clone.e_ref, ...), custom_call_target="tpu_custom_call" | custom-call | flops 2000000000 | bytes 4000000 | tf_op jit(solution)/shard_map/pallas_call | solution.py:269
  105.7 0.0 copy-done.1
  105.7 0.0 collective-permute-done.13.other_ref
  105.7 0.0 copy-start.2
  105.7 0.7 copy-done.2
  106.4 2.5 %shard_map.124 = f32[2592,96]{1,0:T(8,128)} custom-call(bf16[1024,128]{1,0:T(8,128)(2,1)} %bitcast.47, bf16[1024,128]{1,0:T(8,128)(2,1)} %copy-done.2, s32[1]{0:T(128)} %bitcast.12.core_ref), custom_call_target="tpu_custom_call" | custom-call | tf_op jit(solution)/shard_map/pallas_call | solution.py:278
  (8 shorter events, 0.1 us)
Async XLA Ops:
  6.6 17.0 %collective-permute-start.3 = (bf16[96,128]{1,0:T(8,128)(2,1)S(1)}, bf16[96,128]{1,0:T(8,128)(2,1)S(1)}, u32[]{:S(2)}, u32[]{:S(2)}) collective-permute-start(bf16[96,128]{1,0:T(8,128)(2,1)S(1)} %get-tuple-element.32), channel_id=1, source_target_pairs={{0,128},{64,192},{128,0},{192,64},{1,129},{65,193},{129,1},{193,65... | collective-permute-start | bytes 73736 | tf_op jit(solution)/shard_map/ppermute | solution.py:235
  9.9 16.7 %collective-permute-start.2 = (bf16[96,128]{1,0:T(8,128)(2,1)S(1)}, bf16[96,128]{1,0:T(8,128)(2,1)S(1)}, u32[]{:S(2)}, u32[]{:S(2)}) collective-permute-start(bf16[96,128]{1,0:T(8,128)(2,1)S(1)} %get-tuple-element.33), channel_id=1, source_target_pairs={{0,64},{64,0},{128,192},{192,128},{1,65},{65,1},{129,193},{193,129... | collective-permute-start | bytes 73736 | tf_op jit(solution)/shard_map/ppermute | solution.py:234
  10.6 16.0 %collective-permute-start.1 = (bf16[96,128]{1,0:T(8,128)(2,1)S(1)}, bf16[96,128]{1,0:T(8,128)(2,1)S(1)}, u32[]{:S(2)}, u32[]{:S(2)}) collective-permute-start(bf16[96,128]{1,0:T(8,128)(2,1)S(1)} %get-tuple-element.34), channel_id=1, source_target_pairs={{0,32},{32,0},{1,33},{33,1},{2,34},{34,2},{3,35},{35,3},{4,36},{36... | collective-permute-start | bytes 73736 | tf_op jit(solution)/shard_map/ppermute | solution.py:233
  17.8 8.9 %collective-permute-start = (bf16[96,128]{1,0:T(8,128)(2,1)S(1)}, bf16[96,128]{1,0:T(8,128)(2,1)S(1)}, u32[]{:S(2)}, u32[]{:S(2)}) collective-permute-start(bf16[96,128]{1,0:T(8,128)(2,1)S(1)} %get-tuple-element.31), channel_id=1, source_target_pairs={{0,16},{16,0},{1,17},{17,1},{2,18},{18,2},{3,19},{19,3},{4,20},{20... | collective-permute-start | bytes 73736 | tf_op jit(solution)/shard_map/ppermute | solution.py:232
  18.6 8.7 %collective-permute-start.4 = (bf16[2,96,128]{2,1,0:T(8,128)(2,1)S(1)}, bf16[2,96,128]{2,1,0:T(8,128)(2,1)S(1)}, u32[]{:S(2)}, u32[]{:S(2)}) collective-permute-start(bf16[2,96,128]{2,1,0:T(8,128)(2,1)S(1)} %get-tuple-element.30), channel_id=1, source_target_pairs={{0,1},{1,2},{2,3},{3,4},{4,5},{5,6},{6,7},{7,8},{8,9},{9,10},{10,1... | collective-permute-start | bytes 147464 | tf_op jit(solution)/shard_map/ppermute | solution.py:237
  23.6 8.1 %collective-permute-start.5 = (bf16[2,96,128]{2,1,0:T(8,128)(2,1)S(1)}, bf16[2,96,128]{2,1,0:T(8,128)(2,1)S(1)}, u32[]{:S(2)}, u32[]{:S(2)}) collective-permute-start(bf16[2,96,128]{2,1,0:T(8,128)(2,1)S(1)} %get-tuple-element.29), channel_id=1, source_target_pairs={{1,0},{2,1},{3,2},{4,3},{5,4},{6,5},{7,6},{8,7},{9,8},{10,9},{11,1... | collective-permute-start | bytes 147464 | tf_op jit(solution)/shard_map/ppermute | solution.py:238
  27.3 4.4 %copy-start.5 = (bf16[2,96,128]{2,1,0:T(8,128)(2,1)}, bf16[2,96,128]{2,1,0:T(8,128)(2,1)S(1)}, u32[]{:S(2)}) copy-start(bf16[2,96,128]{2,1,0:T(8,128)(2,1)S(1)} %collective-permute-done.4.below_ref) | copy-start | bytes 147460
  31.7 0.6 copy-start.6
  42.9 22.3 %copy-start = (bf16[27,96,96]{2,1,0:T(8,128)(2,1)S(1)}, bf16[27,96,96]{2,1,0:T(8,128)(2,1)}, u32[]{:S(2)}) copy-start(bf16[27,96,96]{2,1,0:T(8,128)(2,1)} %param.12) | copy-start | bytes 1492996
  42.9 2.2 %collective-permute-start.12 = (f32[1024,128]{1,0:T(8,128)}, f32[1024,128]{1,0:T(8,128)S(1)}, u32[]{:S(2)}, u32[]{:S(2)}) collective-permute-start(f32[1024,128]{1,0:T(8,128)} %get-tuple-element.22), channel_id=1, source_target_pairs={{0,16},{16,0},{1,17},{17,1},{2,18},{18,2},{3,19},{19,3},{4,20},{20... | collective-permute-start | bytes 1572872 | tf_op jit(solution)/shard_map/ppermute | solution.py:273
  61.8 14.0 %all-to-all-start.1 = ((f32[8,64,128]{2,1,0:T(8,128)}), f32[8,64,128]{2,1,0:T(8,128)S(1)}, u32[]{:S(2)}, u32[]{:S(2)}) async-start(f32[8,64,128]{2,1,0:T(8,128)} %broadcast_in_dim.7), calls=%async_computation.1 | async-start | bytes 524288 | tf_op jit(solution)/shard_map/all_to_all | solution.py:243
  65.2 18.1 %copy-start.4 = (bf16[4,96,128]{2,1,0:T(8,128)(2,1)S(1)}, bf16[4,96,128]{2,1,0:T(8,128)(2,1)}, u32[]{:S(2)}) copy-start(bf16[4,96,128]{2,1,0:T(8,128)(2,1)} %get-tuple-element.19) | copy-start | bytes 294916
  65.3 22.3 %copy-start.3 = (bf16[2,2,96,128]{3,2,1,0:T(8,128)(2,1)S(1)}, bf16[2,2,96,128]{3,2,1,0:T(8,128)(2,1)}, u32[]{:S(2)}) copy-start(bf16[2,2,96,128]{3,2,1,0:T(8,128)(2,1)} %get-tuple-element.20) | copy-start | bytes 294916
  76.6 16.8 %all-to-all-start.2 = ((bf16[16,64,128]{2,1,0:T(8,128)(2,1)}), bf16[16,64,128]{2,1,0:T(8,128)(2,1)S(1)}, u32[]{:S(2)}, u32[]{:S(2)}) async-start(bf16[16,64,128]{2,1,0:T(8,128)(2,1)} %broadcast_in_dim.8), calls=%async_computation.2 | async-start | bytes 524288 | tf_op jit(solution)/shard_map/all_to_all | solution.py:243
  83.4 7.4 %collective-permute-start.9 = (bf16[96,128]{1,0:T(8,128)(2,1)S(1)}, bf16[96,128]{1,0:T(8,128)(2,1)S(1)}, u32[]{:S(2)}, u32[]{:S(2)}) collective-permute-start(bf16[96,128]{1,0:T(8,128)(2,1)S(1)} %get-tuple-element.26), channel_id=1, source_target_pairs={{0,128},{64,192},{128,0},{192,64},{1,129},{65,193},{129,1},{193,65... | collective-permute-start | bytes 73736 | tf_op jit(solution)/shard_map/ppermute | solution.py:235
  86.4 7.0 %collective-permute-start.8 = (bf16[96,128]{1,0:T(8,128)(2,1)S(1)}, bf16[96,128]{1,0:T(8,128)(2,1)S(1)}, u32[]{:S(2)}, u32[]{:S(2)}) collective-permute-start(bf16[96,128]{1,0:T(8,128)(2,1)S(1)} %get-tuple-element.27), channel_id=1, source_target_pairs={{0,64},{64,0},{128,192},{192,128},{1,65},{65,1},{129,193},{193,129... | collective-permute-start | bytes 73736 | tf_op jit(solution)/shard_map/ppermute | solution.py:234
  87.0 7.8 %collective-permute-start.7 = (bf16[96,128]{1,0:T(8,128)(2,1)S(1)}, bf16[96,128]{1,0:T(8,128)(2,1)S(1)}, u32[]{:S(2)}, u32[]{:S(2)}) collective-permute-start(bf16[96,128]{1,0:T(8,128)(2,1)S(1)} %get-tuple-element.28), channel_id=1, source_target_pairs={{0,32},{32,0},{1,33},{33,1},{2,34},{34,2},{3,35},{35,3},{4,36},{36... | collective-permute-start | bytes 73736 | tf_op jit(solution)/shard_map/ppermute | solution.py:233
  87.6 7.3 %collective-permute-start.6 = (bf16[96,128]{1,0:T(8,128)(2,1)S(1)}, bf16[96,128]{1,0:T(8,128)(2,1)S(1)}, u32[]{:S(2)}, u32[]{:S(2)}) collective-permute-start(bf16[96,128]{1,0:T(8,128)(2,1)S(1)} %get-tuple-element.25), channel_id=1, source_target_pairs={{0,16},{16,0},{1,17},{17,1},{2,18},{18,2},{3,19},{19,3},{4,20},{20... | collective-permute-start | bytes 73736 | tf_op jit(solution)/shard_map/ppermute | solution.py:232
  87.6 7.9 %collective-permute-start.10 = (bf16[2,96,128]{2,1,0:T(8,128)(2,1)S(1)}, bf16[2,96,128]{2,1,0:T(8,128)(2,1)S(1)}, u32[]{:S(2)}, u32[]{:S(2)}) collective-permute-start(bf16[2,96,128]{2,1,0:T(8,128)(2,1)S(1)} %get-tuple-element.24), channel_id=1, source_target_pairs={{0,1},{1,2},{2,3},{3,4},{4,5},{5,6},{6,7},{7,8},{8,9},{9,10},{10,1... | collective-permute-start | bytes 147464 | tf_op jit(solution)/shard_map/ppermute | solution.py:237
  90.7 8.1 %collective-permute-start.11 = (bf16[2,96,128]{2,1,0:T(8,128)(2,1)S(1)}, bf16[2,96,128]{2,1,0:T(8,128)(2,1)S(1)}, u32[]{:S(2)}, u32[]{:S(2)}) collective-permute-start(bf16[2,96,128]{2,1,0:T(8,128)(2,1)S(1)} %get-tuple-element.23), channel_id=1, source_target_pairs={{1,0},{2,1},{3,2},{4,3},{5,4},{6,5},{7,6},{8,7},{9,8},{10,9},{11,1... | collective-permute-start | bytes 147464 | tf_op jit(solution)/shard_map/ppermute | solution.py:238
  93.5 12.3 %copy-start.1 = (bf16[16,64,128]{2,1,0:T(8,128)(2,1)}, bf16[16,64,128]{2,1,0:T(8,128)(2,1)S(1)}, u32[]{:S(2)}) copy-start(bf16[16,64,128]{2,1,0:T(8,128)(2,1)S(1)} %all-to-all-done.2) | copy-start | bytes 786436
  93.5 12.2 %collective-permute-start.13 = (bf16[1024,128]{1,0:T(8,128)(2,1)S(1)}, bf16[1024,128]{1,0:T(8,128)(2,1)S(1)}, u32[]{:S(2)}, u32[]{:S(2)}) collective-permute-start(bf16[1024,128]{1,0:T(8,128)(2,1)S(1)} %bitcast.46), channel_id=1, source_target_pairs={{0,16},{16,0},{1,17},{17,1},{2,18},{18,2},{3,19},{19,3},{4,20},{20... | collective-permute-start | bytes 786440 | tf_op jit(solution)/shard_map/ppermute | solution.py:277
  95.5 3.4 %copy-start.7 = (bf16[2,96,128]{2,1,0:T(8,128)(2,1)}, bf16[2,96,128]{2,1,0:T(8,128)(2,1)S(1)}, u32[]{:S(2)}) copy-start(bf16[2,96,128]{2,1,0:T(8,128)(2,1)S(1)} %collective-permute-done.10.below_ref) | copy-start | bytes 147460
  98.8 0.6 copy-start.8
  105.7 0.7 copy-start.2

commit v2 on v1

v2 whole, which is shorter than its diff:
```python
import functools
import math

import jax
import jax.numpy as jnp
import numpy as np
from jax import lax
from jax.experimental import pallas as pl
from jax.experimental.pallas import tpu as pltpu
from jax.sharding import Mesh
from jax.sharding import PartitionSpec as P

NB, C, V, TAPS = 4, 96, 512, 27
BF16, F32 = jnp.bfloat16, jnp.float32
TILE = ("y", "zh", "c")
BAND = ("zl", "x")
EVERY = TILE + BAND
PLANE = ("y", "x")
COLUMN = ("zh", "zl")
ROWS, HALF, REST = 2048, 1024, 216
MAIN = NB * V
SCALE = 1.0 / math.sqrt(1024 * 512)
SHIFTS = [(dy, dz) for dy in range(3) for dz in range(3)]
VMEM_LIMIT = 26 * 1024 * 1024


def face_matrix():
    table = np.zeros((V, 6 * 128), np.float32)
    for f in range(6):
        for a in range(8):
            for b in range(8):
                if f < 2:
                    v = 448 * f + 8 * a + b
                elif f < 4:
                    v = 64 * a + 56 * (f - 2) + b
                else:
                    v = 64 * a + 8 * b + 7 * (f - 4)
                table[v, 128 * f + 8 * a + b] = 1
                table[v, 128 * f + 64 + 8 * a + b] = 1
    return table


def lane_low(rows):
    return lax.broadcasted_iota(jnp.int32, (rows, 128), 1) < 64


def write_faces(data, pf, send_ref, own_ref, lat_refs, zf_refs, faces_z):
    flat = data.reshape(NB * C, V)
    faces = jnp.dot(flat, pf, preferred_element_type=F32).astype(BF16)
    low = lane_low(C)
    for f in range(4):
        for b in range(NB):
            own_ref[NB * f + b] = faces[C * b : C * (b + 1), 128 * f : 128 * (f + 1)]
    for d in range(2):
        for h in range(2):
            cols = slice(128 * (4 + d), 128 * (5 + d))
            first = faces[C * 2 * h : C * (2 * h + 1), cols]
            second = faces[C * (2 * h + 1) : C * (2 * h + 2), cols]
            faces_z[d, h] = jnp.where(low, first, second)
    odd = lax.axis_index("x") & 1
    zf_refs[0][...] = faces_z[1 - odd]
    zf_refs[1][...] = faces_z[odd]
    for k in range(4):
        lat_refs[k][...] = jnp.where(low, own_ref[send_ref[0, 0, k]], own_ref[send_ref[0, 1, k]])


def fill_pool(recv_refs, pool):
    low = lane_low(C)
    odd = lax.axis_index("x") & 1

    def spread(pair, at):
        turned = pltpu.roll(pair, 64, 1)
        pool[at] = jnp.where(low, pair, turned)
        pool[at + 1] = jnp.where(low, turned, pair)

    for k in range(4):
        spread(recv_refs[k][...], 16 + 2 * k)
    for h in range(2):
        spread(recv_refs[4][h], 30 - 5 * odd + 2 * h)
        spread(recv_refs[5][h], 25 + 5 * odd + 2 * h)
    for at in (24, 29, 34):
        pool[at] = jnp.zeros((C, 128), BF16)


def fill_entries(e_ref):
    lane = lax.broadcasted_iota(jnp.int32, (1, V), 1)
    row = lax.broadcasted_iota(jnp.int32, (256, V), 0)
    x, y, z = lane >> 6, (lane >> 3) & 7, lane & 7
    for t, (dy, dz) in enumerate(SHIFTS):
        if (dy, dz) == (1, 1):
            continue
        at_y, at_z = y + (dy - 1), z + (dz - 1)
        in_y, in_z = (at_y >= 0) & (at_y < 8), (at_z >= 0) & (at_z < 8)
        from_y = jnp.where(at_y < 0, 0, 64) + 8 * x + at_z
        from_z = jnp.where(at_z < 0, 128, 192) + 8 * x + at_y
        entry = jnp.where(in_z & ~in_y, from_y, jnp.where(in_y & ~in_z, from_z, -1))
        e_ref[:, V * t : V * (t + 1)] = jnp.where(row == entry, 1.0, 0.0).astype(BF16)


def build_taps(data, pool, src_ref, down_ref, up_ref, e_ref, slabs, halo, taps):
    low = lane_low(C)
    side_x = []
    for b in range(NB):
        lat = [pool[jnp.where(src_ref[b, i] < 0, 24, src_ref[b, i])] for i in range(4)]
        below = pool[jnp.where(down_ref[b] < 0, 29, 25 + down_ref[b])]
        above = pool[jnp.where(up_ref[b] < 0, 34, 30 + up_ref[b])]
        side_x.append(jnp.where(low, lat[0], lat[1]))
        slabs[C * b : C * (b + 1), 0:128] = jnp.where(low, lat[2], lat[3])
        slabs[C * b : C * (b + 1), 128:256] = jnp.where(low, below, above)
    lanes = lax.broadcasted_iota(jnp.int32, (C, V), 1)
    lane_y, lane_z = (lanes >> 3) & 7, lanes & 7
    for t, (dy, dz) in enumerate(SHIFTS):
        rows = slice(C * t, C * (t + 1))
        step = 8 * (dy - 1) + dz - 1
        if step:
            halo[...] = jnp.dot(
                slabs[...], e_ref[:, V * t : V * (t + 1)], preferred_element_type=F32
            ).astype(BF16)
            at_y, at_z = lane_y + (dy - 1), lane_z + (dz - 1)
            inside = (at_y >= 0) & (at_y < 8) & (at_z >= 0) & (at_z < 8)
        for b in range(NB):
            if step:
                shifted = pltpu.roll(data[b], (-step) % V, 1)
                shifted = jnp.where(inside, shifted, halo[C * b : C * (b + 1), :])
                edge = pltpu.roll(side_x[b], (-step) % 128, 1)
                edge = jnp.where(inside[:, :128], edge, jnp.zeros_like(edge))
            else:
                shifted, edge = data[b], side_x[b]
            taps[rows, V * b : V * (b + 1)] = shifted
            taps[rows, MAIN + 128 * b : MAIN + 128 * (b + 1)] = edge


def convolve(w3, taps, ends, finish):
    low = lane_low(C)
    ends[...] = jnp.dot(w3[: 2 * C, :], taps[:, MAIN:], preferred_element_type=F32)
    for b in range(NB):
        y = jnp.dot(w3[...], taps[:, V * b : V * (b + 1)], preferred_element_type=F32)
        place = slice(128 * b, 128 * (b + 1))
        tiles = [slice(128 * i, 128 * (i + 1)) for i in range(4)]
        before = [ends[:C, place]] + [pltpu.roll(y[:C, tile], 64, 1) for tile in tiles]
        after = [pltpu.roll(y[C : 2 * C, tile], 64, 1) for tile in tiles] + [ends[C:, place]]
        parts = [
            y[2 * C :, tiles[i]]
            + jnp.where(low, before[i], before[i + 1])
            + jnp.where(low, after[i], after[i + 1])
            for i in range(4)
        ]
        finish(b, jnp.concatenate(parts, axis=1))


def kernel_terms(taps, delta_ref, around, terms_ref):
    low = lane_low(C)
    zero = jnp.zeros((C, 128), BF16)
    for b in range(NB):
        tiles = [delta_ref[b, :, 128 * i : 128 * (i + 1)] for i in range(4)]
        turned = [pltpu.roll(tile, 64, 1) for tile in tiles]
        for i in range(4):
            place = slice(V * b + 128 * i, V * b + 128 * (i + 1))
            around[:C, place] = jnp.where(low, turned[i], turned[i + 1] if i < 3 else zero)
            around[C:, place] = jnp.where(low, turned[i - 1] if i else zero, turned[i])
        place = slice(MAIN + 128 * b, MAIN + 128 * (b + 1))
        around[:C, place] = jnp.where(low, tiles[0], zero)
        around[C:, place] = jnp.where(low, zero, tiles[3])
    over_lanes = (((1,), (1,)), ((), ()))
    rows = 9 * C
    sides = lax.dot_general(taps[...], around[...], over_lanes, preferred_element_type=F32)
    terms_ref[0:rows, :] = sides[:, 0:128]
    terms_ref[rows : 2 * rows, 0:64] = sides[:, 128:192]
    delta = jnp.concatenate([delta_ref[b] for b in range(NB)], axis=1)
    middle = lax.dot_general(taps[:, :MAIN], delta, over_lanes, preferred_element_type=F32)
    terms_ref[rows : 2 * rows, 64:128] = middle[:, 0:64]
    for g in range(4):
        terms_ref[2 * rows : 2 * rows + REST, 32 * g : 32 * (g + 1)] = middle[
            REST * g : REST * (g + 1), 64:C
        ]
    terms_ref[2 * rows + REST :, :] = jnp.zeros((ROWS - 2 * rows - REST, 128), F32)


def masked_of(feat_ref, occ_ref):
    occ = occ_ref[...].astype(F32).astype(BF16)
    return jnp.stack([feat_ref[b] * occ[b : b + 1, :] for b in range(NB)])


def started(sems, *pairs):
    copies = [pltpu.make_async_copy(a, b, sems.at[i]) for i, (a, b) in enumerate(pairs)]
    for copy in copies:
        copy.start()
    return copies


def waited(*copies):
    for copy in copies:
        copy.wait()


def faces_kernel(feat_in, occ_in, pf_in, send_in, own_ref, *refs):
    feat, occ, pf, send, faces_z, sems = refs[6:]
    waited(*started(sems, (send_in, send), (occ_in, occ), (feat_in, feat), (pf_in, pf)))
    write_faces(masked_of(feat, occ), pf[...], send, own_ref, refs[:4], refs[4:6], faces_z)


def forward_kernel(
    feat_in, occ_in, grad_in, w_in, pf_in, src_in, down_in, up_in, send_in,
    own_ref, recv0, recv1, recv2, recv3, recv4, recv5,
    out_out, delta_ref, keep_ref, give_ref, delta_own_ref, lat0, lat1, lat2, lat3, zf0, zf1,
    occ, grad, w, src, down, up, out, pool, slabs, halo, taps, w3, e, ends, sems, out_sems,
    feat, pf, send, faces_z, terms_ref, around,
):
    early = started(
        sems, (src_in, src), (down_in, down), (up_in, up), (occ_in, occ), (feat_in, feat),
    )
    later = started(sems.at[5:], (w_in, w), (grad_in, grad), (pf_in, pf), (send_in, send))
    for i in range(16):
        pool[i] = own_ref[i]
    fill_pool((recv0, recv1, recv2, recv3, recv4, recv5), pool)
    fill_entries(e)
    waited(*early)
    build_taps(masked_of(feat, occ), pool, src, down, up, e, slabs, halo, taps)
    waited(*later)
    for i, dx in enumerate((0, 2, 1)):
        w3[C * i : C * (i + 1), :] = w[9 * dx : 9 * (dx + 1)].reshape(9 * C, C).T
    leaving = []

    def finish(b, pre):
        mask = occ[b : b + 1, :].astype(F32)
        sig = jax.nn.sigmoid(pre)
        out[b] = (feat[b].astype(F32) + mask * (pre * sig)).astype(BF16)
        leaving.extend(started(out_sems.at[b:], (out.at[b], out_out.at[b])))
        delta = grad[b].astype(F32) * mask * (sig * (1.0 + pre * (1.0 - sig)))
        delta_ref[b] = delta.astype(BF16)

    convolve(w3, taps, ends, finish)
    write_faces(
        delta_ref[...], pf[...], send, delta_own_ref, (lat0, lat1, lat2, lat3), (zf0, zf1), faces_z
    )
    kernel_terms(taps, delta_ref, around, terms_ref)
    core = lax.axis_index("c")
    keep_ref[...] = terms_ref[pl.ds(pl.multiple_of(core * HALF, HALF), HALF), :]
    give_ref[...] = terms_ref[pl.ds(pl.multiple_of((1 - core) * HALF, HALF), HALF), :]
    waited(*leaving)


def backward_kernel(
    occ_in, grad_in, w_in, src_in, down_in, up_in, delta_in, own_in,
    recv0, recv1, recv2, recv3, recv4, recv5,
    out_out,
    occ, grad, w, src, down, up, out, pool, slabs, halo, taps, w3, e, ends, sems, out_sems,
    delta, lateral, vertical,
):
    early = started(
        sems,
        *[(recv, lateral.at[k]) for k, recv in enumerate((recv0, recv1, recv2, recv3))],
        (recv4, vertical.at[0]), (recv5, vertical.at[1]), (own_in, pool.at[0:16]),
        (src_in, src), (down_in, down), (up_in, up), (delta_in, delta),
    )
    later = started(sems.at[11:], (w_in, w), (grad_in, grad), (occ_in, occ))
    fill_entries(e)
    waited(*early)
    fill_pool([lateral.at[k] for k in range(4)] + [vertical.at[0], vertical.at[1]], pool)
    build_taps(delta[...], pool, src, down, up, e, slabs, halo, taps)
    waited(*later)
    for i, dx in enumerate((0, 2, 1)):
        last = TAPS - 1 - 9 * dx
        w3[C * i : C * (i + 1), :] = jnp.concatenate([w[last - t] for t in range(9)], axis=1)
    leaving = []

    def finish(b, back):
        mask = occ[b : b + 1, :].astype(F32)
        out[b] = (grad[b].astype(F32) + mask * back).astype(BF16)
        leaving.extend(started(out_sems.at[b:], (out.at[b], out_out.at[b])))

    convolve(w3, taps, ends, finish)
    waited(*leaving)


def sum_kernel(pieces_ref, out_ref):
    total = pieces_ref[0]
    for i in range(1, pieces_ref.shape[0]):
        total = total + pieces_ref[i]
    total = total.astype(out_ref.dtype)
    for i in range(out_ref.shape[0]):
        out_ref[i] = total


def unpack_kernel(mine_ref, other_ref, out_ref, packed):
    core = lax.axis_index("c")
    packed[pl.ds(pl.multiple_of(core * HALF, HALF), HALF), :] = mine_ref[...].astype(F32) * SCALE
    packed[pl.ds(pl.multiple_of((1 - core) * HALF, HALF), HALF), :] = other_ref[...].astype(F32) * SCALE
    rows = 9 * C
    out_ref[0:rows, :] = packed[0:rows, 0:C]
    out_ref[2 * rows :, 0:32] = packed[0:rows, C:128]
    out_ref[2 * rows :, 32:C] = packed[rows : 2 * rows, 0:64]
    out_ref[rows : 2 * rows, 0:64] = packed[rows : 2 * rows, 64:128]
    for g in range(4):
        out_ref[rows + REST * g : rows + REST * (g + 1), 64:C] = packed[
            2 * rows : 2 * rows + REST, 32 * g : 32 * (g + 1)
        ]


VM = pl.BlockSpec(memory_space=pltpu.VMEM)
HB = pl.BlockSpec(memory_space=pltpu.HBM)
MIB = 1024 * 1024


def call(kernel, ins, outs, scratch=(), flops=0, moved=0, limit=8 * MIB):
    return pl.pallas_call(
        kernel,
        in_specs=ins,
        out_specs=[spec for spec, _, _ in outs],
        out_shape=[jax.ShapeDtypeStruct(shape, kind) for _, shape, kind in outs],
        scratch_shapes=list(scratch),
        compiler_params=pltpu.CompilerParams(vmem_limit_bytes=limit),
        cost_estimate=pl.CostEstimate(flops=flops, bytes_accessed=moved, transcendentals=0),
    )


FACE_OUTS = [(VM, (16, C, 128), BF16)] + [(VM, (C, 128), BF16)] * 4 + [(VM, (2, C, 128), BF16)] * 2
BLOCKS = (NB, C, V)
FEAT, OCC = pltpu.VMEM(BLOCKS, BF16), pltpu.VMEM((NB, V), jnp.int32)
PF, SEND = pltpu.VMEM((V, 768), BF16), pltpu.SMEM((1, 2, 4), jnp.int32)
FACES_Z = pltpu.VMEM((2, 2, C, 128), BF16)
SCRATCH = [
    OCC,
    pltpu.VMEM(BLOCKS, BF16),
    pltpu.VMEM((TAPS, C, C), BF16),
    pltpu.SMEM((NB, 4), jnp.int32),
    pltpu.SMEM((NB,), jnp.int32),
    pltpu.SMEM((NB,), jnp.int32),
    pltpu.VMEM(BLOCKS, BF16),
    pltpu.VMEM((35, C, 128), BF16),
    pltpu.VMEM((NB * C, 256), BF16),
    pltpu.VMEM((NB * C, V), BF16),
    pltpu.VMEM((9 * C, MAIN + NB * 128), BF16),
    pltpu.VMEM((3 * C, 9 * C), BF16),
    pltpu.VMEM((256, 9 * V), BF16),
    pltpu.VMEM((2 * C, NB * 128), F32),
    pltpu.SemaphoreType.DMA((16,)),
    pltpu.SemaphoreType.DMA((NB,)),
]


def exchange(lat0, lat1, lat2, lat3, zf0, zf1):
    pairs = [(i, i + 1) for i in range(16)]
    flip2 = [(0, 1), (1, 0)]
    return [
        lax.ppermute(lat0, "c", flip2),
        lax.ppermute(lat1, "zh", flip2),
        lax.ppermute(lat2, "y", [(i, i ^ 1) for i in range(4)]),
        lax.ppermute(lat3, "y", [(i, i ^ 2) for i in range(4)]),
        lax.ppermute(zf0, BAND, [p for i, j in pairs[0:15:2] for p in ((i, j), (j, i))]),
        lax.ppermute(zf1, BAND, [p for i, j in pairs[1:15:2] for p in ((i, j), (j, i))]),
    ]


def exchanged(pieces, axes):
    return lax.all_to_all(pieces, axes, 0, 0, tiled=True)


def summed(pieces, count, kind):
    (out,) = call(
        sum_kernel, [VM], [(VM, (count, 64, 128), kind)], flops=pieces.size, moved=4 * pieces.size
    )(pieces)
    return out


def in_hbm(*values):
    return [pltpu.with_memory_space_constraint(value, pltpu.HBM) for value in values]


def on_device(features, occupancy, weights, grad_out, lat_src, down_src, up_src, send_faces):
    pf = jnp.asarray(face_matrix(), BF16)
    sends = send_faces.transpose(0, 2, 1)
    own, *out = call(
        faces_kernel, [HB] * 4, FACE_OUTS,
        [FEAT, OCC, PF, SEND, FACES_Z, pltpu.SemaphoreType.DMA((4,))],
    )(*in_hbm(features, occupancy, pf, sends))
    half = (VM, (HALF, 128), F32)
    layer_out, delta, keep, give, delta_own, *out = call(
        forward_kernel,
        [HB] * 9 + [VM] * 7,
        [(HB, BLOCKS, BF16), (VM, BLOCKS, BF16), half, half] + FACE_OUTS,
        SCRATCH
        + [FEAT, PF, SEND, FACES_Z, pltpu.VMEM((ROWS, 128), F32)]
        + [pltpu.VMEM((2 * C, MAIN + NB * 128), BF16)],
        limit=VMEM_LIMIT,
    )(
        *in_hbm(features, occupancy, grad_out, weights, pf, lat_src, down_src, up_src, sends),
        own,
        *exchange(*out),
    )
    halos = exchange(*out)
    part = keep + lax.ppermute(give, "c", [(0, 1), (1, 0)])
    part = exchanged(part.reshape(16, HALF // 16, 128), PLANE)
    part, *halos[:4] = lax.optimization_barrier((part, *halos[:4]))
    part = exchanged(summed(part, 8, F32), COLUMN)
    part, *halos[4:] = lax.optimization_barrier((part, *halos[4:]))
    part = exchanged(summed(part, 16, BF16), PLANE)
    (input_grad,) = call(
        backward_kernel,
        [HB] * 14,
        [(HB, BLOCKS, BF16)],
        SCRATCH + [FEAT, pltpu.VMEM((4, C, 128), BF16), pltpu.VMEM((2, 2, C, 128), BF16)],
        flops=5 * 10**9, moved=4 * 10**6, limit=VMEM_LIMIT,
    )(
        *in_hbm(occupancy, grad_out, weights, lat_src, down_src, up_src, delta, delta_own),
        *in_hbm(*halos),
    )
    mine, input_grad = lax.optimization_barrier((part.reshape(HALF, 128), input_grad))
    other = lax.ppermute(mine, "c", [(0, 1), (1, 0)])
    (weight_grad,) = call(
        unpack_kernel, [VM, VM], [(VM, (TAPS * C, C), F32)], [pltpu.VMEM((ROWS, 128), F32)]
    )(mine, other)
    return layer_out, input_grad, weight_grad.reshape(TAPS, C, C)


def solution(mesh):
    fine = Mesh(mesh.devices.reshape(4, 2, 2, 4, 4), EVERY)
    split = P(EVERY)
    return jax.shard_map(
        on_device,
        mesh=fine,
        in_specs=(split, split, P(), split, split, split, split, split),
        out_specs=(split, split, P()),
        check_vma=False,
    )
```

time: 110 us -> 85.2 us (0.77)
  the two profiles are of different devices: /device:TPU:6 before, /device:TPU:1 now
where the time goes in v2:
time: 85.2 us; the launch traced here: 84.7 us
  starting transfers between devices  44.7 us (52%)
  waiting for transfers between devices  20.6 us (24%)
  Pallas kernels  17.7 us (21%)
  other arithmetic  0.87 us (1%)
    all_to_all x3, starting transfers between devices, exchanged(): return lax.all_to_all(pieces, axes, 0, 0, tiled=True)  16 us
    all_to_all x3, waiting for transfers between devices, exchanged(): return lax.all_to_all(pieces, axes, 0, 0, tiled=True)  8.99 us
    ppermute x2, starting transfers between devices, exchange(): lax.ppermute(lat1, 'zh', flip2)  7.62 us
    pallas_call x1, Pallas kernels, on_device(): call(forward_kernel, [HB] * 9 + [VM] * 7, [(HB, BLOCKS, BF16), (VM, BLOCK...  7.44 us
    pallas_call x1, Pallas kernels, on_device(): call(backward_kernel, [HB] * 14, [(HB, BLOCKS, BF16)], SCRATCH + [FEAT, p...  5.28 us
    ppermute x1, starting transfers between devices, on_device(): other = lax.ppermute(mine, 'c', [(0, 1), (1, 0)])  5.19 us
    ppermute x2, starting transfers between devices, exchange(): lax.ppermute(lat3, 'y', [(i, i ^ 2) for i in range(4)])  5.02 us
    ppermute x2, waiting for transfers between devices, exchange(): lax.ppermute(lat3, 'y', [(i, i ^ 2) for i in range(4)])  4.76 us
  transfers between devices with their start and end apart: 17, of which 8 were waited for; matrix products, arithmetic and copies ran while one was open for 0% of the time, Pallas kernels for 6%

profile of v2, /device:TPU:1, one launch (start us, length us, event | category | flops | bytes accessed | tf_op | source)
XLA Modules:
  0.0 84.7 jit_solution(17853197664676245032)
XLA Ops:
  0.6 1.8 %shard_map.112 = (bf16[16,96,128]{2,1,0:T(8,128)(2,1)S(1)}, bf16[96,128]{1,0:T(8,128)(2,1)S(1)}, bf16[96,128]{1,0:T(8,128)(2,1)S(1)}, bf16[96,128]{1,0:T(8,128)(...) custom-call(bf16[4,96,512]{2,1,0:T(8,128)(2,1)} %feat_in.3, ...), custom_call_target="tpu_custom_call" | custom-call | tf_op jit(solution)/shard_map/pallas_call | solution.py:373
  2.5 3.3 %collective-permute-start = (bf16[96,128]{1,0:T(8,128)(2,1)S(1)}, bf16[96,128]{1,0:T(8,128)(2,1)S(1)}, u32[]{:S(2)}, u32[]{:S(2)}) collective-permute-start(bf16[96,128]{1,0:T(8,128)(2,1)S(1)} %get-tuple-element.32), channel_id=1, source_target_pairs={{0,16},{16,0},{1,17},{17,1},{2,18},{18,2},{3,19},{19,3},{4,20},{20... | collective-permute-start | bytes 73736 | tf_op jit(solution)/shard_map/ppermute | solution.py:346
  5.8 0.0 collective-permute-start.4
  5.8 0.7 collective-permute-start.5
  6.5 6.5 %collective-permute-start.1 = (bf16[96,128]{1,0:T(8,128)(2,1)S(1)}, bf16[96,128]{1,0:T(8,128)(2,1)S(1)}, u32[]{:S(2)}, u32[]{:S(2)}) collective-permute-start(bf16[96,128]{1,0:T(8,128)(2,1)S(1)} %get-tuple-element.33), channel_id=1, source_target_pairs={{0,32},{32,0},{1,33},{33,1},{2,34},{34,2},{3,35},{35,3},{4,36},{36... | collective-permute-start | bytes 73736 | tf_op jit(solution)/shard_map/ppermute | solution.py:347
  13.0 1.3 %collective-permute-start.2 = (bf16[96,128]{1,0:T(8,128)(2,1)S(1)}, bf16[96,128]{1,0:T(8,128)(2,1)S(1)}, u32[]{:S(2)}, u32[]{:S(2)}) collective-permute-start(bf16[96,128]{1,0:T(8,128)(2,1)S(1)} %get-tuple-element.34), channel_id=1, source_target_pairs={{0,64},{64,0},{128,192},{192,128},{1,65},{65,1},{129,193},{193,129... | collective-permute-start | bytes 73736 | tf_op jit(solution)/shard_map/ppermute | solution.py:348
  14.2 0.0 collective-permute-done.recv0
  14.3 2.6 %collective-permute-start.3 = (bf16[96,128]{1,0:T(8,128)(2,1)S(1)}, bf16[96,128]{1,0:T(8,128)(2,1)S(1)}, u32[]{:S(2)}, u32[]{:S(2)}) collective-permute-start(bf16[96,128]{1,0:T(8,128)(2,1)S(1)} %get-tuple-element.35), channel_id=1, source_target_pairs={{0,128},{64,192},{128,0},{192,64},{1,129},{65,193},{129,1},{193,65... | collective-permute-start | bytes 73736 | tf_op jit(solution)/shard_map/ppermute | solution.py:349
  16.9 0.0 collective-permute-done.1.recv1
  16.9 0.0 collective-permute-done.2.recv2
  16.9 1.6 %collective-permute-done.3.recv3 = bf16[96,128]{1,0:T(8,128)(2,1)S(1)} collective-permute-done((bf16[96,128]{1,0:T(8,128)(2,1)S(1)}, bf16[96,128]{1,0:T(8,128)(2,1)S(1)}, u32[]{:S(2)}, u32[]{:S(2)}) %collective-permute-start.3) | collective-permute-done | bytes 24608 | tf_op jit(solution)/shard_map/ppermute | solution.py:349
  18.4 0.0 collective-permute-done.4.recv4
  18.4 0.0 collective-permute-done.5.recv5
  18.4 7.4 %shard_map.113 = (bf16[4,96,512]{2,1,0:T(8,128)(2,1)}, bf16[4,96,512]{2,1,0:T(8,128)(2,1)S(1)}, f32[1024,128]{1,0:T(8,128)S(1)}, f32[1024,128]{1,0:T(8,128)S(1)}...) custom-call(bf16[4,96,512]{2,1,0:T(8,128)(2,1)} %feat_in.3, ...), custom_call_target="tpu_custom_call" | custom-call | tf_op jit(solution)/shard_map/pallas_call | solution.py:378
  25.9 0.0 copy-start
  25.9 0.0 copy-start.1
  25.9 2.2 %collective-permute-start.6 = (f32[1024,128]{1,0:T(8,128)S(1)}, f32[1024,128]{1,0:T(8,128)S(1)}, u32[]{:S(2)}, u32[]{:S(2)}) collective-permute-start(f32[1024,128]{1,0:T(8,128)S(1)} %get-tuple-element.40), channel_id=1, source_target_pairs={{0,16},{16,0},{1,17},{17,1},{2,18},{18,2},{3,19},{19,3},{4,20},{20... | collective-permute-start | bytes 1572872 | tf_op jit(solution)/shard_map/ppermute | solution.py:392
  28.1 1.5 %collective-permute-done.6 = f32[1024,128]{1,0:T(8,128)S(1)} collective-permute-done((f32[1024,128]{1,0:T(8,128)S(1)}, f32[1024,128]{1,0:T(8,128)S(1)}, u32[]{:S(2)}, u32[]{:S(2)}) %collective-permute-start.6) | collective-permute-done | bytes 524320 | tf_op jit(solution)/shard_map/ppermute | solution.py:392
  29.6 0.9 %add.3 = f32[1024,128]{1,0:T(8,128)} add(f32[1024,128]{1,0:T(8,128)S(1)} %get-tuple-element.39, f32[1024,128]{1,0:T(8,128)S(1)} %collective-permute-done.6) | non-fusion elementwise | flops 131072 | bytes 1572864 | tf_op jit(solution)/shard_map/add | solution.py:392
  30.5 0.0 copy-done
  30.5 0.0 copy-done.1
  30.5 8.4 %all-to-all-start = ((f32[16,64,128]{2,1,0:T(8,128)}), f32[16,64,128]{2,1,0:T(8,128)S(1)}, u32[]{:S(2)}, u32[]{:S(2)}) async-start(f32[16,64,128]{2,1,0:T(8,128)} %bitcast.1), calls=%async_computation | async-start | bytes 1048576 | tf_op jit(solution)/shard_map/all_to_all | solution.py:356
  38.9 0.7 collective-permute-start.7
  39.6 1.1 %collective-permute-start.8 = (bf16[96,128]{1,0:T(8,128)(2,1)S(1)}, bf16[96,128]{1,0:T(8,128)(2,1)S(1)}, u32[]{:S(2)}, u32[]{:S(2)}) collective-permute-start(bf16[96,128]{1,0:T(8,128)(2,1)S(1)} %get-tuple-element.42), channel_id=1, source_target_pairs={{0,32},{32,0},{1,33},{33,1},{2,34},{34,2},{3,35},{35,3},{4,36},{36... | collective-permute-start | bytes 73736 | tf_op jit(solution)/shard_map/ppermute | solution.py:347
  40.7 1.6 %collective-permute-start.9 = (bf16[96,128]{1,0:T(8,128)(2,1)S(1)}, bf16[96,128]{1,0:T(8,128)(2,1)S(1)}, u32[]{:S(2)}, u32[]{:S(2)}) collective-permute-start(bf16[96,128]{1,0:T(8,128)(2,1)S(1)} %get-tuple-element.43), channel_id=1, source_target_pairs={{0,64},{64,0},{128,192},{192,128},{1,65},{65,1},{129,193},{193,129... | collective-permute-start | bytes 73736 | tf_op jit(solution)/shard_map/ppermute | solution.py:348
  42.3 2.4 %collective-permute-start.10 = (bf16[96,128]{1,0:T(8,128)(2,1)S(1)}, bf16[96,128]{1,0:T(8,128)(2,1)S(1)}, u32[]{:S(2)}, u32[]{:S(2)}) collective-permute-start(bf16[96,128]{1,0:T(8,128)(2,1)S(1)} %get-tuple-element.44), channel_id=1, source_target_pairs={{0,128},{64,192},{128,0},{192,64},{1,129},{65,193},{129,1},{193,65... | collective-permute-start | bytes 73736 | tf_op jit(solution)/shard_map/ppermute | solution.py:349
  44.7 0.0 collective-permute-done.7.recv0
  44.7 0.0 copy-start.4
  44.7 2.0 %collective-permute-done.8.recv1 = bf16[96,128]{1,0:T(8,128)(2,1)S(1)} collective-permute-done((bf16[96,128]{1,0:T(8,128)(2,1)S(1)}, bf16[96,128]{1,0:T(8,128)(2,1)S(1)}, u32[]{:S(2)}, u32[]{:S(2)}) %collective-permute-start.8) | collective-permute-done | bytes 24608 | tf_op jit(solution)/shard_map/ppermute | solution.py:347
  46.8 0.0 copy-start.5
  46.8 0.0 collective-permute-done.9.recv2
  46.8 0.0 copy-start.6
  46.8 3.2 %collective-permute-done.10.recv3 = bf16[96,128]{1,0:T(8,128)(2,1)S(1)} collective-permute-done((bf16[96,128]{1,0:T(8,128)(2,1)S(1)}, bf16[96,128]{1,0:T(8,128)(2,1)S(1)}, u32[]{:S(2)}, u32[]{:S(2)}) %collective-permute-start.10) | collective-permute-done | bytes 24608 | tf_op jit(solution)/shard_map/ppermute | solution.py:349
  50.0 0.0 copy-start.7
  50.0 0.0 all-to-all-done.pieces_ref
  50.0 0.7 shard_map.114
  50.7 3.4 %all-to-all-start.1 = ((f32[8,64,128]{2,1,0:T(8,128)}), f32[8,64,128]{2,1,0:T(8,128)S(1)}, u32[]{:S(2)}, u32[]{:S(2)}) async-start(f32[8,64,128]{2,1,0:T(8,128)} %shard_map.114), calls=%async_computation.1 | async-start | bytes 524288 | tf_op jit(solution)/shard_map/all_to_all | solution.py:356
  54.1 0.5 collective-permute-start.11
  54.6 0.7 collective-permute-start.12
  55.3 2.1 %collective-permute-done.11.recv4 = bf16[2,96,128]{2,1,0:T(8,128)(2,1)S(1)} collective-permute-done((bf16[2,96,128]{2,1,0:T(8,128)(2,1)S(1)}, bf16[2,96,128]{2,1,0:T(8,128)(2,1)S(1)}, u32[]{:S(2)}, u32[]{:S(2)}) %collective-permute-start.11) | collective-permute-done | bytes 49184 | tf_op jit(solution)/shard_map/ppermute | solution.py:350
  57.3 0.0 copy-start.2
  57.3 0.0 collective-permute-done.12.recv5
  57.4 0.0 copy-start.3
  57.4 6.8 %all-to-all-done.1.pieces_ref = f32[8,64,128]{2,1,0:T(8,128)S(1)} async-done(((f32[8,64,128]{2,1,0:T(8,128)}), f32[8,64,128]{2,1,0:T(8,128)S(1)}, u32[]{:S(2)}, u32[]{:S(2)}) %all-to-all-start.1) | async-done | bytes 262176 | tf_op jit(solution)/shard_map/all_to_all | solution.py:356
  64.1 0.7 shard_map.115
  64.9 4.2 %all-to-all-start.2 = ((bf16[16,64,128]{2,1,0:T(8,128)(2,1)}), bf16[16,64,128]{2,1,0:T(8,128)(2,1)S(1)}, u32[]{:S(2)}, u32[]{:S(2)}) async-start(bf16[16,64,128]{2,1,0:T(8,128)(2,1)} %shard_map.115), calls=%async_computation.2 | async-start | bytes 524288 | tf_op jit(solution)/shard_map/all_to_all | solution.py:356
  69.1 0.0 copy-done.4
  69.1 0.0 copy-done.5
  69.1 0.0 copy-done.6
  69.1 0.0 copy-done.7
  69.1 0.0 copy-done.2
  69.2 0.0 copy-done.3
  69.2 5.3 %shard_map.116 = bf16[4,96,512]{2,1,0:T(8,128)(2,1)} custom-call(s32[4,512]{1,0:T(4,128)} %occ_in.5, bf16[4,96,512]{2,1,0:T(8,128)(2,1)} %grad_in.3, bf16[27,96,96]{2,1,0:T(8,128)(2,1)} %w_in.3, s32[4,4]{1,0:T(4,128)} %src_in.3, s32[4]{0:T(128)} %down_in.3, s32[4]{0:T(128)} %up_in.3, bf16[4,96,512]{2,1,0:T(8,128)(2,1)} %copy-done, ...), custom_call_target="tpu_custom_call" | custom-call | flops 5000000000 | bytes 4000000 | tf_op jit(solution)/shard_map/pallas_call | solution.py:398
  74.5 2.2 %all-to-all-done.2 = bf16[16,64,128]{2,1,0:T(8,128)(2,1)S(1)} async-done(((bf16[16,64,128]{2,1,0:T(8,128)(2,1)}), bf16[16,64,128]{2,1,0:T(8,128)(2,1)S(1)}, u32[]{:S(2)}, u32[]{:S(2)}) %all-to-all-start.2) | async-done | bytes 262176 | tf_op jit(solution)/shard_map/all_to_all | solution.py:356
  76.6 5.2 %collective-permute-start.13 = (bf16[1024,128]{1,0:T(8,128)(2,1)S(1)}, bf16[1024,128]{1,0:T(8,128)(2,1)S(1)}, u32[]{:S(2)}, u32[]{:S(2)}) collective-permute-start(bf16[1024,128]{1,0:T(8,128)(2,1)S(1)} %bitcast.4), channel_id=1, source_target_pairs={{0,16},{16,0},{1,17},{17,1},{2,18},{18,2},{3,19},{19,3},{4,20},{20... | collective-permute-start | bytes 786440 | tf_op jit(solution)/shard_map/ppermute | solution.py:409
  81.8 1.2 %collective-permute-done.13.other_ref = bf16[1024,128]{1,0:T(8,128)(2,1)S(1)} collective-permute-done((bf16[1024,128]{1,0:T(8,128)(2,1)S(1)}, bf16[1024,128]{1,0:T(8,128)(2,1)S(1)}, u32[]{:S(2)}, u32[]{:S(2)}) %collective-permute-start.13) | collective-permute-done | bytes 262176 | tf_op jit(solution)/shard_map/ppermute | solution.py:409
  83.0 1.7 %shard_map.117 = f32[2592,96]{1,0:T(8,128)} custom-call(bf16[1024,128]{1,0:T(8,128)(2,1)S(1)} %bitcast.5, bf16[1024,128]{1,0:T(8,128)(2,1)S(1)} %collective-permute-done.13.other_ref), custom_call_target="tpu_custom_call" | custom-call | tf_op jit(solution)/shard_map/pallas_call | solution.py:410
Async XLA Ops:
  2.5 11.8 %collective-permute-start = (bf16[96,128]{1,0:T(8,128)(2,1)S(1)}, bf16[96,128]{1,0:T(8,128)(2,1)S(1)}, u32[]{:S(2)}, u32[]{:S(2)}) collective-permute-start(bf16[96,128]{1,0:T(8,128)(2,1)S(1)} %get-tuple-element.32), channel_id=1, source_target_pairs={{0,16},{16,0},{1,17},{17,1},{2,18},{18,2},{3,19},{19,3},{4,20},{20... | collective-permute-start | bytes 73736 | tf_op jit(solution)/shard_map/ppermute | solution.py:346
  5.8 12.6 %collective-permute-start.4 = (bf16[2,96,128]{2,1,0:T(8,128)(2,1)S(1)}, bf16[2,96,128]{2,1,0:T(8,128)(2,1)S(1)}, u32[]{:S(2)}, u32[]{:S(2)}) collective-permute-start(bf16[2,96,128]{2,1,0:T(8,128)(2,1)S(1)} %get-tuple-element.36), channel_id=1, source_target_pairs={{0,1},{1,0},{2,3},{3,2},{4,5},{5,4},{6,7},{7,6},{8,9},{9,8},{10,11... | collective-permute-start | bytes 147464 | tf_op jit(solution)/shard_map/ppermute | solution.py:350
  5.8 12.6 %collective-permute-start.5 = (bf16[2,96,128]{2,1,0:T(8,128)(2,1)S(1)}, bf16[2,96,128]{2,1,0:T(8,128)(2,1)S(1)}, u32[]{:S(2)}, u32[]{:S(2)}) collective-permute-start(bf16[2,96,128]{2,1,0:T(8,128)(2,1)S(1)} %get-tuple-element.37), channel_id=1, source_target_pairs={{1,2},{2,1},{3,4},{4,3},{5,6},{6,5},{7,8},{8,7},{9,10},{10,9},{11,... | collective-permute-start | bytes 147464 | tf_op jit(solution)/shard_map/ppermute | solution.py:351
  6.5 10.4 %collective-permute-start.1 = (bf16[96,128]{1,0:T(8,128)(2,1)S(1)}, bf16[96,128]{1,0:T(8,128)(2,1)S(1)}, u32[]{:S(2)}, u32[]{:S(2)}) collective-permute-start(bf16[96,128]{1,0:T(8,128)(2,1)S(1)} %get-tuple-element.33), channel_id=1, source_target_pairs={{0,32},{32,0},{1,33},{33,1},{2,34},{34,2},{3,35},{35,3},{4,36},{36... | collective-permute-start | bytes 73736 | tf_op jit(solution)/shard_map/ppermute | solution.py:347
  13.0 3.9 %collective-permute-start.2 = (bf16[96,128]{1,0:T(8,128)(2,1)S(1)}, bf16[96,128]{1,0:T(8,128)(2,1)S(1)}, u32[]{:S(2)}, u32[]{:S(2)}) collective-permute-start(bf16[96,128]{1,0:T(8,128)(2,1)S(1)} %get-tuple-element.34), channel_id=1, source_target_pairs={{0,64},{64,0},{128,192},{192,128},{1,65},{65,1},{129,193},{193,129... | collective-permute-start | bytes 73736 | tf_op jit(solution)/shard_map/ppermute | solution.py:348
  14.3 4.2 %collective-permute-start.3 = (bf16[96,128]{1,0:T(8,128)(2,1)S(1)}, bf16[96,128]{1,0:T(8,128)(2,1)S(1)}, u32[]{:S(2)}, u32[]{:S(2)}) collective-permute-start(bf16[96,128]{1,0:T(8,128)(2,1)S(1)} %get-tuple-element.35), channel_id=1, source_target_pairs={{0,128},{64,192},{128,0},{192,64},{1,129},{65,193},{129,1},{193,65... | collective-permute-start | bytes 73736 | tf_op jit(solution)/shard_map/ppermute | solution.py:349
  25.9 4.6 %copy-start = (bf16[4,96,512]{2,1,0:T(8,128)(2,1)}, bf16[4,96,512]{2,1,0:T(8,128)(2,1)S(1)}, u32[]{:S(2)}) copy-start(bf16[4,96,512]{2,1,0:T(8,128)(2,1)S(1)} %get-tuple-element.49.delta_in) | copy-start | bytes 1179652
  25.9 4.6 %copy-start.1 = (bf16[16,96,128]{2,1,0:T(8,128)(2,1)}, bf16[16,96,128]{2,1,0:T(8,128)(2,1)S(1)}, u32[]{:S(2)}) copy-start(bf16[16,96,128]{2,1,0:T(8,128)(2,1)S(1)} %get-tuple-element.50.own_in) | copy-start | bytes 1179652
  25.9 3.7 %collective-permute-start.6 = (f32[1024,128]{1,0:T(8,128)S(1)}, f32[1024,128]{1,0:T(8,128)S(1)}, u32[]{:S(2)}, u32[]{:S(2)}) collective-permute-start(f32[1024,128]{1,0:T(8,128)S(1)} %get-tuple-element.40), channel_id=1, source_target_pairs={{0,16},{16,0},{1,17},{17,1},{2,18},{18,2},{3,19},{19,3},{4,20},{20... | collective-permute-start | bytes 1572872 | tf_op jit(solution)/shard_map/ppermute | solution.py:392
  30.5 19.5 %all-to-all-start = ((f32[16,64,128]{2,1,0:T(8,128)}), f32[16,64,128]{2,1,0:T(8,128)S(1)}, u32[]{:S(2)}, u32[]{:S(2)}) async-start(f32[16,64,128]{2,1,0:T(8,128)} %bitcast.1), calls=%async_computation | async-start | bytes 1048576 | tf_op jit(solution)/shard_map/all_to_all | solution.py:356
  38.9 5.8 %collective-permute-start.7 = (bf16[96,128]{1,0:T(8,128)(2,1)S(1)}, bf16[96,128]{1,0:T(8,128)(2,1)S(1)}, u32[]{:S(2)}, u32[]{:S(2)}) collective-permute-start(bf16[96,128]{1,0:T(8,128)(2,1)S(1)} %get-tuple-element.41), channel_id=1, source_target_pairs={{0,16},{16,0},{1,17},{17,1},{2,18},{18,2},{3,19},{19,3},{4,20},{20... | collective-permute-start | bytes 73736 | tf_op jit(solution)/shard_map/ppermute | solution.py:346
  39.6 7.1 %collective-permute-start.8 = (bf16[96,128]{1,0:T(8,128)(2,1)S(1)}, bf16[96,128]{1,0:T(8,128)(2,1)S(1)}, u32[]{:S(2)}, u32[]{:S(2)}) collective-permute-start(bf16[96,128]{1,0:T(8,128)(2,1)S(1)} %get-tuple-element.42), channel_id=1, source_target_pairs={{0,32},{32,0},{1,33},{33,1},{2,34},{34,2},{3,35},{35,3},{4,36},{36... | collective-permute-start | bytes 73736 | tf_op jit(solution)/shard_map/ppermute | solution.py:347
  40.7 6.0 %collective-permute-start.9 = (bf16[96,128]{1,0:T(8,128)(2,1)S(1)}, bf16[96,128]{1,0:T(8,128)(2,1)S(1)}, u32[]{:S(2)}, u32[]{:S(2)}) collective-permute-start(bf16[96,128]{1,0:T(8,128)(2,1)S(1)} %get-tuple-element.43), channel_id=1, source_target_pairs={{0,64},{64,0},{128,192},{192,128},{1,65},{65,1},{129,193},{193,129... | collective-permute-start | bytes 73736 | tf_op jit(solution)/shard_map/ppermute | solution.py:348
  42.3 7.7 %collective-permute-start.10 = (bf16[96,128]{1,0:T(8,128)(2,1)S(1)}, bf16[96,128]{1,0:T(8,128)(2,1)S(1)}, u32[]{:S(2)}, u32[]{:S(2)}) collective-permute-start(bf16[96,128]{1,0:T(8,128)(2,1)S(1)} %get-tuple-element.44), channel_id=1, source_target_pairs={{0,128},{64,192},{128,0},{192,64},{1,129},{65,193},{129,1},{193,65... | collective-permute-start | bytes 73736 | tf_op jit(solution)/shard_map/ppermute | solution.py:349
  44.7 24.4 %copy-start.4 = (bf16[96,128]{1,0:T(8,128)(2,1)}, bf16[96,128]{1,0:T(8,128)(2,1)S(1)}, u32[]{:S(2)}) copy-start(bf16[96,128]{1,0:T(8,128)(2,1)S(1)} %collective-permute-done.7.recv0) | copy-start | bytes 73732
  46.8 22.4 %copy-start.5 = (bf16[96,128]{1,0:T(8,128)(2,1)}, bf16[96,128]{1,0:T(8,128)(2,1)S(1)}, u32[]{:S(2)}) copy-start(bf16[96,128]{1,0:T(8,128)(2,1)S(1)} %collective-permute-done.8.recv1) | copy-start | bytes 73732
  46.8 22.4 %copy-start.6 = (bf16[96,128]{1,0:T(8,128)(2,1)}, bf16[96,128]{1,0:T(8,128)(2,1)S(1)}, u32[]{:S(2)}) copy-start(bf16[96,128]{1,0:T(8,128)(2,1)S(1)} %collective-permute-done.9.recv2) | copy-start | bytes 73732
  50.0 19.2 %copy-start.7 = (bf16[96,128]{1,0:T(8,128)(2,1)}, bf16[96,128]{1,0:T(8,128)(2,1)S(1)}, u32[]{:S(2)}) copy-start(bf16[96,128]{1,0:T(8,128)(2,1)S(1)} %collective-permute-done.10.recv3) | copy-start | bytes 73732
  50.7 13.4 %all-to-all-start.1 = ((f32[8,64,128]{2,1,0:T(8,128)}), f32[8,64,128]{2,1,0:T(8,128)S(1)}, u32[]{:S(2)}, u32[]{:S(2)}) async-start(f32[8,64,128]{2,1,0:T(8,128)} %shard_map.114), calls=%async_computation.1 | async-start | bytes 524288 | tf_op jit(solution)/shard_map/all_to_all | solution.py:356
  54.1 3.2 %collective-permute-start.11 = (bf16[2,96,128]{2,1,0:T(8,128)(2,1)S(1)}, bf16[2,96,128]{2,1,0:T(8,128)(2,1)S(1)}, u32[]{:S(2)}, u32[]{:S(2)}) collective-permute-start(bf16[2,96,128]{2,1,0:T(8,128)(2,1)S(1)} %get-tuple-element.46), channel_id=1, source_target_pairs={{0,1},{1,0},{2,3},{3,2},{4,5},{5,4},{6,7},{7,6},{8,9},{9,8},{10,11... | collective-permute-start | bytes 147464 | tf_op jit(solution)/shard_map/ppermute | solution.py:350
  54.6 2.7 %collective-permute-start.12 = (bf16[2,96,128]{2,1,0:T(8,128)(2,1)S(1)}, bf16[2,96,128]{2,1,0:T(8,128)(2,1)S(1)}, u32[]{:S(2)}, u32[]{:S(2)}) collective-permute-start(bf16[2,96,128]{2,1,0:T(8,128)(2,1)S(1)} %get-tuple-element.47), channel_id=1, source_target_pairs={{1,2},{2,1},{3,4},{4,3},{5,6},{6,5},{7,8},{8,7},{9,10},{10,9},{11,... | collective-permute-start | bytes 147464 | tf_op jit(solution)/shard_map/ppermute | solution.py:351
  57.3 11.8 %copy-start.2 = (bf16[2,96,128]{2,1,0:T(8,128)(2,1)}, bf16[2,96,128]{2,1,0:T(8,128)(2,1)S(1)}, u32[]{:S(2)}) copy-start(bf16[2,96,128]{2,1,0:T(8,128)(2,1)S(1)} %collective-permute-done.11.recv4) | copy-start | bytes 147460
  57.4 11.8 %copy-start.3 = (bf16[2,96,128]{2,1,0:T(8,128)(2,1)}, bf16[2,96,128]{2,1,0:T(8,128)(2,1)S(1)}, u32[]{:S(2)}) copy-start(bf16[2,96,128]{2,1,0:T(8,128)(2,1)S(1)} %collective-permute-done.12.recv5) | copy-start | bytes 147460
  64.9 11.8 %all-to-all-start.2 = ((bf16[16,64,128]{2,1,0:T(8,128)(2,1)}), bf16[16,64,128]{2,1,0:T(8,128)(2,1)S(1)}, u32[]{:S(2)}, u32[]{:S(2)}) async-start(bf16[16,64,128]{2,1,0:T(8,128)(2,1)} %shard_map.115), calls=%async_computation.2 | async-start | bytes 524288 | tf_op jit(solution)/shard_map/all_to_all | solution.py:356
  76.6 6.4 %collective-permute-start.13 = (bf16[1024,128]{1,0:T(8,128)(2,1)S(1)}, bf16[1024,128]{1,0:T(8,128)(2,1)S(1)}, u32[]{:S(2)}, u32[]{:S(2)}) collective-permute-start(bf16[1024,128]{1,0:T(8,128)(2,1)S(1)} %bitcast.4), channel_id=1, source_target_pairs={{0,16},{16,0},{1,17},{17,1},{2,18},{18,2},{3,19},{19,3},{4,20},{20... | collective-permute-start | bytes 786440 | tf_op jit(solution)/shard_map/ppermute | solution.py:409

commit v3 on v2

--- a/solution.py
+++ b/solution.py
@@ -193,29 +193,32 @@
         copy.wait()
 
 
-def faces_kernel(feat_in, occ_in, pf_in, send_in, own_ref, *refs):
+def faces_kernel(feat_in, occ_in, pf_in, send_in, masked_ref, own_ref, *refs):
     feat, occ, pf, send, faces_z, sems = refs[6:]
-    waited(*started(sems, (send_in, send), (occ_in, occ), (feat_in, feat), (pf_in, pf)))
-    write_faces(masked_of(feat, occ), pf[...], send, own_ref, refs[:4], refs[4:6], faces_z)
+    copies = started(sems, (send_in, send), (occ_in, occ), (feat_in, feat), (pf_in, pf))
+    waited(*copies[1:3])
+    masked_ref[...] = masked_of(feat, occ)
+    waited(copies[0], copies[3])
+    write_faces(masked_ref[...], pf[...], send, own_ref, refs[:4], refs[4:6], faces_z)
 
 
 def forward_kernel(
     feat_in, occ_in, grad_in, w_in, pf_in, src_in, down_in, up_in, send_in,
-    own_ref, recv0, recv1, recv2, recv3, recv4, recv5,
+    masked_ref, own_ref, recv0, recv1, recv2, recv3, recv4, recv5,
     out_out, delta_ref, keep_ref, give_ref, delta_own_ref, lat0, lat1, lat2, lat3, zf0, zf1,
     occ, grad, w, src, down, up, out, pool, slabs, halo, taps, w3, e, ends, sems, out_sems,
     feat, pf, send, faces_z, terms_ref, around,
 ):
-    early = started(
-        sems, (src_in, src), (down_in, down), (up_in, up), (occ_in, occ), (feat_in, feat),
-    )
-    later = started(sems.at[5:], (w_in, w), (grad_in, grad), (pf_in, pf), (send_in, send))
+    early = started(sems, (src_in, src), (down_in, down), (up_in, up))
+    later = started(
+        sems.at[3:], (w_in, w), (occ_in, occ), (feat_in, feat), (grad_in, grad), (pf_in, pf), (send_in, send)
+    )
     for i in range(16):
         pool[i] = own_ref[i]
     fill_pool((recv0, recv1, recv2, recv3, recv4, recv5), pool)
     fill_entries(e)
     waited(*early)
-    build_taps(masked_of(feat, occ), pool, src, down, up, e, slabs, halo, taps)
+    build_taps(masked_ref[...], pool, src, down, up, e, slabs, halo, taps)
     waited(*later)
     for i, dx in enumerate((0, 2, 1)):
         w3[C * i : C * (i + 1), :] = w[9 * dx : 9 * (dx + 1)].reshape(9 * C, C).T
@@ -282,19 +285,24 @@
         out_ref[i] = total
 
 
-def unpack_kernel(mine_ref, other_ref, out_ref, packed):
+def unpack_kernel(mine_ref, other_ref, out_out, packed, out, sems):
     core = lax.axis_index("c")
     packed[pl.ds(pl.multiple_of(core * HALF, HALF), HALF), :] = mine_ref[...].astype(F32) * SCALE
     packed[pl.ds(pl.multiple_of((1 - core) * HALF, HALF), HALF), :] = other_ref[...].astype(F32) * SCALE
     rows = 9 * C
-    out_ref[0:rows, :] = packed[0:rows, 0:C]
-    out_ref[2 * rows :, 0:32] = packed[0:rows, C:128]
-    out_ref[2 * rows :, 32:C] = packed[rows : 2 * rows, 0:64]
-    out_ref[rows : 2 * rows, 0:64] = packed[rows : 2 * rows, 64:128]
+    third = [pl.ds(rows * i, rows) for i in range(3)]
+    out[0:rows, :] = packed[0:rows, 0:C]
+    leaving = started(sems, (out.at[third[0]], out_out.at[third[0]]))
+    out[2 * rows :, 0:32] = packed[0:rows, C:128]
+    out[2 * rows :, 32:C] = packed[rows : 2 * rows, 0:64]
+    leaving += started(sems.at[1:], (out.at[third[2]], out_out.at[third[2]]))
+    out[rows : 2 * rows, 0:64] = packed[rows : 2 * rows, 64:128]
     for g in range(4):
-        out_ref[rows + REST * g : rows + REST * (g + 1), 64:C] = packed[
+        out[rows + REST * g : rows + REST * (g + 1), 64:C] = packed[
             2 * rows : 2 * rows + REST, 32 * g : 32 * (g + 1)
         ]
+    leaving += started(sems.at[2:], (out.at[third[1]], out_out.at[third[1]]))
+    waited(*leaving)
 
 
 VM = pl.BlockSpec(memory_space=pltpu.VMEM)
@@ -370,14 +378,14 @@
 def on_device(features, occupancy, weights, grad_out, lat_src, down_src, up_src, send_faces):
     pf = jnp.asarray(face_matrix(), BF16)
     sends = send_faces.transpose(0, 2, 1)
-    own, *out = call(
-        faces_kernel, [HB] * 4, FACE_OUTS,
+    masked, own, *out = call(
+        faces_kernel, [HB] * 4, [(VM, BLOCKS, BF16)] + FACE_OUTS,
         [FEAT, OCC, PF, SEND, FACES_Z, pltpu.SemaphoreType.DMA((4,))],
     )(*in_hbm(features, occupancy, pf, sends))
     half = (VM, (HALF, 128), F32)
     layer_out, delta, keep, give, delta_own, *out = call(
         forward_kernel,
-        [HB] * 9 + [VM] * 7,
+        [HB] * 9 + [VM] * 8,
         [(HB, BLOCKS, BF16), (VM, BLOCKS, BF16), half, half] + FACE_OUTS,
         SCRATCH
         + [FEAT, PF, SEND, FACES_Z, pltpu.VMEM((ROWS, 128), F32)]
@@ -385,15 +393,16 @@
         limit=VMEM_LIMIT,
     )(
         *in_hbm(features, occupancy, grad_out, weights, pf, lat_src, down_src, up_src, sends),
+        masked,
         own,
         *exchange(*out),
     )
     halos = exchange(*out)
     part = keep + lax.ppermute(give, "c", [(0, 1), (1, 0)])
     part = exchanged(part.reshape(16, HALF // 16, 128), PLANE)
-    part, *halos[:4] = lax.optimization_barrier((part, *halos[:4]))
+    part, halos[1], halos[2], halos[4] = lax.optimization_barrier((part, halos[1], halos[2], halos[4]))
     part = exchanged(summed(part, 8, F32), COLUMN)
-    part, *halos[4:] = lax.optimization_barrier((part, *halos[4:]))
+    part, halos[0], halos[3], halos[5] = lax.optimization_barrier((part, halos[0], halos[3], halos[5]))
     part = exchanged(summed(part, 16, BF16), PLANE)
     (input_grad,) = call(
         backward_kernel,
@@ -408,7 +417,8 @@
     mine, input_grad = lax.optimization_barrier((part.reshape(HALF, 128), input_grad))
     other = lax.ppermute(mine, "c", [(0, 1), (1, 0)])
     (weight_grad,) = call(
-        unpack_kernel, [VM, VM], [(VM, (TAPS * C, C), F32)], [pltpu.VMEM((ROWS, 128), F32)]
+        unpack_kernel, [VM, VM], [(HB, (TAPS * C, C), F32)],
+        [pltpu.VMEM((ROWS, 128), F32), pltpu.VMEM((TAPS * C, C), F32), pltpu.SemaphoreType.DMA((3,))],
     )(mine, other)
     return layer_out, input_grad, weight_grad.reshape(TAPS, C, C)
 

time: 85.2 us -> 83 us (0.974)
  waiting for transfers between devices: 20.6 us -> 19 us
    all_to_all x3, waiting for transfers between devices: 8.99 us -> 5.07 us  [exchanged(): return lax.all_to_all(pieces, axes, 0, 0, tiled=True)]
    ppermute x2, waiting for transfers between devices: 2.05 us -> 4.82 us  [exchange(): lax.ppermute(lat1, 'zh', flip2)]
    ppermute x2, waiting for transfers between devices: 2.07 us -> 0.01 us  [exchange(): lax.ppermute(zf0, BAND, [p for i, j in pairs[0:15:2] for p in ((i, j), (j...]
    ppermute x1, starting transfers between devices: 5.19 us -> 3.2 us  [on_device(): other = lax.ppermute(mine, 'c', [(0, 1), (1, 0)])]
    ppermute x2, starting transfers between devices: 4.07 us -> 5.9 us  [exchange(): lax.ppermute(lat0, 'c', flip2)]
    ppermute x2, starting transfers between devices: 5.02 us -> 3.21 us  [exchange(): lax.ppermute(lat3, 'y', [(i, i ^ 2) for i in range(4)])]
    all_to_all x3, starting transfers between devices: 16 us -> 17.4 us  [exchanged(): return lax.all_to_all(pieces, axes, 0, 0, tiled=True)]
    ppermute x2, waiting for transfers between devices: 0.01 us -> 1.27 us  [exchange(): lax.ppermute(lat2, 'y', [(i, i ^ 1) for i in range(4)])]
  transfers between devices with their start and end apart: 17 -> 17, of which waited for: 8 -> 10; matrix products, arithmetic and copies ran while one was open for 0% -> 0% of each run, Pallas kernels for 6% -> 6%
where the time goes in v3:
time: 83 us; the launch traced here: 82.5 us
  starting transfers between devices  44.6 us (54%)
  waiting for transfers between devices  19 us (23%)
  Pallas kernels  17.1 us (21%)
  between operations  0.94 us (1%)
  other arithmetic  0.87 us (1%)
    all_to_all x3, starting transfers between devices, exchanged(): return lax.all_to_all(pieces, axes, 0, 0, tiled=True)  17.4 us
    ppermute x2, starting transfers between devices, exchange(): lax.ppermute(lat1, 'zh', flip2)  7.62 us
    pallas_call x1, Pallas kernels, on_device(): call(forward_kernel, [HB] * 9 + [VM] * 8, [(HB, BLOCKS, BF16), (VM, BLOCK...  7.07 us
    ppermute x2, starting transfers between devices, exchange(): lax.ppermute(lat0, 'c', flip2)  5.9 us
    pallas_call x1, Pallas kernels, on_device(): call(backward_kernel, [HB] * 14, [(HB, BLOCKS, BF16)], SCRATCH + [FEAT, p...  5.28 us
    all_to_all x3, waiting for transfers between devices, exchanged(): return lax.all_to_all(pieces, axes, 0, 0, tiled=True)  5.07 us
    ppermute x2, waiting for transfers between devices, exchange(): lax.ppermute(lat3, 'y', [(i, i ^ 2) for i in range(4)])  4.9 us
    ppermute x2, waiting for transfers between devices, exchange(): lax.ppermute(lat1, 'zh', flip2)  4.82 us
  transfers between devices with their start and end apart: 17, of which 10 were waited for; matrix products, arithmetic and copies ran while one was open for 0% of the time, Pallas kernels for 6%

profile of v3, /device:TPU:1, one launch (start us, length us, event | category | flops | bytes accessed | tf_op | source)
XLA Modules:
  0.0 82.5 jit_solution(9410300396218918826)
XLA Ops:
  0.6 1.8 %shard_map.112 = (bf16[4,96,512]{2,1,0:T(8,128)(2,1)S(1)}, bf16[16,96,128]{2,1,0:T(8,128)(2,1)S(1)}, bf16[96,128]{1,0:T(8,128)(2,1)S(1)}, bf16[96,128]{1,0:T(8,1...) custom-call(bf16[4,96,512]{2,1,0:T(8,128)(2,1)} %feat_in.3, ...), custom_call_target="tpu_custom_call" | custom-call | tf_op jit(solution)/shard_map/pallas_call | solution.py:381
  2.5 3.3 %collective-permute-start = (bf16[96,128]{1,0:T(8,128)(2,1)S(1)}, bf16[96,128]{1,0:T(8,128)(2,1)S(1)}, u32[]{:S(2)}, u32[]{:S(2)}) collective-permute-start(bf16[96,128]{1,0:T(8,128)(2,1)S(1)} %get-tuple-element.34), channel_id=1, source_target_pairs={{0,16},{16,0},{1,17},{17,1},{2,18},{18,2},{3,19},{19,3},{4,20},{20... | collective-permute-start | bytes 73736 | tf_op jit(solution)/shard_map/ppermute | solution.py:354
  5.8 0.0 collective-permute-start.4
  5.8 0.7 collective-permute-start.5
  6.5 6.5 %collective-permute-start.1 = (bf16[96,128]{1,0:T(8,128)(2,1)S(1)}, bf16[96,128]{1,0:T(8,128)(2,1)S(1)}, u32[]{:S(2)}, u32[]{:S(2)}) collective-permute-start(bf16[96,128]{1,0:T(8,128)(2,1)S(1)} %get-tuple-element.35), channel_id=1, source_target_pairs={{0,32},{32,0},{1,33},{33,1},{2,34},{34,2},{3,35},{35,3},{4,36},{36... | collective-permute-start | bytes 73736 | tf_op jit(solution)/shard_map/ppermute | solution.py:355
  13.0 1.3 %collective-permute-start.2 = (bf16[96,128]{1,0:T(8,128)(2,1)S(1)}, bf16[96,128]{1,0:T(8,128)(2,1)S(1)}, u32[]{:S(2)}, u32[]{:S(2)}) collective-permute-start(bf16[96,128]{1,0:T(8,128)(2,1)S(1)} %get-tuple-element.36), channel_id=1, source_target_pairs={{0,64},{64,0},{128,192},{192,128},{1,65},{65,1},{129,193},{193,129... | collective-permute-start | bytes 73736 | tf_op jit(solution)/shard_map/ppermute | solution.py:356
  14.2 0.0 collective-permute-done.recv0
  14.3 2.6 %collective-permute-start.3 = (bf16[96,128]{1,0:T(8,128)(2,1)S(1)}, bf16[96,128]{1,0:T(8,128)(2,1)S(1)}, u32[]{:S(2)}, u32[]{:S(2)}) collective-permute-start(bf16[96,128]{1,0:T(8,128)(2,1)S(1)} %get-tuple-element.37), channel_id=1, source_target_pairs={{0,128},{64,192},{128,0},{192,64},{1,129},{65,193},{129,1},{193,65... | collective-permute-start | bytes 73736 | tf_op jit(solution)/shard_map/ppermute | solution.py:357
  16.9 0.0 collective-permute-done.1.recv1
  16.9 0.0 collective-permute-done.2.recv2
  16.9 1.6 %collective-permute-done.3.recv3 = bf16[96,128]{1,0:T(8,128)(2,1)S(1)} collective-permute-done((bf16[96,128]{1,0:T(8,128)(2,1)S(1)}, bf16[96,128]{1,0:T(8,128)(2,1)S(1)}, u32[]{:S(2)}, u32[]{:S(2)}) %collective-permute-start.3) | collective-permute-done | bytes 24608 | tf_op jit(solution)/shard_map/ppermute | solution.py:357
  18.4 0.0 collective-permute-done.4.recv4
  18.4 0.0 collective-permute-done.5.recv5
  18.4 7.1 %shard_map.113 = (bf16[4,96,512]{2,1,0:T(8,128)(2,1)}, bf16[4,96,512]{2,1,0:T(8,128)(2,1)S(1)}, f32[1024,128]{1,0:T(8,128)S(1)}, f32[1024,128]{1,0:T(8,128)S(1)}...) custom-call(bf16[4,96,512]{2,1,0:T(8,128)(2,1)} %feat_in.3, ...), custom_call_target="tpu_custom_call" | custom-call | tf_op jit(solution)/shard_map/pallas_call | solution.py:386
  25.5 0.0 copy-start
  25.5 0.0 copy-start.1
  25.5 2.2 %collective-permute-start.6 = (f32[1024,128]{1,0:T(8,128)S(1)}, f32[1024,128]{1,0:T(8,128)S(1)}, u32[]{:S(2)}, u32[]{:S(2)}) collective-permute-start(f32[1024,128]{1,0:T(8,128)S(1)} %get-tuple-element.42), channel_id=1, source_target_pairs={{0,16},{16,0},{1,17},{17,1},{2,18},{18,2},{3,19},{19,3},{4,20},{20... | collective-permute-start | bytes 1572872 | tf_op jit(solution)/shard_map/ppermute | solution.py:401
  27.7 1.5 %collective-permute-done.6 = f32[1024,128]{1,0:T(8,128)S(1)} collective-permute-done((f32[1024,128]{1,0:T(8,128)S(1)}, f32[1024,128]{1,0:T(8,128)S(1)}, u32[]{:S(2)}, u32[]{:S(2)}) %collective-permute-start.6) | collective-permute-done | bytes 524320 | tf_op jit(solution)/shard_map/ppermute | solution.py:401
  29.2 0.9 %add.3 = f32[1024,128]{1,0:T(8,128)} add(f32[1024,128]{1,0:T(8,128)S(1)} %get-tuple-element.41, f32[1024,128]{1,0:T(8,128)S(1)} %collective-permute-done.6) | non-fusion elementwise | flops 131072 | bytes 1572864 | tf_op jit(solution)/shard_map/add | solution.py:401
  30.1 0.0 copy-done
  30.1 0.0 copy-done.1
  30.1 8.4 %all-to-all-start = ((f32[16,64,128]{2,1,0:T(8,128)}), f32[16,64,128]{2,1,0:T(8,128)S(1)}, u32[]{:S(2)}, u32[]{:S(2)}) async-start(f32[16,64,128]{2,1,0:T(8,128)} %bitcast.1), calls=%async_computation | async-start | bytes 1048576 | tf_op jit(solution)/shard_map/all_to_all | solution.py:364
  38.5 1.4 %collective-permute-start.9 = (bf16[2,96,128]{2,1,0:T(8,128)(2,1)S(1)}, bf16[2,96,128]{2,1,0:T(8,128)(2,1)S(1)}, u32[]{:S(2)}, u32[]{:S(2)}) collective-permute-start(bf16[2,96,128]{2,1,0:T(8,128)(2,1)S(1)} %get-tuple-element.45), channel_id=1, source_target_pairs={{0,1},{1,0},{2,3},{3,2},{4,5},{5,4},{6,7},{7,6},{8,9},{9,8},{10,11... | collective-permute-start | bytes 147464 | tf_op jit(solution)/shard_map/ppermute | solution.py:358
  39.9 1.1 %collective-permute-start.7 = (bf16[96,128]{1,0:T(8,128)(2,1)S(1)}, bf16[96,128]{1,0:T(8,128)(2,1)S(1)}, u32[]{:S(2)}, u32[]{:S(2)}) collective-permute-start(bf16[96,128]{1,0:T(8,128)(2,1)S(1)} %get-tuple-element.43), channel_id=1, source_target_pairs={{0,32},{32,0},{1,33},{33,1},{2,34},{34,2},{3,35},{35,3},{4,36},{36... | collective-permute-start | bytes 73736 | tf_op jit(solution)/shard_map/ppermute | solution.py:355
  41.0 1.2 %collective-permute-start.8 = (bf16[96,128]{1,0:T(8,128)(2,1)S(1)}, bf16[96,128]{1,0:T(8,128)(2,1)S(1)}, u32[]{:S(2)}, u32[]{:S(2)}) collective-permute-start(bf16[96,128]{1,0:T(8,128)(2,1)S(1)} %get-tuple-element.44), channel_id=1, source_target_pairs={{0,64},{64,0},{128,192},{192,128},{1,65},{65,1},{129,193},{193,129... | collective-permute-start | bytes 73736 | tf_op jit(solution)/shard_map/ppermute | solution.py:356
  42.2 4.8 %collective-permute-done.7.recv1 = bf16[96,128]{1,0:T(8,128)(2,1)S(1)} collective-permute-done((bf16[96,128]{1,0:T(8,128)(2,1)S(1)}, bf16[96,128]{1,0:T(8,128)(2,1)S(1)}, u32[]{:S(2)}, u32[]{:S(2)}) %collective-permute-start.7) | collective-permute-done | bytes 24608 | tf_op jit(solution)/shard_map/ppermute | solution.py:355
  47.0 0.0 copy-start.4
  47.0 1.3 %collective-permute-done.8.recv2 = bf16[96,128]{1,0:T(8,128)(2,1)S(1)} collective-permute-done((bf16[96,128]{1,0:T(8,128)(2,1)S(1)}, bf16[96,128]{1,0:T(8,128)(2,1)S(1)}, u32[]{:S(2)}, u32[]{:S(2)}) %collective-permute-start.8) | collective-permute-done | bytes 24608 | tf_op jit(solution)/shard_map/ppermute | solution.py:356
  48.3 0.0 copy-start.5
  48.3 0.0 collective-permute-done.9.recv4
  48.3 0.0 copy-start.2
  48.3 0.9 %all-to-all-done.pieces_ref = f32[16,64,128]{2,1,0:T(8,128)S(1)} async-done(((f32[16,64,128]{2,1,0:T(8,128)}), f32[16,64,128]{2,1,0:T(8,128)S(1)}, u32[]{:S(2)}, u32[]{:S(2)}) %all-to-all-start) | async-done | bytes 524320 | tf_op jit(solution)/shard_map/all_to_all | solution.py:364
  49.2 0.7 shard_map.114
  49.9 3.4 %all-to-all-start.1 = ((f32[8,64,128]{2,1,0:T(8,128)}), f32[8,64,128]{2,1,0:T(8,128)S(1)}, u32[]{:S(2)}, u32[]{:S(2)}) async-start(f32[8,64,128]{2,1,0:T(8,128)} %shard_map.114), calls=%async_computation.1 | async-start | bytes 524288 | tf_op jit(solution)/shard_map/all_to_all | solution.py:364
  53.4 0.7 collective-permute-start.12
  54.0 2.6 %collective-permute-start.10 = (bf16[96,128]{1,0:T(8,128)(2,1)S(1)}, bf16[96,128]{1,0:T(8,128)(2,1)S(1)}, u32[]{:S(2)}, u32[]{:S(2)}) collective-permute-start(bf16[96,128]{1,0:T(8,128)(2,1)S(1)} %get-tuple-element.47), channel_id=1, source_target_pairs={{0,16},{16,0},{1,17},{17,1},{2,18},{18,2},{3,19},{19,3},{4,20},{20... | collective-permute-start | bytes 73736 | tf_op jit(solution)/shard_map/ppermute | solution.py:354
  56.6 0.6 collective-permute-start.11
  57.2 0.3 collective-permute-done.10.recv0
  57.5 0.0 copy-start.6
  57.5 3.3 %collective-permute-done.11.recv3 = bf16[96,128]{1,0:T(8,128)(2,1)S(1)} collective-permute-done((bf16[96,128]{1,0:T(8,128)(2,1)S(1)}, bf16[96,128]{1,0:T(8,128)(2,1)S(1)}, u32[]{:S(2)}, u32[]{:S(2)}) %collective-permute-start.11) | collective-permute-done | bytes 24608 | tf_op jit(solution)/shard_map/ppermute | solution.py:357
  60.8 0.0 copy-start.7
  60.8 0.0 collective-permute-done.12.recv5
  60.8 0.0 copy-start.3
  60.8 1.9 %all-to-all-done.1.pieces_ref = f32[8,64,128]{2,1,0:T(8,128)S(1)} async-done(((f32[8,64,128]{2,1,0:T(8,128)}), f32[8,64,128]{2,1,0:T(8,128)S(1)}, u32[]{:S(2)}, u32[]{:S(2)}) %all-to-all-start.1) | async-done | bytes 262176 | tf_op jit(solution)/shard_map/all_to_all | solution.py:364
  62.8 0.7 shard_map.115
  63.5 5.6 %all-to-all-start.2 = ((bf16[16,64,128]{2,1,0:T(8,128)(2,1)}), bf16[16,64,128]{2,1,0:T(8,128)(2,1)S(1)}, u32[]{:S(2)}, u32[]{:S(2)}) async-start(bf16[16,64,128]{2,1,0:T(8,128)(2,1)} %shard_map.115), calls=%async_computation.2 | async-start | bytes 524288 | tf_op jit(solution)/shard_map/all_to_all | solution.py:364
  69.1 0.0 copy-done.4
  69.1 0.0 copy-done.5
  69.1 0.0 copy-done.2
  69.1 0.0 copy-done.6
  69.1 0.0 copy-done.7
  69.1 0.0 copy-done.3
  69.1 5.3 %shard_map.116 = bf16[4,96,512]{2,1,0:T(8,128)(2,1)} custom-call(s32[4,512]{1,0:T(4,128)} %occ_in.5, bf16[4,96,512]{2,1,0:T(8,128)(2,1)} %grad_in.3, bf16[27,96,96]{2,1,0:T(8,128)(2,1)} %w_in.3, s32[4,4]{1,0:T(4,128)} %src_in.3, s32[4]{0:T(128)} %down_in.3, s32[4]{0:T(128)} %up_in.3, bf16[4,96,512]{2,1,0:T(8,128)(2,1)} %copy-done, ...), custom_call_target="tpu_custom_call" | custom-call | flops 5000000000 | bytes 4000000 | tf_op jit(solution)/shard_map/pallas_call | solution.py:407
  74.4 2.2 %all-to-all-done.2 = bf16[16,64,128]{2,1,0:T(8,128)(2,1)S(1)} async-done(((bf16[16,64,128]{2,1,0:T(8,128)(2,1)}), bf16[16,64,128]{2,1,0:T(8,128)(2,1)S(1)}, u32[]{:S(2)}, u32[]{:S(2)}) %all-to-all-start.2) | async-done | bytes 262176 | tf_op jit(solution)/shard_map/all_to_all | solution.py:364
  76.6 3.2 %collective-permute-start.13 = (bf16[1024,128]{1,0:T(8,128)(2,1)S(1)}, bf16[1024,128]{1,0:T(8,128)(2,1)S(1)}, u32[]{:S(2)}, u32[]{:S(2)}) collective-permute-start(bf16[1024,128]{1,0:T(8,128)(2,1)S(1)} %bitcast.4), channel_id=1, source_target_pairs={{0,16},{16,0},{1,17},{17,1},{2,18},{18,2},{3,19},{19,3},{4,20},{20... | collective-permute-start | bytes 786440 | tf_op jit(solution)/shard_map/ppermute | solution.py:418
  79.8 1.2 %collective-permute-done.13.other_ref = bf16[1024,128]{1,0:T(8,128)(2,1)S(1)} collective-permute-done((bf16[1024,128]{1,0:T(8,128)(2,1)S(1)}, bf16[1024,128]{1,0:T(8,128)(2,1)S(1)}, u32[]{:S(2)}, u32[]{:S(2)}) %collective-permute-start.13) | collective-permute-done | bytes 262176 | tf_op jit(solution)/shard_map/ppermute | solution.py:418
  81.0 1.4 %shard_map.117 = f32[2592,96]{1,0:T(8,128)} custom-call(bf16[1024,128]{1,0:T(8,128)(2,1)S(1)} %bitcast.5, bf16[1024,128]{1,0:T(8,128)(2,1)S(1)} %collective-permute-done.13.other_ref), custom_call_target="tpu_custom_call" | custom-call | tf_op jit(solution)/shard_map/pallas_call | solution.py:419
Async XLA Ops:
  2.5 11.8 %collective-permute-start = (bf16[96,128]{1,0:T(8,128)(2,1)S(1)}, bf16[96,128]{1,0:T(8,128)(2,1)S(1)}, u32[]{:S(2)}, u32[]{:S(2)}) collective-permute-start(bf16[96,128]{1,0:T(8,128)(2,1)S(1)} %get-tuple-element.34), channel_id=1, source_target_pairs={{0,16},{16,0},{1,17},{17,1},{2,18},{18,2},{3,19},{19,3},{4,20},{20... | collective-permute-start | bytes 73736 | tf_op jit(solution)/shard_map/ppermute | solution.py:354
  5.8 12.6 %collective-permute-start.4 = (bf16[2,96,128]{2,1,0:T(8,128)(2,1)S(1)}, bf16[2,96,128]{2,1,0:T(8,128)(2,1)S(1)}, u32[]{:S(2)}, u32[]{:S(2)}) collective-permute-start(bf16[2,96,128]{2,1,0:T(8,128)(2,1)S(1)} %get-tuple-element.38), channel_id=1, source_target_pairs={{0,1},{1,0},{2,3},{3,2},{4,5},{5,4},{6,7},{7,6},{8,9},{9,8},{10,11... | collective-permute-start | bytes 147464 | tf_op jit(solution)/shard_map/ppermute | solution.py:358
  5.8 12.6 %collective-permute-start.5 = (bf16[2,96,128]{2,1,0:T(8,128)(2,1)S(1)}, bf16[2,96,128]{2,1,0:T(8,128)(2,1)S(1)}, u32[]{:S(2)}, u32[]{:S(2)}) collective-permute-start(bf16[2,96,128]{2,1,0:T(8,128)(2,1)S(1)} %get-tuple-element.39), channel_id=1, source_target_pairs={{1,2},{2,1},{3,4},{4,3},{5,6},{6,5},{7,8},{8,7},{9,10},{10,9},{11,... | collective-permute-start | bytes 147464 | tf_op jit(solution)/shard_map/ppermute | solution.py:359
  6.5 10.4 %collective-permute-start.1 = (bf16[96,128]{1,0:T(8,128)(2,1)S(1)}, bf16[96,128]{1,0:T(8,128)(2,1)S(1)}, u32[]{:S(2)}, u32[]{:S(2)}) collective-permute-start(bf16[96,128]{1,0:T(8,128)(2,1)S(1)} %get-tuple-element.35), channel_id=1, source_target_pairs={{0,32},{32,0},{1,33},{33,1},{2,34},{34,2},{3,35},{35,3},{4,36},{36... | collective-permute-start | bytes 73736 | tf_op jit(solution)/shard_map/ppermute | solution.py:355
  13.0 3.9 %collective-permute-start.2 = (bf16[96,128]{1,0:T(8,128)(2,1)S(1)}, bf16[96,128]{1,0:T(8,128)(2,1)S(1)}, u32[]{:S(2)}, u32[]{:S(2)}) collective-permute-start(bf16[96,128]{1,0:T(8,128)(2,1)S(1)} %get-tuple-element.36), channel_id=1, source_target_pairs={{0,64},{64,0},{128,192},{192,128},{1,65},{65,1},{129,193},{193,129... | collective-permute-start | bytes 73736 | tf_op jit(solution)/shard_map/ppermute | solution.py:356
  14.3 4.2 %collective-permute-start.3 = (bf16[96,128]{1,0:T(8,128)(2,1)S(1)}, bf16[96,128]{1,0:T(8,128)(2,1)S(1)}, u32[]{:S(2)}, u32[]{:S(2)}) collective-permute-start(bf16[96,128]{1,0:T(8,128)(2,1)S(1)} %get-tuple-element.37), channel_id=1, source_target_pairs={{0,128},{64,192},{128,0},{192,64},{1,129},{65,193},{129,1},{193,65... | collective-permute-start | bytes 73736 | tf_op jit(solution)/shard_map/ppermute | solution.py:357
  25.5 4.6 %copy-start = (bf16[4,96,512]{2,1,0:T(8,128)(2,1)}, bf16[4,96,512]{2,1,0:T(8,128)(2,1)S(1)}, u32[]{:S(2)}) copy-start(bf16[4,96,512]{2,1,0:T(8,128)(2,1)S(1)} %get-tuple-element.51.delta_in) | copy-start | bytes 1179652
  25.5 4.6 %copy-start.1 = (bf16[16,96,128]{2,1,0:T(8,128)(2,1)}, bf16[16,96,128]{2,1,0:T(8,128)(2,1)S(1)}, u32[]{:S(2)}) copy-start(bf16[16,96,128]{2,1,0:T(8,128)(2,1)S(1)} %get-tuple-element.52.own_in) | copy-start | bytes 1179652
  25.5 3.7 %collective-permute-start.6 = (f32[1024,128]{1,0:T(8,128)S(1)}, f32[1024,128]{1,0:T(8,128)S(1)}, u32[]{:S(2)}, u32[]{:S(2)}) collective-permute-start(f32[1024,128]{1,0:T(8,128)S(1)} %get-tuple-element.42), channel_id=1, source_target_pairs={{0,16},{16,0},{1,17},{17,1},{2,18},{18,2},{3,19},{19,3},{4,20},{20... | collective-permute-start | bytes 1572872 | tf_op jit(solution)/shard_map/ppermute | solution.py:401
  30.1 19.1 %all-to-all-start = ((f32[16,64,128]{2,1,0:T(8,128)}), f32[16,64,128]{2,1,0:T(8,128)S(1)}, u32[]{:S(2)}, u32[]{:S(2)}) async-start(f32[16,64,128]{2,1,0:T(8,128)} %bitcast.1), calls=%async_computation | async-start | bytes 1048576 | tf_op jit(solution)/shard_map/all_to_all | solution.py:364
  38.5 9.8 %collective-permute-start.9 = (bf16[2,96,128]{2,1,0:T(8,128)(2,1)S(1)}, bf16[2,96,128]{2,1,0:T(8,128)(2,1)S(1)}, u32[]{:S(2)}, u32[]{:S(2)}) collective-permute-start(bf16[2,96,128]{2,1,0:T(8,128)(2,1)S(1)} %get-tuple-element.45), channel_id=1, source_target_pairs={{0,1},{1,0},{2,3},{3,2},{4,5},{5,4},{6,7},{7,6},{8,9},{9,8},{10,11... | collective-permute-start | bytes 147464 | tf_op jit(solution)/shard_map/ppermute | solution.py:358
  39.9 7.1 %collective-permute-start.7 = (bf16[96,128]{1,0:T(8,128)(2,1)S(1)}, bf16[96,128]{1,0:T(8,128)(2,1)S(1)}, u32[]{:S(2)}, u32[]{:S(2)}) collective-permute-start(bf16[96,128]{1,0:T(8,128)(2,1)S(1)} %get-tuple-element.43), channel_id=1, source_target_pairs={{0,32},{32,0},{1,33},{33,1},{2,34},{34,2},{3,35},{35,3},{4,36},{36... | collective-permute-start | bytes 73736 | tf_op jit(solution)/shard_map/ppermute | solution.py:355
  41.0 7.3 %collective-permute-start.8 = (bf16[96,128]{1,0:T(8,128)(2,1)S(1)}, bf16[96,128]{1,0:T(8,128)(2,1)S(1)}, u32[]{:S(2)}, u32[]{:S(2)}) collective-permute-start(bf16[96,128]{1,0:T(8,128)(2,1)S(1)} %get-tuple-element.44), channel_id=1, source_target_pairs={{0,64},{64,0},{128,192},{192,128},{1,65},{65,1},{129,193},{193,129... | collective-permute-start | bytes 73736 | tf_op jit(solution)/shard_map/ppermute | solution.py:356
  47.0 22.1 %copy-start.4 = (bf16[96,128]{1,0:T(8,128)(2,1)}, bf16[96,128]{1,0:T(8,128)(2,1)S(1)}, u32[]{:S(2)}) copy-start(bf16[96,128]{1,0:T(8,128)(2,1)S(1)} %collective-permute-done.7.recv1) | copy-start | bytes 73732
  48.3 20.8 %copy-start.5 = (bf16[96,128]{1,0:T(8,128)(2,1)}, bf16[96,128]{1,0:T(8,128)(2,1)S(1)}, u32[]{:S(2)}) copy-start(bf16[96,128]{1,0:T(8,128)(2,1)S(1)} %collective-permute-done.8.recv2) | copy-start | bytes 73732
  48.3 20.8 %copy-start.2 = (bf16[2,96,128]{2,1,0:T(8,128)(2,1)}, bf16[2,96,128]{2,1,0:T(8,128)(2,1)S(1)}, u32[]{:S(2)}) copy-start(bf16[2,96,128]{2,1,0:T(8,128)(2,1)S(1)} %collective-permute-done.9.recv4) | copy-start | bytes 147460
  49.9 12.8 %all-to-all-start.1 = ((f32[8,64,128]{2,1,0:T(8,128)}), f32[8,64,128]{2,1,0:T(8,128)S(1)}, u32[]{:S(2)}, u32[]{:S(2)}) async-start(f32[8,64,128]{2,1,0:T(8,128)} %shard_map.114), calls=%async_computation.1 | async-start | bytes 524288 | tf_op jit(solution)/shard_map/all_to_all | solution.py:364
  53.4 7.4 %collective-permute-start.12 = (bf16[2,96,128]{2,1,0:T(8,128)(2,1)S(1)}, bf16[2,96,128]{2,1,0:T(8,128)(2,1)S(1)}, u32[]{:S(2)}, u32[]{:S(2)}) collective-permute-start(bf16[2,96,128]{2,1,0:T(8,128)(2,1)S(1)} %get-tuple-element.49), channel_id=1, source_target_pairs={{1,2},{2,1},{3,4},{4,3},{5,6},{6,5},{7,8},{8,7},{9,10},{10,9},{11,... | collective-permute-start | bytes 147464 | tf_op jit(solution)/shard_map/ppermute | solution.py:359
  54.0 3.4 %collective-permute-start.10 = (bf16[96,128]{1,0:T(8,128)(2,1)S(1)}, bf16[96,128]{1,0:T(8,128)(2,1)S(1)}, u32[]{:S(2)}, u32[]{:S(2)}) collective-permute-start(bf16[96,128]{1,0:T(8,128)(2,1)S(1)} %get-tuple-element.47), channel_id=1, source_target_pairs={{0,16},{16,0},{1,17},{17,1},{2,18},{18,2},{3,19},{19,3},{4,20},{20... | collective-permute-start | bytes 73736 | tf_op jit(solution)/shard_map/ppermute | solution.py:354
  56.6 4.2 %collective-permute-start.11 = (bf16[96,128]{1,0:T(8,128)(2,1)S(1)}, bf16[96,128]{1,0:T(8,128)(2,1)S(1)}, u32[]{:S(2)}, u32[]{:S(2)}) collective-permute-start(bf16[96,128]{1,0:T(8,128)(2,1)S(1)} %get-tuple-element.48), channel_id=1, source_target_pairs={{0,128},{64,192},{128,0},{192,64},{1,129},{65,193},{129,1},{193,65... | collective-permute-start | bytes 73736 | tf_op jit(solution)/shard_map/ppermute | solution.py:357
  57.5 11.7 %copy-start.6 = (bf16[96,128]{1,0:T(8,128)(2,1)}, bf16[96,128]{1,0:T(8,128)(2,1)S(1)}, u32[]{:S(2)}) copy-start(bf16[96,128]{1,0:T(8,128)(2,1)S(1)} %collective-permute-done.10.recv0) | copy-start | bytes 73732
  60.8 8.3 %copy-start.7 = (bf16[96,128]{1,0:T(8,128)(2,1)}, bf16[96,128]{1,0:T(8,128)(2,1)S(1)}, u32[]{:S(2)}) copy-start(bf16[96,128]{1,0:T(8,128)(2,1)S(1)} %collective-permute-done.11.recv3) | copy-start | bytes 73732
  60.8 8.3 %copy-start.3 = (bf16[2,96,128]{2,1,0:T(8,128)(2,1)}, bf16[2,96,128]{2,1,0:T(8,128)(2,1)S(1)}, u32[]{:S(2)}) copy-start(bf16[2,96,128]{2,1,0:T(8,128)(2,1)S(1)} %collective-permute-done.12.recv5) | copy-start | bytes 147460
  63.5 13.1 %all-to-all-start.2 = ((bf16[16,64,128]{2,1,0:T(8,128)(2,1)}), bf16[16,64,128]{2,1,0:T(8,128)(2,1)S(1)}, u32[]{:S(2)}, u32[]{:S(2)}) async-start(bf16[16,64,128]{2,1,0:T(8,128)(2,1)} %shard_map.115), calls=%async_computation.2 | async-start | bytes 524288 | tf_op jit(solution)/shard_map/all_to_all | solution.py:364
  76.6 4.4 %collective-permute-start.13 = (bf16[1024,128]{1,0:T(8,128)(2,1)S(1)}, bf16[1024,128]{1,0:T(8,128)(2,1)S(1)}, u32[]{:S(2)}, u32[]{:S(2)}) collective-permute-start(bf16[1024,128]{1,0:T(8,128)(2,1)S(1)} %bitcast.4), channel_id=1, source_target_pairs={{0,16},{16,0},{1,17},{17,1},{2,18},{18,2},{3,19},{19,3},{4,20},{20... | collective-permute-start | bytes 786440 | tf_op jit(solution)/shard_map/ppermute | solution.py:418

commit v4 on v3

--- a/solution.py
+++ b/solution.py
@@ -19,25 +19,22 @@
 COLUMN = ("zh", "zl")
 ROWS, HALF, REST = 2048, 1024, 216
 MAIN = NB * V
+LAT_ROWS = (C, 224, C, 160)
 SCALE = 1.0 / math.sqrt(1024 * 512)
 SHIFTS = [(dy, dz) for dy in range(3) for dz in range(3)]
 VMEM_LIMIT = 26 * 1024 * 1024
 
 
-def face_matrix():
-    table = np.zeros((V, 6 * 128), np.float32)
-    for f in range(6):
-        for a in range(8):
-            for b in range(8):
-                if f < 2:
-                    v = 448 * f + 8 * a + b
-                elif f < 4:
-                    v = 64 * a + 56 * (f - 2) + b
-                else:
-                    v = 64 * a + 8 * b + 7 * (f - 4)
-                table[v, 128 * f + 8 * a + b] = 1
-                table[v, 128 * f + 64 + 8 * a + b] = 1
-    return table
+def fill_faces(pf_ref):
+    lane = lax.broadcasted_iota(jnp.int32, (1, 6 * 128), 1)
+    row = lax.broadcasted_iota(jnp.int32, (V, 6 * 128), 0)
+    f, p = lane >> 7, lane & 63
+    first, second = p >> 3, p & 7
+    on_x = 448 * f + p
+    on_y = 64 * first + 56 * (f - 2) + second
+    on_z = 64 * first + 8 * second + 7 * (f - 4)
+    voxel = jnp.where(f < 2, on_x, jnp.where(f < 4, on_y, on_z))
+    pf_ref[...] = jnp.where(row == voxel, 1.0, 0.0).astype(BF16)
 
 
 def lane_low(rows):
@@ -61,7 +58,9 @@
     zf_refs[0][...] = faces_z[1 - odd]
     zf_refs[1][...] = faces_z[odd]
     for k in range(4):
-        lat_refs[k][...] = jnp.where(low, own_ref[send_ref[0, 0, k]], own_ref[send_ref[0, 1, k]])
+        lat_refs[k][0:C, :] = jnp.where(low, own_ref[send_ref[0, 0, k]], own_ref[send_ref[0, 1, k]])
+    for k in (1, 3):
+        lat_refs[k][C:, :] = jnp.zeros((LAT_ROWS[k] - C, 128), BF16)
 
 
 def fill_pool(recv_refs, pool):
@@ -74,7 +73,7 @@
         pool[at + 1] = jnp.where(low, turned, pair)
 
     for k in range(4):
-        spread(recv_refs[k][...], 16 + 2 * k)
+        spread(recv_refs[k][0:C, :], 16 + 2 * k)
     for h in range(2):
         spread(recv_refs[4][h], 30 - 5 * odd + 2 * h)
         spread(recv_refs[5][h], 25 + 5 * odd + 2 * h)
@@ -193,25 +192,44 @@
         copy.wait()
 
 
-def faces_kernel(feat_in, occ_in, pf_in, send_in, masked_ref, own_ref, *refs):
+def faces_kernel(feat_in, occ_in, send_in, masked_ref, own_ref, *refs):
     feat, occ, pf, send, faces_z, sems = refs[6:]
-    copies = started(sems, (send_in, send), (occ_in, occ), (feat_in, feat), (pf_in, pf))
-    waited(*copies[1:3])
+    copies = started(sems, (send_in, send), (occ_in, occ), (feat_in, feat))
+    fill_faces(pf)
+    waited(*copies)
     masked_ref[...] = masked_of(feat, occ)
-    waited(copies[0], copies[3])
     write_faces(masked_ref[...], pf[...], send, own_ref, refs[:4], refs[4:6], faces_z)
 
 
+def delta_faces_kernel(delta_ref, send_in, *refs):
+    own, pf, send, faces_z, sems = refs[6:]
+    copies = started(sems, (send_in, send))
+    fill_faces(pf)
+    waited(*copies)
+    write_faces(delta_ref[...], pf[...], send, own, refs[:4], refs[4:6], faces_z)
+
+
+def delta_own_kernel(delta_in, own_out, delta, own, pf, sems):
+    copies = started(sems, (delta_in, delta))
+    fill_faces(pf)
+    waited(*copies)
+    faces = jnp.dot(delta[...].reshape(NB * C, V), pf[:, :512], preferred_element_type=F32).astype(BF16)
+    for f in range(4):
+        for b in range(NB):
+            own[NB * f + b] = faces[C * b : C * (b + 1), 128 * f : 128 * (f + 1)]
+    waited(*started(sems.at[1:], (own, own_out)))
+
+
 def forward_kernel(
-    feat_in, occ_in, grad_in, w_in, pf_in, src_in, down_in, up_in, send_in,
+    feat_in, occ_in, grad_in, w_in, src_in, down_in, up_in,
     masked_ref, own_ref, recv0, recv1, recv2, recv3, recv4, recv5,
-    out_out, delta_ref, keep_ref, give_ref, delta_own_ref, lat0, lat1, lat2, lat3, zf0, zf1,
+    out_out, delta_ref, keep_ref, give_ref,
     occ, grad, w, src, down, up, out, pool, slabs, halo, taps, w3, e, ends, sems, out_sems,
-    feat, pf, send, faces_z, terms_ref, around,
+    feat, terms_ref, around,
 ):
     early = started(sems, (src_in, src), (down_in, down), (up_in, up))
     later = started(
-        sems.at[3:], (w_in, w), (occ_in, occ), (feat_in, feat), (grad_in, grad), (pf_in, pf), (send_in, send)
+        sems.at[3:], (w_in, w), (occ_in, occ), (feat_in, feat), (grad_in, grad)
     )
     for i in range(16):
         pool[i] = own_ref[i]
@@ -233,9 +251,6 @@
         delta_ref[b] = delta.astype(BF16)
 
     convolve(w3, taps, ends, finish)
-    write_faces(
-        delta_ref[...], pf[...], send, delta_own_ref, (lat0, lat1, lat2, lat3), (zf0, zf1), faces_z
-    )
     kernel_terms(taps, delta_ref, around, terms_ref)
     core = lax.axis_index("c")
     keep_ref[...] = terms_ref[pl.ds(pl.multiple_of(core * HALF, HALF), HALF), :]
@@ -252,7 +267,7 @@
 ):
     early = started(
         sems,
-        *[(recv, lateral.at[k]) for k, recv in enumerate((recv0, recv1, recv2, recv3))],
+        *[(recv.at[0:C], lateral.at[k]) for k, recv in enumerate((recv0, recv1, recv2, recv3))],
         (recv4, vertical.at[0]), (recv5, vertical.at[1]), (own_in, pool.at[0:16]),
         (src_in, src), (down_in, down), (up_in, up), (delta_in, delta),
     )
@@ -314,15 +329,16 @@
     return pl.pallas_call(
         kernel,
         in_specs=ins,
-        out_specs=[spec for spec, _, _ in outs],
-        out_shape=[jax.ShapeDtypeStruct(shape, kind) for _, shape, kind in outs],
+        out_specs=[out[0] for out in outs],
+        out_shape=[(out[3] if len(out) > 3 else jax.ShapeDtypeStruct)(out[1], out[2]) for out in outs],
         scratch_shapes=list(scratch),
         compiler_params=pltpu.CompilerParams(vmem_limit_bytes=limit),
         cost_estimate=pl.CostEstimate(flops=flops, bytes_accessed=moved, transcendentals=0),
     )
 
 
-FACE_OUTS = [(VM, (16, C, 128), BF16)] + [(VM, (C, 128), BF16)] * 4 + [(VM, (2, C, 128), BF16)] * 2
+FACE_OUTS = [(VM, (16, C, 128), BF16)] + [(VM, (n, 128), BF16) for n in LAT_ROWS]
+FACE_OUTS += [(VM, (2, C, 128), BF16)] * 2
 BLOCKS = (NB, C, V)
 FEAT, OCC = pltpu.VMEM(BLOCKS, BF16), pltpu.VMEM((NB, V), jnp.int32)
 PF, SEND = pltpu.VMEM((V, 768), BF16), pltpu.SMEM((1, 2, 4), jnp.int32)
@@ -376,33 +392,45 @@
 
 
 def on_device(features, occupancy, weights, grad_out, lat_src, down_src, up_src, send_faces):
-    pf = jnp.asarray(face_matrix(), BF16)
     sends = send_faces.transpose(0, 2, 1)
     masked, own, *out = call(
-        faces_kernel, [HB] * 4, [(VM, BLOCKS, BF16)] + FACE_OUTS,
-        [FEAT, OCC, PF, SEND, FACES_Z, pltpu.SemaphoreType.DMA((4,))],
-    )(*in_hbm(features, occupancy, pf, sends))
+        faces_kernel, [HB] * 3, [(VM, BLOCKS, BF16)] + FACE_OUTS,
+        [FEAT, OCC, PF, SEND, FACES_Z, pltpu.SemaphoreType.DMA((3,))],
+    )(*in_hbm(features, occupancy, sends))
     half = (VM, (HALF, 128), F32)
-    layer_out, delta, keep, give, delta_own, *out = call(
+    layer_out, delta, keep, give = call(
         forward_kernel,
-        [HB] * 9 + [VM] * 8,
-        [(HB, BLOCKS, BF16), (VM, BLOCKS, BF16), half, half] + FACE_OUTS,
+        [HB] * 7 + [VM] * 8,
+        [(HB, BLOCKS, BF16), (VM, BLOCKS, BF16), half, half],
         SCRATCH
-        + [FEAT, PF, SEND, FACES_Z, pltpu.VMEM((ROWS, 128), F32)]
-        + [pltpu.VMEM((2 * C, MAIN + NB * 128), BF16)],
+        + [FEAT, pltpu.VMEM((ROWS, 128), F32), pltpu.VMEM((2 * C, MAIN + NB * 128), BF16)],
         limit=VMEM_LIMIT,
     )(
-        *in_hbm(features, occupancy, grad_out, weights, pf, lat_src, down_src, up_src, sends),
+        *in_hbm(features, occupancy, grad_out, weights, lat_src, down_src, up_src),
         masked,
         own,
         *exchange(*out),
     )
+    out = call(
+        delta_faces_kernel, [VM, HB], FACE_OUTS[1:],
+        [pltpu.VMEM((16, C, 128), BF16), PF, SEND, FACES_Z, pltpu.SemaphoreType.DMA((1,))],
+        flops=2 * 384 * 512 * 768, moved=2 * 10**6,
+    )(delta, *in_hbm(sends))
+    (delta_own,) = call(
+        delta_own_kernel, [HB], [(HB, (16, C, 128), BF16, pltpu.HBM)],
+        [FEAT, pltpu.VMEM((16, C, 128), BF16), PF, pltpu.SemaphoreType.DMA((2,))],
+        flops=2 * 384 * 512 * 512, moved=2 * 10**6,
+    )(*in_hbm(delta))
+    other = lax.ppermute(give, "c", [(0, 1), (1, 0)])
+    other, *out = lax.optimization_barrier((other, *out))
     halos = exchange(*out)
-    part = keep + lax.ppermute(give, "c", [(0, 1), (1, 0)])
+    part = keep + other
     part = exchanged(part.reshape(16, HALF // 16, 128), PLANE)
     part, halos[1], halos[2], halos[4] = lax.optimization_barrier((part, halos[1], halos[2], halos[4]))
     part = exchanged(summed(part, 8, F32), COLUMN)
-    part, halos[0], halos[3], halos[5] = lax.optimization_barrier((part, halos[0], halos[3], halos[5]))
+    part, delta_own, halos[0], halos[3], halos[5] = lax.optimization_barrier(
+        (part, delta_own, halos[0], halos[3], halos[5])
+    )
     part = exchanged(summed(part, 16, BF16), PLANE)
     (input_grad,) = call(
         backward_kernel,

time: 83 us -> 81 us (0.976)
  starting transfers between devices: 44.6 us -> 41.7 us
  Pallas kernels: 17.1 us -> 19.3 us
  waiting for transfers between devices: 19 us -> 17.6 us
    ppermute x2, waiting for transfers between devices: 4.9 us -> 0.01 us  [exchange(): lax.ppermute(lat3, 'y', [(i, i ^ 2) for i in range(4)])]
    ppermute x2, waiting for transfers between devices: 4.82 us -> 0.01 us  [exchange(): lax.ppermute(lat1, 'zh', flip2)]
    ppermute x2, waiting for transfers between devices: 0.01 us -> 3.75 us  [exchange(): lax.ppermute(zf0, BAND, [p for i, j in pairs[0:15:2] for p in ((i, j), (j...]
    ppermute x2, waiting for transfers between devices: 1.27 us -> 4.44 us  [exchange(): lax.ppermute(lat2, 'y', [(i, i ^ 1) for i in range(4)])]
    all_to_all x3, waiting for transfers between devices: 5.07 us -> 7.9 us  [exchanged(): return lax.all_to_all(pieces, axes, 0, 0, tiled=True)]
    ppermute x2, starting transfers between devices: 5.9 us -> 3.24 us  [exchange(): lax.ppermute(lat0, 'c', flip2)]
    pallas_call x2 -> x4, Pallas kernels: 8.91 us -> 11.2 us  [the longest x1 6.28 us: on_device(): call(forward_kernel, [HB] * 7 + [VM] * 8, [(HB, BLOCKS, BF16), (VM, BLOCK...]
    ppermute x1, waiting for transfers between devices: 1.54 us -> 0.31 us  [on_device(): other = lax.ppermute(give, 'c', [(0, 1), (1, 0)])]
  transfers between devices with their start and end apart: 17 -> 17, of which waited for: 10 -> 8; matrix products, arithmetic and copies ran while one was open for 0% -> 0% of each run, Pallas kernels for 6% -> 11%
where the time goes in v4:
time: 81 us; the launch traced here: 80.5 us
  starting transfers between devices  41.7 us (51%)
  Pallas kernels  19.3 us (24%)
  waiting for transfers between devices  17.6 us (22%)
  between operations  0.98 us (1%)
  other arithmetic  0.87 us (1%)
    all_to_all x3, starting transfers between devices, exchanged(): return lax.all_to_all(pieces, axes, 0, 0, tiled=True)  16.6 us
    ppermute x2, starting transfers between devices, exchange(): lax.ppermute(lat1, 'zh', flip2)  7.92 us
    all_to_all x3, waiting for transfers between devices, exchanged(): return lax.all_to_all(pieces, axes, 0, 0, tiled=True)  7.9 us
    pallas_call x1, Pallas kernels, on_device(): call(forward_kernel, [HB] * 7 + [VM] * 8, [(HB, BLOCKS, BF16), (VM, BLOCK...  6.28 us
    pallas_call x1, Pallas kernels, on_device(): call(backward_kernel, [HB] * 14, [(HB, BLOCKS, BF16)], SCRATCH + [FEAT, p...  5.27 us
    ppermute x2, waiting for transfers between devices, exchange(): lax.ppermute(lat2, 'y', [(i, i ^ 1) for i in range(4)])  4.44 us
    ppermute x2, starting transfers between devices, exchange(): lax.ppermute(lat3, 'y', [(i, i ^ 2) for i in range(4)])  3.96 us
    ppermute x2, waiting for transfers between devices, exchange(): lax.ppermute(zf0, BAND, [p for i, j in pairs[0:15:2] for p in ((i, j), (j...  3.75 us
  transfers between devices with their start and end apart: 17, of which 8 were waited for; matrix products, arithmetic and copies ran while one was open for 0% of the time, Pallas kernels for 11%

profile of v4, /device:TPU:1, one launch (start us, length us, event | category | flops | bytes accessed | tf_op | source)
XLA Modules:
  0.0 80.5 jit_solution(5438552691372657486)
XLA Ops:
  0.6 1.6 %shard_map.103 = (bf16[4,96,512]{2,1,0:T(8,128)(2,1)S(1)}, bf16[16,96,128]{2,1,0:T(8,128)(2,1)S(1)}, bf16[96,128]{1,0:T(8,128)(2,1)S(1)}, bf16[224,128]{1,0:T(8,...) custom-call(bf16[4,96,512]{2,1,0:T(8,128)(2,1)} %feat_in.3, ...), custom_call_target="tpu_custom_call" | custom-call | tf_op jit(solution)/shard_map/pallas_call | solution.py:396
  2.2 7.8 %collective-permute-start.1 = (bf16[224,128]{1,0:T(8,128)(2,1)S(1)}, bf16[224,128]{1,0:T(8,128)(2,1)S(1)}, u32[]{:S(2)}, u32[]{:S(2)}) collective-permute-start(bf16[224,128]{1,0:T(8,128)(2,1)S(1)} %get-tuple-element.42), channel_id=1, source_target_pairs={{0,32},{32,0},{1,33},{33,1},{2,34},{34,2},{3,35},{35,3},{4,36},{36... | collective-permute-start | bytes 172040 | tf_op jit(solution)/shard_map/ppermute | solution.py:371
  10.0 1.0 %collective-permute-start = (bf16[96,128]{1,0:T(8,128)(2,1)S(1)}, bf16[96,128]{1,0:T(8,128)(2,1)S(1)}, u32[]{:S(2)}, u32[]{:S(2)}) collective-permute-start(bf16[96,128]{1,0:T(8,128)(2,1)S(1)} %get-tuple-element.41), channel_id=1, source_target_pairs={{0,16},{16,0},{1,17},{17,1},{2,18},{18,2},{3,19},{19,3},{4,20},{20... | collective-permute-start | bytes 73736 | tf_op jit(solution)/shard_map/ppermute | solution.py:370
  11.0 1.2 %collective-permute-start.4 = (bf16[2,96,128]{2,1,0:T(8,128)(2,1)S(1)}, bf16[2,96,128]{2,1,0:T(8,128)(2,1)S(1)}, u32[]{:S(2)}, u32[]{:S(2)}) collective-permute-start(bf16[2,96,128]{2,1,0:T(8,128)(2,1)S(1)} %get-tuple-element.45), channel_id=1, source_target_pairs={{0,1},{1,0},{2,3},{3,2},{4,5},{5,4},{6,7},{7,6},{8,9},{9,8},{10,11... | collective-permute-start | bytes 147464 | tf_op jit(solution)/shard_map/ppermute | solution.py:374
  12.2 0.7 collective-permute-start.5
  12.9 3.0 %collective-permute-start.3 = (bf16[160,128]{1,0:T(8,128)(2,1)S(1)}, bf16[160,128]{1,0:T(8,128)(2,1)S(1)}, u32[]{:S(2)}, u32[]{:S(2)}) collective-permute-start(bf16[160,128]{1,0:T(8,128)(2,1)S(1)} %get-tuple-element.44), channel_id=1, source_target_pairs={{0,128},{64,192},{128,0},{192,64},{1,129},{65,193},{129,1},{193,65... | collective-permute-start | bytes 122888 | tf_op jit(solution)/shard_map/ppermute | solution.py:373
  15.9 0.0 collective-permute-done.recv0
  15.9 0.4 collective-permute-start.2
  16.3 2.4 %collective-permute-done.2.recv2 = bf16[96,128]{1,0:T(8,128)(2,1)S(1)} collective-permute-done((bf16[96,128]{1,0:T(8,128)(2,1)S(1)}, bf16[96,128]{1,0:T(8,128)(2,1)S(1)}, u32[]{:S(2)}, u32[]{:S(2)}) %collective-permute-start.2) | collective-permute-done | bytes 24608 | tf_op jit(solution)/shard_map/ppermute | solution.py:372
  18.7 0.0 collective-permute-done.3.recv3
  18.7 0.0 collective-permute-done.4.recv4
  18.7 0.0 collective-permute-done.5.recv5
  18.7 0.0 collective-permute-done.1.recv1
  18.7 6.3 %shard_map.104 = (bf16[4,96,512]{2,1,0:T(8,128)(2,1)}, bf16[4,96,512]{2,1,0:T(8,128)(2,1)S(1)}, f32[1024,128]{1,0:T(8,128)S(1)}, f32[1024,128]{1,0:T(8,128)S(1)}) custom-call(bf16[4,96,512]{2,1,0:T(8,128)(2,1)} %feat_in.3, s32[4,512]{1,0:T(4,128)} %occ_in.5, bf16[4,96,512]{2,1,0:T(8,128)(2,1)} %grad_in.3, bf16[27,96,96]{2,1,0:T(8,128)(2,1)} %w_in.3, ...), custom_call_target="tpu_custom_call" | custom-call | tf_op jit(solution)/shard_map/pallas_call | solution.py:401
  25.0 0.0 copy-start
  25.0 1.7 %collective-permute-start.6 = (f32[1024,128]{1,0:T(8,128)S(1)}, f32[1024,128]{1,0:T(8,128)S(1)}, u32[]{:S(2)}, u32[]{:S(2)}) collective-permute-start(f32[1024,128]{1,0:T(8,128)S(1)} %get-tuple-element.49), channel_id=1, source_target_pairs={{0,16},{16,0},{1,17},{17,1},{2,18},{18,2},{3,19},{19,3},{4,20},{20... | collective-permute-start | bytes 1572872 | tf_op jit(solution)/shard_map/ppermute | solution.py:424
  26.7 1.2 %shard_map.105 = (bf16[96,128]{1,0:T(8,128)(2,1)S(1)}, bf16[224,128]{1,0:T(8,128)(2,1)S(1)}, bf16[96,128]{1,0:T(8,128)(2,1)S(1)}, bf16[160,128]{1,0:T(8,128)(2,1...) custom-call(bf16[4,96,512]{2,1,0:T(8,128)(2,1)S(1)} %get-tuple-element.50.delta_ref.delta_in, ...), custom_call_target="tpu_custom_call" | custom-call | flops 301989888 | bytes 2000000 | tf_op jit(solution)/shard_map/pallas_call | solution.py:414
  27.9 0.3 collective-permute-done.6
  28.2 0.9 %add.3 = f32[1024,128]{1,0:T(8,128)} add(f32[1024,128]{1,0:T(8,128)S(1)} %get-tuple-element.48, f32[1024,128]{1,0:T(8,128)S(1)} %collective-permute-done.6) | non-fusion elementwise | flops 131072 | bytes 1572864 | tf_op jit(solution)/shard_map/add | solution.py:427
  29.1 0.0 copy-done
  29.1 7.2 %all-to-all-start = ((f32[16,64,128]{2,1,0:T(8,128)}), f32[16,64,128]{2,1,0:T(8,128)S(1)}, u32[]{:S(2)}, u32[]{:S(2)}) async-start(f32[16,64,128]{2,1,0:T(8,128)} %bitcast.1), calls=%async_computation | async-start | bytes 1048576 | tf_op jit(solution)/shard_map/all_to_all | solution.py:380
  36.3 0.1 collective-permute-start.7
  36.4 1.4 %collective-permute-start.9 = (bf16[2,96,128]{2,1,0:T(8,128)(2,1)S(1)}, bf16[2,96,128]{2,1,0:T(8,128)(2,1)S(1)}, u32[]{:S(2)}, u32[]{:S(2)}) collective-permute-start(bf16[2,96,128]{2,1,0:T(8,128)(2,1)S(1)} %get-tuple-element.60), channel_id=1, source_target_pairs={{0,1},{1,0},{2,3},{3,2},{4,5},{5,4},{6,7},{7,6},{8,9},{9,8},{10,11... | collective-permute-start | bytes 147464 | tf_op jit(solution)/shard_map/ppermute | solution.py:374
  37.8 1.2 %collective-permute-start.8 = (bf16[96,128]{1,0:T(8,128)(2,1)S(1)}, bf16[96,128]{1,0:T(8,128)(2,1)S(1)}, u32[]{:S(2)}, u32[]{:S(2)}) collective-permute-start(bf16[96,128]{1,0:T(8,128)(2,1)S(1)} %get-tuple-element.59), channel_id=1, source_target_pairs={{0,64},{64,0},{128,192},{192,128},{1,65},{65,1},{129,193},{193,129... | collective-permute-start | bytes 73736 | tf_op jit(solution)/shard_map/ppermute | solution.py:372
  39.0 2.0 %collective-permute-done.8.recv2 = bf16[96,128]{1,0:T(8,128)(2,1)S(1)} collective-permute-done((bf16[96,128]{1,0:T(8,128)(2,1)S(1)}, bf16[96,128]{1,0:T(8,128)(2,1)S(1)}, u32[]{:S(2)}, u32[]{:S(2)}) %collective-permute-start.8) | collective-permute-done | bytes 24608 | tf_op jit(solution)/shard_map/ppermute | solution.py:372
  41.0 0.0 copy-start.5
  41.0 3.8 %collective-permute-done.9.recv4 = bf16[2,96,128]{2,1,0:T(8,128)(2,1)S(1)} collective-permute-done((bf16[2,96,128]{2,1,0:T(8,128)(2,1)S(1)}, bf16[2,96,128]{2,1,0:T(8,128)(2,1)S(1)}, u32[]{:S(2)}, u32[]{:S(2)}) %collective-permute-start.9) | collective-permute-done | bytes 49184 | tf_op jit(solution)/shard_map/ppermute | solution.py:374
  44.8 0.0 copy-start.2
  44.8 0.0 collective-permute-done.7.recv1
  44.8 0.0 copy-start.1
  44.8 2.3 %all-to-all-done.pieces_ref = f32[16,64,128]{2,1,0:T(8,128)S(1)} async-done(((f32[16,64,128]{2,1,0:T(8,128)}), f32[16,64,128]{2,1,0:T(8,128)S(1)}, u32[]{:S(2)}, u32[]{:S(2)}) %all-to-all-start) | async-done | bytes 524320 | tf_op jit(solution)/shard_map/all_to_all | solution.py:380
  47.0 0.7 shard_map.106
  47.8 3.6 %all-to-all-start.1 = ((f32[8,64,128]{2,1,0:T(8,128)}), f32[8,64,128]{2,1,0:T(8,128)S(1)}, u32[]{:S(2)}, u32[]{:S(2)}) async-start(f32[8,64,128]{2,1,0:T(8,128)} %shard_map.106), calls=%async_computation.1 | async-start | bytes 524288 | tf_op jit(solution)/shard_map/all_to_all | solution.py:380
  51.4 0.7 collective-permute-start.12
  52.0 1.0 %collective-permute-start.11 = (bf16[160,128]{1,0:T(8,128)(2,1)S(1)}, bf16[160,128]{1,0:T(8,128)(2,1)S(1)}, u32[]{:S(2)}, u32[]{:S(2)}) collective-permute-start(bf16[160,128]{1,0:T(8,128)(2,1)S(1)} %get-tuple-element.63), channel_id=1, source_target_pairs={{0,128},{64,192},{128,0},{192,64},{1,129},{65,193},{129,1},{193,65... | collective-permute-start | bytes 122888 | tf_op jit(solution)/shard_map/ppermute | solution.py:373
  53.0 2.3 %collective-permute-start.10 = (bf16[96,128]{1,0:T(8,128)(2,1)S(1)}, bf16[96,128]{1,0:T(8,128)(2,1)S(1)}, u32[]{:S(2)}, u32[]{:S(2)}) collective-permute-start(bf16[96,128]{1,0:T(8,128)(2,1)S(1)} %get-tuple-element.62), channel_id=1, source_target_pairs={{0,16},{16,0},{1,17},{17,1},{2,18},{18,2},{3,19},{19,3},{4,20},{20... | collective-permute-start | bytes 73736 | tf_op jit(solution)/shard_map/ppermute | solution.py:370
  55.3 2.1 %shard_map.107.own_in = bf16[16,96,128]{2,1,0:T(8,128)(2,1)} custom-call(bf16[4,96,512]{2,1,0:T(8,128)(2,1)} %copy-done), custom_call_target="tpu_custom_call" | custom-call | flops 201326592 | bytes 2000000 | tf_op jit(solution)/shard_map/pallas_call | solution.py:419
  57.4 0.0 collective-permute-done.10.recv0
  57.4 0.0 copy-start.6
  57.4 0.0 collective-permute-done.11.recv3
  57.4 0.0 copy-start.4
  57.4 0.0 collective-permute-done.12.recv5
  57.4 0.0 copy-start.3
  57.5 3.3 %all-to-all-done.1.pieces_ref = f32[8,64,128]{2,1,0:T(8,128)S(1)} async-done(((f32[8,64,128]{2,1,0:T(8,128)}), f32[8,64,128]{2,1,0:T(8,128)S(1)}, u32[]{:S(2)}, u32[]{:S(2)}) %all-to-all-start.1) | async-done | bytes 262176 | tf_op jit(solution)/shard_map/all_to_all | solution.py:380
  60.8 0.7 shard_map.108
  61.5 0.0 copy-done.5
  61.5 0.0 copy-done.2
  61.5 0.0 copy-done.1
  61.5 5.8 %all-to-all-start.2 = ((bf16[16,64,128]{2,1,0:T(8,128)(2,1)}), bf16[16,64,128]{2,1,0:T(8,128)(2,1)S(1)}, u32[]{:S(2)}, u32[]{:S(2)}) async-start(bf16[16,64,128]{2,1,0:T(8,128)(2,1)} %shard_map.108), calls=%async_computation.2 | async-start | bytes 524288 | tf_op jit(solution)/shard_map/all_to_all | solution.py:380
  67.3 0.0 copy-done.6
  67.3 0.0 copy-done.4
  67.3 0.0 copy-done.3
  67.3 5.3 %shard_map.109 = bf16[4,96,512]{2,1,0:T(8,128)(2,1)} custom-call(s32[4,512]{1,0:T(4,128)} %occ_in.5, bf16[4,96,512]{2,1,0:T(8,128)(2,1)} %grad_in.3, bf16[27,96,96]{2,1,0:T(8,128)(2,1)} %w_in.3, s32[4,4]{1,0:T(4,128)} %src_in.3, s32[4]{0:T(128)} %down_in.3, s32[4]{0:T(128)} %up_in.3, bf16[4,96,512]{2,1,0:T(8,128)(2,1)} %copy-done, ...), custom_call_target="tpu_custom_call" | custom-call | flops 5000000000 | bytes 4000000 | tf_op jit(solution)/shard_map/pallas_call | solution.py:435
  72.6 2.3 %all-to-all-done.2 = bf16[16,64,128]{2,1,0:T(8,128)(2,1)S(1)} async-done(((bf16[16,64,128]{2,1,0:T(8,128)(2,1)}), bf16[16,64,128]{2,1,0:T(8,128)(2,1)S(1)}, u32[]{:S(2)}, u32[]{:S(2)}) %all-to-all-start.2) | async-done | bytes 262176 | tf_op jit(solution)/shard_map/all_to_all | solution.py:380
  74.9 2.9 %collective-permute-start.13 = (bf16[1024,128]{1,0:T(8,128)(2,1)S(1)}, bf16[1024,128]{1,0:T(8,128)(2,1)S(1)}, u32[]{:S(2)}, u32[]{:S(2)}) collective-permute-start(bf16[1024,128]{1,0:T(8,128)(2,1)S(1)} %bitcast.4), channel_id=1, source_target_pairs={{0,16},{16,0},{1,17},{17,1},{2,18},{18,2},{3,19},{19,3},{4,20},{20... | collective-permute-start | bytes 786440 | tf_op jit(solution)/shard_map/ppermute | solution.py:446
  77.8 1.2 %collective-permute-done.13.other_ref = bf16[1024,128]{1,0:T(8,128)(2,1)S(1)} collective-permute-done((bf16[1024,128]{1,0:T(8,128)(2,1)S(1)}, bf16[1024,128]{1,0:T(8,128)(2,1)S(1)}, u32[]{:S(2)}, u32[]{:S(2)}) %collective-permute-start.13) | collective-permute-done | bytes 262176 | tf_op jit(solution)/shard_map/ppermute | solution.py:446
  78.9 1.4 %shard_map.110 = f32[2592,96]{1,0:T(8,128)} custom-call(bf16[1024,128]{1,0:T(8,128)(2,1)S(1)} %bitcast.5, bf16[1024,128]{1,0:T(8,128)(2,1)S(1)} %collective-permute-done.13.other_ref), custom_call_target="tpu_custom_call" | custom-call | tf_op jit(solution)/shard_map/pallas_call | solution.py:447
Async XLA Ops:
  2.2 16.5 %collective-permute-start.1 = (bf16[224,128]{1,0:T(8,128)(2,1)S(1)}, bf16[224,128]{1,0:T(8,128)(2,1)S(1)}, u32[]{:S(2)}, u32[]{:S(2)}) collective-permute-start(bf16[224,128]{1,0:T(8,128)(2,1)S(1)} %get-tuple-element.42), channel_id=1, source_target_pairs={{0,32},{32,0},{1,33},{33,1},{2,34},{34,2},{3,35},{35,3},{4,36},{36... | collective-permute-start | bytes 172040 | tf_op jit(solution)/shard_map/ppermute | solution.py:371
  10.0 5.8 %collective-permute-start = (bf16[96,128]{1,0:T(8,128)(2,1)S(1)}, bf16[96,128]{1,0:T(8,128)(2,1)S(1)}, u32[]{:S(2)}, u32[]{:S(2)}) collective-permute-start(bf16[96,128]{1,0:T(8,128)(2,1)S(1)} %get-tuple-element.41), channel_id=1, source_target_pairs={{0,16},{16,0},{1,17},{17,1},{2,18},{18,2},{3,19},{19,3},{4,20},{20... | collective-permute-start | bytes 73736 | tf_op jit(solution)/shard_map/ppermute | solution.py:370
  11.0 7.7 %collective-permute-start.4 = (bf16[2,96,128]{2,1,0:T(8,128)(2,1)S(1)}, bf16[2,96,128]{2,1,0:T(8,128)(2,1)S(1)}, u32[]{:S(2)}, u32[]{:S(2)}) collective-permute-start(bf16[2,96,128]{2,1,0:T(8,128)(2,1)S(1)} %get-tuple-element.45), channel_id=1, source_target_pairs={{0,1},{1,0},{2,3},{3,2},{4,5},{5,4},{6,7},{7,6},{8,9},{9,8},{10,11... | collective-permute-start | bytes 147464 | tf_op jit(solution)/shard_map/ppermute | solution.py:374
  12.2 6.5 %collective-permute-start.5 = (bf16[2,96,128]{2,1,0:T(8,128)(2,1)S(1)}, bf16[2,96,128]{2,1,0:T(8,128)(2,1)S(1)}, u32[]{:S(2)}, u32[]{:S(2)}) collective-permute-start(bf16[2,96,128]{2,1,0:T(8,128)(2,1)S(1)} %get-tuple-element.46), channel_id=1, source_target_pairs={{1,2},{2,1},{3,4},{4,3},{5,6},{6,5},{7,8},{8,7},{9,10},{10,9},{11,... | collective-permute-start | bytes 147464 | tf_op jit(solution)/shard_map/ppermute | solution.py:375
  12.9 5.8 %collective-permute-start.3 = (bf16[160,128]{1,0:T(8,128)(2,1)S(1)}, bf16[160,128]{1,0:T(8,128)(2,1)S(1)}, u32[]{:S(2)}, u32[]{:S(2)}) collective-permute-start(bf16[160,128]{1,0:T(8,128)(2,1)S(1)} %get-tuple-element.44), channel_id=1, source_target_pairs={{0,128},{64,192},{128,0},{192,64},{1,129},{65,193},{129,1},{193,65... | collective-permute-start | bytes 122888 | tf_op jit(solution)/shard_map/ppermute | solution.py:373
  15.9 2.8 %collective-permute-start.2 = (bf16[96,128]{1,0:T(8,128)(2,1)S(1)}, bf16[96,128]{1,0:T(8,128)(2,1)S(1)}, u32[]{:S(2)}, u32[]{:S(2)}) collective-permute-start(bf16[96,128]{1,0:T(8,128)(2,1)S(1)} %get-tuple-element.43), channel_id=1, source_target_pairs={{0,64},{64,0},{128,192},{192,128},{1,65},{65,1},{129,193},{193,129... | collective-permute-start | bytes 73736 | tf_op jit(solution)/shard_map/ppermute | solution.py:372
  25.0 4.1 %copy-start = (bf16[4,96,512]{2,1,0:T(8,128)(2,1)}, bf16[4,96,512]{2,1,0:T(8,128)(2,1)S(1)}, u32[]{:S(2)}) copy-start(bf16[4,96,512]{2,1,0:T(8,128)(2,1)S(1)} %get-tuple-element.50.delta_ref.delta_in) | copy-start | bytes 1179652
  25.0 3.2 %collective-permute-start.6 = (f32[1024,128]{1,0:T(8,128)S(1)}, f32[1024,128]{1,0:T(8,128)S(1)}, u32[]{:S(2)}, u32[]{:S(2)}) collective-permute-start(f32[1024,128]{1,0:T(8,128)S(1)} %get-tuple-element.49), channel_id=1, source_target_pairs={{0,16},{16,0},{1,17},{17,1},{2,18},{18,2},{3,19},{19,3},{4,20},{20... | collective-permute-start | bytes 1572872 | tf_op jit(solution)/shard_map/ppermute | solution.py:424
  29.1 17.9 %all-to-all-start = ((f32[16,64,128]{2,1,0:T(8,128)}), f32[16,64,128]{2,1,0:T(8,128)S(1)}, u32[]{:S(2)}, u32[]{:S(2)}) async-start(f32[16,64,128]{2,1,0:T(8,128)} %bitcast.1), calls=%async_computation | async-start | bytes 1048576 | tf_op jit(solution)/shard_map/all_to_all | solution.py:380
  36.3 8.5 %collective-permute-start.7 = (bf16[224,128]{1,0:T(8,128)(2,1)S(1)}, bf16[224,128]{1,0:T(8,128)(2,1)S(1)}, u32[]{:S(2)}, u32[]{:S(2)}) collective-permute-start(bf16[224,128]{1,0:T(8,128)(2,1)S(1)} %get-tuple-element.58), channel_id=1, source_target_pairs={{0,32},{32,0},{1,33},{33,1},{2,34},{34,2},{3,35},{35,3},{4,36},{36... | collective-permute-start | bytes 172040 | tf_op jit(solution)/shard_map/ppermute | solution.py:371
  36.4 8.3 %collective-permute-start.9 = (bf16[2,96,128]{2,1,0:T(8,128)(2,1)S(1)}, bf16[2,96,128]{2,1,0:T(8,128)(2,1)S(1)}, u32[]{:S(2)}, u32[]{:S(2)}) collective-permute-start(bf16[2,96,128]{2,1,0:T(8,128)(2,1)S(1)} %get-tuple-element.60), channel_id=1, source_target_pairs={{0,1},{1,0},{2,3},{3,2},{4,5},{5,4},{6,7},{7,6},{8,9},{9,8},{10,11... | collective-permute-start | bytes 147464 | tf_op jit(solution)/shard_map/ppermute | solution.py:374
  37.8 3.2 %collective-permute-start.8 = (bf16[96,128]{1,0:T(8,128)(2,1)S(1)}, bf16[96,128]{1,0:T(8,128)(2,1)S(1)}, u32[]{:S(2)}, u32[]{:S(2)}) collective-permute-start(bf16[96,128]{1,0:T(8,128)(2,1)S(1)} %get-tuple-element.59), channel_id=1, source_target_pairs={{0,64},{64,0},{128,192},{192,128},{1,65},{65,1},{129,193},{193,129... | collective-permute-start | bytes 73736 | tf_op jit(solution)/shard_map/ppermute | solution.py:372
  41.0 20.5 %copy-start.5 = (bf16[96,128]{1,0:T(8,128)(2,1)}, bf16[96,128]{1,0:T(8,128)(2,1)S(1)}, u32[]{:S(2)}) copy-start(bf16[96,128]{1,0:T(8,128)(2,1)S(1)} %collective-permute-done.8.recv2) | copy-start | bytes 73732
  44.8 16.7 %copy-start.2 = (bf16[2,96,128]{2,1,0:T(8,128)(2,1)}, bf16[2,96,128]{2,1,0:T(8,128)(2,1)S(1)}, u32[]{:S(2)}) copy-start(bf16[2,96,128]{2,1,0:T(8,128)(2,1)S(1)} %collective-permute-done.9.recv4) | copy-start | bytes 147460
  44.8 16.7 %copy-start.1 = (bf16[224,128]{1,0:T(8,128)(2,1)}, bf16[224,128]{1,0:T(8,128)(2,1)S(1)}, u32[]{:S(2)}) copy-start(bf16[224,128]{1,0:T(8,128)(2,1)S(1)} %collective-permute-done.7.recv1) | copy-start | bytes 172036
  47.8 13.0 %all-to-all-start.1 = ((f32[8,64,128]{2,1,0:T(8,128)}), f32[8,64,128]{2,1,0:T(8,128)S(1)}, u32[]{:S(2)}, u32[]{:S(2)}) async-start(f32[8,64,128]{2,1,0:T(8,128)} %shard_map.106), calls=%async_computation.1 | async-start | bytes 524288 | tf_op jit(solution)/shard_map/all_to_all | solution.py:380
  51.4 6.1 %collective-permute-start.12 = (bf16[2,96,128]{2,1,0:T(8,128)(2,1)S(1)}, bf16[2,96,128]{2,1,0:T(8,128)(2,1)S(1)}, u32[]{:S(2)}, u32[]{:S(2)}) collective-permute-start(bf16[2,96,128]{2,1,0:T(8,128)(2,1)S(1)} %get-tuple-element.64), channel_id=1, source_target_pairs={{1,2},{2,1},{3,4},{4,3},{5,6},{6,5},{7,8},{8,7},{9,10},{10,9},{11,... | collective-permute-start | bytes 147464 | tf_op jit(solution)/shard_map/ppermute | solution.py:375
  52.0 5.4 %collective-permute-start.11 = (bf16[160,128]{1,0:T(8,128)(2,1)S(1)}, bf16[160,128]{1,0:T(8,128)(2,1)S(1)}, u32[]{:S(2)}, u32[]{:S(2)}) collective-permute-start(bf16[160,128]{1,0:T(8,128)(2,1)S(1)} %get-tuple-element.63), channel_id=1, source_target_pairs={{0,128},{64,192},{128,0},{192,64},{1,129},{65,193},{129,1},{193,65... | collective-permute-start | bytes 122888 | tf_op jit(solution)/shard_map/ppermute | solution.py:373
  53.0 4.4 %collective-permute-start.10 = (bf16[96,128]{1,0:T(8,128)(2,1)S(1)}, bf16[96,128]{1,0:T(8,128)(2,1)S(1)}, u32[]{:S(2)}, u32[]{:S(2)}) collective-permute-start(bf16[96,128]{1,0:T(8,128)(2,1)S(1)} %get-tuple-element.62), channel_id=1, source_target_pairs={{0,16},{16,0},{1,17},{17,1},{2,18},{18,2},{3,19},{19,3},{4,20},{20... | collective-permute-start | bytes 73736 | tf_op jit(solution)/shard_map/ppermute | solution.py:370
  57.4 9.9 %copy-start.6 = (bf16[96,128]{1,0:T(8,128)(2,1)}, bf16[96,128]{1,0:T(8,128)(2,1)S(1)}, u32[]{:S(2)}) copy-start(bf16[96,128]{1,0:T(8,128)(2,1)S(1)} %collective-permute-done.10.recv0) | copy-start | bytes 73732
  57.4 9.9 %copy-start.4 = (bf16[160,128]{1,0:T(8,128)(2,1)}, bf16[160,128]{1,0:T(8,128)(2,1)S(1)}, u32[]{:S(2)}) copy-start(bf16[160,128]{1,0:T(8,128)(2,1)S(1)} %collective-permute-done.11.recv3) | copy-start | bytes 122884
  57.4 9.8 %copy-start.3 = (bf16[2,96,128]{2,1,0:T(8,128)(2,1)}, bf16[2,96,128]{2,1,0:T(8,128)(2,1)S(1)}, u32[]{:S(2)}) copy-start(bf16[2,96,128]{2,1,0:T(8,128)(2,1)S(1)} %collective-permute-done.12.recv5) | copy-start | bytes 147460
  61.5 13.4 %all-to-all-start.2 = ((bf16[16,64,128]{2,1,0:T(8,128)(2,1)}), bf16[16,64,128]{2,1,0:T(8,128)(2,1)S(1)}, u32[]{:S(2)}, u32[]{:S(2)}) async-start(bf16[16,64,128]{2,1,0:T(8,128)(2,1)} %shard_map.108), calls=%async_computation.2 | async-start | bytes 524288 | tf_op jit(solution)/shard_map/all_to_all | solution.py:380
  74.9 4.0 %collective-permute-start.13 = (bf16[1024,128]{1,0:T(8,128)(2,1)S(1)}, bf16[1024,128]{1,0:T(8,128)(2,1)S(1)}, u32[]{:S(2)}, u32[]{:S(2)}) collective-permute-start(bf16[1024,128]{1,0:T(8,128)(2,1)S(1)} %bitcast.4), channel_id=1, source_target_pairs={{0,16},{16,0},{1,17},{17,1},{2,18},{18,2},{3,19},{19,3},{4,20},{20... | collective-permute-start | bytes 786440 | tf_op jit(solution)/shard_map/ppermute | solution.py:446

commit v5 on v4

--- a/solution.py
+++ b/solution.py
@@ -426,10 +426,12 @@
     halos = exchange(*out)
     part = keep + other
     part = exchanged(part.reshape(16, HALF // 16, 128), PLANE)
-    part, halos[1], halos[2], halos[4] = lax.optimization_barrier((part, halos[1], halos[2], halos[4]))
+    part, delta_own, halos[1], halos[2], halos[4] = lax.optimization_barrier(
+        (part, delta_own, halos[1], halos[2], halos[4])
+    )
     part = exchanged(summed(part, 8, F32), COLUMN)
-    part, delta_own, halos[0], halos[3], halos[5] = lax.optimization_barrier(
-        (part, delta_own, halos[0], halos[3], halos[5])
+    part, halos[0], halos[3], halos[5] = lax.optimization_barrier(
+        (part, halos[0], halos[3], halos[5])
     )
     part = exchanged(summed(part, 16, BF16), PLANE)
     (input_grad,) = call(

time: 81 us -> 80.8 us (level)
    ppermute x2, waiting for transfers between devices: 4.44 us -> 2.39 us  [exchange(): lax.ppermute(lat2, 'y', [(i, i ^ 1) for i in range(4)])]
    all_to_all x3, starting transfers between devices: 16.6 us -> 15.1 us  [exchanged(): return lax.all_to_all(pieces, axes, 0, 0, tiled=True)]
    ppermute x1, starting transfers between devices: 2.86 us -> 4.16 us  [on_device(): other = lax.ppermute(mine, 'c', [(0, 1), (1, 0)])]
    all_to_all x3, waiting for transfers between devices: 7.9 us -> 8.83 us  [exchanged(): return lax.all_to_all(pieces, axes, 0, 0, tiled=True)]
    ppermute x2, waiting for transfers between devices: 0.01 us -> 0.85 us  [exchange(): lax.ppermute(lat0, 'c', flip2)]
  transfers between devices with their start and end apart: 17 -> 17, of which waited for: 8 -> 9; matrix products, arithmetic and copies ran while one was open for 0% -> 0% of each run, Pallas kernels for 11% -> 11%
where the time goes in v5:
time: 80.8 us; the launch traced here: 80.3 us
  starting transfers between devices  41.5 us (51%)
  Pallas kernels  19.3 us (24%)
  waiting for transfers between devices  17.6 us (22%)
  between operations  0.98 us (1%)
  other arithmetic  0.87 us (1%)
    all_to_all x3, starting transfers between devices, exchanged(): return lax.all_to_all(pieces, axes, 0, 0, tiled=True)  15.1 us
    all_to_all x3, waiting for transfers between devices, exchanged(): return lax.all_to_all(pieces, axes, 0, 0, tiled=True)  8.83 us
    ppermute x2, starting transfers between devices, exchange(): lax.ppermute(lat1, 'zh', flip2)  7.92 us
    pallas_call x1, Pallas kernels, on_device(): call(forward_kernel, [HB] * 7 + [VM] * 8, [(HB, BLOCKS, BF16), (VM, BLOCK...  6.28 us
    pallas_call x1, Pallas kernels, on_device(): call(backward_kernel, [HB] * 14, [(HB, BLOCKS, BF16)], SCRATCH + [FEAT, p...  5.28 us
    ppermute x1, starting transfers between devices, on_device(): other = lax.ppermute(mine, 'c', [(0, 1), (1, 0)])  4.16 us
    ppermute x2, starting transfers between devices, exchange(): lax.ppermute(lat3, 'y', [(i, i ^ 2) for i in range(4)])  3.96 us
    ppermute x2, waiting for transfers between devices, exchange(): lax.ppermute(zf0, BAND, [p for i, j in pairs[0:15:2] for p in ((i, j), (j...  3.67 us
  transfers between devices with their start and end apart: 17, of which 9 were waited for; matrix products, arithmetic and copies ran while one was open for 0% of the time, Pallas kernels for 11%

profile of v5, /device:TPU:1, one launch (start us, length us, event | category | flops | bytes accessed | tf_op | source)
XLA Modules:
  0.0 80.3 jit_solution(18056130220972520860)
XLA Ops:
  0.6 1.6 %shard_map.103 = (bf16[4,96,512]{2,1,0:T(8,128)(2,1)S(1)}, bf16[16,96,128]{2,1,0:T(8,128)(2,1)S(1)}, bf16[96,128]{1,0:T(8,128)(2,1)S(1)}, bf16[224,128]{1,0:T(8,...) custom-call(bf16[4,96,512]{2,1,0:T(8,128)(2,1)} %feat_in.3, ...), custom_call_target="tpu_custom_call" | custom-call | tf_op jit(solution)/shard_map/pallas_call | solution.py:396
  2.2 7.8 %collective-permute-start.1 = (bf16[224,128]{1,0:T(8,128)(2,1)S(1)}, bf16[224,128]{1,0:T(8,128)(2,1)S(1)}, u32[]{:S(2)}, u32[]{:S(2)}) collective-permute-start(bf16[224,128]{1,0:T(8,128)(2,1)S(1)} %get-tuple-element.42), channel_id=1, source_target_pairs={{0,32},{32,0},{1,33},{33,1},{2,34},{34,2},{3,35},{35,3},{4,36},{36... | collective-permute-start | bytes 172040 | tf_op jit(solution)/shard_map/ppermute | solution.py:371
  10.0 1.0 %collective-permute-start = (bf16[96,128]{1,0:T(8,128)(2,1)S(1)}, bf16[96,128]{1,0:T(8,128)(2,1)S(1)}, u32[]{:S(2)}, u32[]{:S(2)}) collective-permute-start(bf16[96,128]{1,0:T(8,128)(2,1)S(1)} %get-tuple-element.41), channel_id=1, source_target_pairs={{0,16},{16,0},{1,17},{17,1},{2,18},{18,2},{3,19},{19,3},{4,20},{20... | collective-permute-start | bytes 73736 | tf_op jit(solution)/shard_map/ppermute | solution.py:370
  11.0 1.2 %collective-permute-start.4 = (bf16[2,96,128]{2,1,0:T(8,128)(2,1)S(1)}, bf16[2,96,128]{2,1,0:T(8,128)(2,1)S(1)}, u32[]{:S(2)}, u32[]{:S(2)}) collective-permute-start(bf16[2,96,128]{2,1,0:T(8,128)(2,1)S(1)} %get-tuple-element.45), channel_id=1, source_target_pairs={{0,1},{1,0},{2,3},{3,2},{4,5},{5,4},{6,7},{7,6},{8,9},{9,8},{10,11... | collective-permute-start | bytes 147464 | tf_op jit(solution)/shard_map/ppermute | solution.py:374
  12.2 0.7 collective-permute-start.5
  12.9 3.0 %collective-permute-start.3 = (bf16[160,128]{1,0:T(8,128)(2,1)S(1)}, bf16[160,128]{1,0:T(8,128)(2,1)S(1)}, u32[]{:S(2)}, u32[]{:S(2)}) collective-permute-start(bf16[160,128]{1,0:T(8,128)(2,1)S(1)} %get-tuple-element.44), channel_id=1, source_target_pairs={{0,128},{64,192},{128,0},{192,64},{1,129},{65,193},{129,1},{193,65... | collective-permute-start | bytes 122888 | tf_op jit(solution)/shard_map/ppermute | solution.py:373
  15.9 0.0 collective-permute-done.recv0
  15.9 0.4 collective-permute-start.2
  16.3 2.4 %collective-permute-done.2.recv2 = bf16[96,128]{1,0:T(8,128)(2,1)S(1)} collective-permute-done((bf16[96,128]{1,0:T(8,128)(2,1)S(1)}, bf16[96,128]{1,0:T(8,128)(2,1)S(1)}, u32[]{:S(2)}, u32[]{:S(2)}) %collective-permute-start.2) | collective-permute-done | bytes 24608 | tf_op jit(solution)/shard_map/ppermute | solution.py:372
  18.7 0.0 collective-permute-done.3.recv3
  18.7 0.0 collective-permute-done.4.recv4
  18.7 0.0 collective-permute-done.5.recv5
  18.7 0.0 collective-permute-done.1.recv1
  18.7 6.3 %shard_map.104 = (bf16[4,96,512]{2,1,0:T(8,128)(2,1)}, bf16[4,96,512]{2,1,0:T(8,128)(2,1)S(1)}, f32[1024,128]{1,0:T(8,128)S(1)}, f32[1024,128]{1,0:T(8,128)S(1)}) custom-call(bf16[4,96,512]{2,1,0:T(8,128)(2,1)} %feat_in.3, s32[4,512]{1,0:T(4,128)} %occ_in.5, bf16[4,96,512]{2,1,0:T(8,128)(2,1)} %grad_in.3, bf16[27,96,96]{2,1,0:T(8,128)(2,1)} %w_in.3, ...), custom_call_target="tpu_custom_call" | custom-call | tf_op jit(solution)/shard_map/pallas_call | solution.py:401
  25.0 0.0 copy-start
  25.0 1.7 %collective-permute-start.6 = (f32[1024,128]{1,0:T(8,128)S(1)}, f32[1024,128]{1,0:T(8,128)S(1)}, u32[]{:S(2)}, u32[]{:S(2)}) collective-permute-start(f32[1024,128]{1,0:T(8,128)S(1)} %get-tuple-element.49), channel_id=1, source_target_pairs={{0,16},{16,0},{1,17},{17,1},{2,18},{18,2},{3,19},{19,3},{4,20},{20... | collective-permute-start | bytes 1572872 | tf_op jit(solution)/shard_map/ppermute | solution.py:424
  26.7 1.2 %shard_map.105 = (bf16[96,128]{1,0:T(8,128)(2,1)S(1)}, bf16[224,128]{1,0:T(8,128)(2,1)S(1)}, bf16[96,128]{1,0:T(8,128)(2,1)S(1)}, bf16[160,128]{1,0:T(8,128)(2,1...) custom-call(bf16[4,96,512]{2,1,0:T(8,128)(2,1)S(1)} %get-tuple-element.50.delta_ref.delta_in, ...), custom_call_target="tpu_custom_call" | custom-call | flops 301989888 | bytes 2000000 | tf_op jit(solution)/shard_map/pallas_call | solution.py:414
  27.9 0.3 collective-permute-done.6
  28.2 0.9 %add.3 = f32[1024,128]{1,0:T(8,128)} add(f32[1024,128]{1,0:T(8,128)S(1)} %get-tuple-element.48, f32[1024,128]{1,0:T(8,128)S(1)} %collective-permute-done.6) | non-fusion elementwise | flops 131072 | bytes 1572864 | tf_op jit(solution)/shard_map/add | solution.py:427
  29.1 0.0 copy-done
  29.1 7.2 %all-to-all-start = ((f32[16,64,128]{2,1,0:T(8,128)}), f32[16,64,128]{2,1,0:T(8,128)S(1)}, u32[]{:S(2)}, u32[]{:S(2)}) async-start(f32[16,64,128]{2,1,0:T(8,128)} %bitcast.1), calls=%async_computation | async-start | bytes 1048576 | tf_op jit(solution)/shard_map/all_to_all | solution.py:380
  36.3 0.1 collective-permute-start.7
  36.4 1.4 %collective-permute-start.9 = (bf16[2,96,128]{2,1,0:T(8,128)(2,1)S(1)}, bf16[2,96,128]{2,1,0:T(8,128)(2,1)S(1)}, u32[]{:S(2)}, u32[]{:S(2)}) collective-permute-start(bf16[2,96,128]{2,1,0:T(8,128)(2,1)S(1)} %get-tuple-element.60), channel_id=1, source_target_pairs={{0,1},{1,0},{2,3},{3,2},{4,5},{5,4},{6,7},{7,6},{8,9},{9,8},{10,11... | collective-permute-start | bytes 147464 | tf_op jit(solution)/shard_map/ppermute | solution.py:374
  37.8 1.2 %collective-permute-start.8 = (bf16[96,128]{1,0:T(8,128)(2,1)S(1)}, bf16[96,128]{1,0:T(8,128)(2,1)S(1)}, u32[]{:S(2)}, u32[]{:S(2)}) collective-permute-start(bf16[96,128]{1,0:T(8,128)(2,1)S(1)} %get-tuple-element.59), channel_id=1, source_target_pairs={{0,64},{64,0},{128,192},{192,128},{1,65},{65,1},{129,193},{193,129... | collective-permute-start | bytes 73736 | tf_op jit(solution)/shard_map/ppermute | solution.py:372
  39.0 2.1 %shard_map.106.own_in = bf16[16,96,128]{2,1,0:T(8,128)(2,1)} custom-call(bf16[4,96,512]{2,1,0:T(8,128)(2,1)} %copy-done), custom_call_target="tpu_custom_call" | custom-call | flops 201326592 | bytes 2000000 | tf_op jit(solution)/shard_map/pallas_call | solution.py:419
  41.1 0.0 collective-permute-done.8.recv2
  41.1 0.0 copy-start.5
  41.1 3.7 %collective-permute-done.9.recv4 = bf16[2,96,128]{2,1,0:T(8,128)(2,1)S(1)} collective-permute-done((bf16[2,96,128]{2,1,0:T(8,128)(2,1)S(1)}, bf16[2,96,128]{2,1,0:T(8,128)(2,1)S(1)}, u32[]{:S(2)}, u32[]{:S(2)}) %collective-permute-start.9) | collective-permute-done | bytes 49184 | tf_op jit(solution)/shard_map/ppermute | solution.py:374
  44.8 0.0 copy-start.2
  44.8 0.0 collective-permute-done.7.recv1
  44.8 0.0 copy-start.1
  44.8 2.3 %all-to-all-done.pieces_ref = f32[16,64,128]{2,1,0:T(8,128)S(1)} async-done(((f32[16,64,128]{2,1,0:T(8,128)}), f32[16,64,128]{2,1,0:T(8,128)S(1)}, u32[]{:S(2)}, u32[]{:S(2)}) %all-to-all-start) | async-done | bytes 524320 | tf_op jit(solution)/shard_map/all_to_all | solution.py:380
  47.0 0.7 shard_map.107
  47.8 3.4 %all-to-all-start.1 = ((f32[8,64,128]{2,1,0:T(8,128)}), f32[8,64,128]{2,1,0:T(8,128)S(1)}, u32[]{:S(2)}, u32[]{:S(2)}) async-start(f32[8,64,128]{2,1,0:T(8,128)} %shard_map.107), calls=%async_computation.1 | async-start | bytes 524288 | tf_op jit(solution)/shard_map/all_to_all | solution.py:380
  51.2 0.7 collective-permute-start.12
  51.9 1.0 %collective-permute-start.11 = (bf16[160,128]{1,0:T(8,128)(2,1)S(1)}, bf16[160,128]{1,0:T(8,128)(2,1)S(1)}, u32[]{:S(2)}, u32[]{:S(2)}) collective-permute-start(bf16[160,128]{1,0:T(8,128)(2,1)S(1)} %get-tuple-element.63), channel_id=1, source_target_pairs={{0,128},{64,192},{128,0},{192,64},{1,129},{65,193},{129,1},{193,65... | collective-permute-start | bytes 122888 | tf_op jit(solution)/shard_map/ppermute | solution.py:373
  52.8 2.3 %collective-permute-start.10 = (bf16[96,128]{1,0:T(8,128)(2,1)S(1)}, bf16[96,128]{1,0:T(8,128)(2,1)S(1)}, u32[]{:S(2)}, u32[]{:S(2)}) collective-permute-start(bf16[96,128]{1,0:T(8,128)(2,1)S(1)} %get-tuple-element.62), channel_id=1, source_target_pairs={{0,16},{16,0},{1,17},{17,1},{2,18},{18,2},{3,19},{19,3},{4,20},{20... | collective-permute-start | bytes 73736 | tf_op jit(solution)/shard_map/ppermute | solution.py:370
  55.1 0.8 %collective-permute-done.10.recv0 = bf16[96,128]{1,0:T(8,128)(2,1)S(1)} collective-permute-done((bf16[96,128]{1,0:T(8,128)(2,1)S(1)}, bf16[96,128]{1,0:T(8,128)(2,1)S(1)}, u32[]{:S(2)}, u32[]{:S(2)}) %collective-permute-start.10) | collective-permute-done | bytes 24608 | tf_op jit(solution)/shard_map/ppermute | solution.py:370
  55.9 0.0 copy-start.6
  55.9 0.3 collective-permute-done.11.recv3
  56.3 0.0 copy-start.4
  56.3 0.0 collective-permute-done.12.recv5
  56.3 0.0 copy-start.3
  56.3 4.3 %all-to-all-done.1.pieces_ref = f32[8,64,128]{2,1,0:T(8,128)S(1)} async-done(((f32[8,64,128]{2,1,0:T(8,128)}), f32[8,64,128]{2,1,0:T(8,128)S(1)}, u32[]{:S(2)}, u32[]{:S(2)}) %all-to-all-start.1) | async-done | bytes 262176 | tf_op jit(solution)/shard_map/all_to_all | solution.py:380
  60.6 0.7 shard_map.108
  61.3 4.4 %all-to-all-start.2 = ((bf16[16,64,128]{2,1,0:T(8,128)(2,1)}), bf16[16,64,128]{2,1,0:T(8,128)(2,1)S(1)}, u32[]{:S(2)}, u32[]{:S(2)}) async-start(bf16[16,64,128]{2,1,0:T(8,128)(2,1)} %shard_map.108), calls=%async_computation.2 | async-start | bytes 524288 | tf_op jit(solution)/shard_map/all_to_all | solution.py:380
  65.8 0.0 copy-done.5
  65.8 0.0 copy-done.2
  65.8 0.0 copy-done.1
  65.8 0.0 copy-done.6
  65.8 0.0 copy-done.4
  65.8 0.0 copy-done.3
  65.8 5.3 %shard_map.109 = bf16[4,96,512]{2,1,0:T(8,128)(2,1)} custom-call(s32[4,512]{1,0:T(4,128)} %occ_in.5, bf16[4,96,512]{2,1,0:T(8,128)(2,1)} %grad_in.3, bf16[27,96,96]{2,1,0:T(8,128)(2,1)} %w_in.3, s32[4,4]{1,0:T(4,128)} %src_in.3, s32[4]{0:T(128)} %down_in.3, s32[4]{0:T(128)} %up_in.3, bf16[4,96,512]{2,1,0:T(8,128)(2,1)} %copy-done, ...), custom_call_target="tpu_custom_call" | custom-call | flops 5000000000 | bytes 4000000 | tf_op jit(solution)/shard_map/pallas_call | solution.py:437
  71.1 2.3 %all-to-all-done.2 = bf16[16,64,128]{2,1,0:T(8,128)(2,1)S(1)} async-done(((bf16[16,64,128]{2,1,0:T(8,128)(2,1)}), bf16[16,64,128]{2,1,0:T(8,128)(2,1)S(1)}, u32[]{:S(2)}, u32[]{:S(2)}) %all-to-all-start.2) | async-done | bytes 262176 | tf_op jit(solution)/shard_map/all_to_all | solution.py:380
  73.4 4.2 %collective-permute-start.13 = (bf16[1024,128]{1,0:T(8,128)(2,1)S(1)}, bf16[1024,128]{1,0:T(8,128)(2,1)S(1)}, u32[]{:S(2)}, u32[]{:S(2)}) collective-permute-start(bf16[1024,128]{1,0:T(8,128)(2,1)S(1)} %bitcast.4), channel_id=1, source_target_pairs={{0,16},{16,0},{1,17},{17,1},{2,18},{18,2},{3,19},{19,3},{4,20},{20... | collective-permute-start | bytes 786440 | tf_op jit(solution)/shard_map/ppermute | solution.py:448
  77.6 1.2 %collective-permute-done.13.other_ref = bf16[1024,128]{1,0:T(8,128)(2,1)S(1)} collective-permute-done((bf16[1024,128]{1,0:T(8,128)(2,1)S(1)}, bf16[1024,128]{1,0:T(8,128)(2,1)S(1)}, u32[]{:S(2)}, u32[]{:S(2)}) %collective-permute-start.13) | collective-permute-done | bytes 262176 | tf_op jit(solution)/shard_map/ppermute | solution.py:448
  78.7 1.4 %shard_map.110 = f32[2592,96]{1,0:T(8,128)} custom-call(bf16[1024,128]{1,0:T(8,128)(2,1)S(1)} %bitcast.5, bf16[1024,128]{1,0:T(8,128)(2,1)S(1)} %collective-permute-done.13.other_ref), custom_call_target="tpu_custom_call" | custom-call | tf_op jit(solution)/shard_map/pallas_call | solution.py:449
Async XLA Ops:
  2.2 16.5 %collective-permute-start.1 = (bf16[224,128]{1,0:T(8,128)(2,1)S(1)}, bf16[224,128]{1,0:T(8,128)(2,1)S(1)}, u32[]{:S(2)}, u32[]{:S(2)}) collective-permute-start(bf16[224,128]{1,0:T(8,128)(2,1)S(1)} %get-tuple-element.42), channel_id=1, source_target_pairs={{0,32},{32,0},{1,33},{33,1},{2,34},{34,2},{3,35},{35,3},{4,36},{36... | collective-permute-start | bytes 172040 | tf_op jit(solution)/shard_map/ppermute | solution.py:371
  10.0 5.8 %collective-permute-start = (bf16[96,128]{1,0:T(8,128)(2,1)S(1)}, bf16[96,128]{1,0:T(8,128)(2,1)S(1)}, u32[]{:S(2)}, u32[]{:S(2)}) collective-permute-start(bf16[96,128]{1,0:T(8,128)(2,1)S(1)} %get-tuple-element.41), channel_id=1, source_target_pairs={{0,16},{16,0},{1,17},{17,1},{2,18},{18,2},{3,19},{19,3},{4,20},{20... | collective-permute-start | bytes 73736 | tf_op jit(solution)/shard_map/ppermute | solution.py:370
  11.0 7.7 %collective-permute-start.4 = (bf16[2,96,128]{2,1,0:T(8,128)(2,1)S(1)}, bf16[2,96,128]{2,1,0:T(8,128)(2,1)S(1)}, u32[]{:S(2)}, u32[]{:S(2)}) collective-permute-start(bf16[2,96,128]{2,1,0:T(8,128)(2,1)S(1)} %get-tuple-element.45), channel_id=1, source_target_pairs={{0,1},{1,0},{2,3},{3,2},{4,5},{5,4},{6,7},{7,6},{8,9},{9,8},{10,11... | collective-permute-start | bytes 147464 | tf_op jit(solution)/shard_map/ppermute | solution.py:374
  12.2 6.5 %collective-permute-start.5 = (bf16[2,96,128]{2,1,0:T(8,128)(2,1)S(1)}, bf16[2,96,128]{2,1,0:T(8,128)(2,1)S(1)}, u32[]{:S(2)}, u32[]{:S(2)}) collective-permute-start(bf16[2,96,128]{2,1,0:T(8,128)(2,1)S(1)} %get-tuple-element.46), channel_id=1, source_target_pairs={{1,2},{2,1},{3,4},{4,3},{5,6},{6,5},{7,8},{8,7},{9,10},{10,9},{11,... | collective-permute-start | bytes 147464 | tf_op jit(solution)/shard_map/ppermute | solution.py:375
  12.9 5.8 %collective-permute-start.3 = (bf16[160,128]{1,0:T(8,128)(2,1)S(1)}, bf16[160,128]{1,0:T(8,128)(2,1)S(1)}, u32[]{:S(2)}, u32[]{:S(2)}) collective-permute-start(bf16[160,128]{1,0:T(8,128)(2,1)S(1)} %get-tuple-element.44), channel_id=1, source_target_pairs={{0,128},{64,192},{128,0},{192,64},{1,129},{65,193},{129,1},{193,65... | collective-permute-start | bytes 122888 | tf_op jit(solution)/shard_map/ppermute | solution.py:373
  15.9 2.8 %collective-permute-start.2 = (bf16[96,128]{1,0:T(8,128)(2,1)S(1)}, bf16[96,128]{1,0:T(8,128)(2,1)S(1)}, u32[]{:S(2)}, u32[]{:S(2)}) collective-permute-start(bf16[96,128]{1,0:T(8,128)(2,1)S(1)} %get-tuple-element.43), channel_id=1, source_target_pairs={{0,64},{64,0},{128,192},{192,128},{1,65},{65,1},{129,193},{193,129... | collective-permute-start | bytes 73736 | tf_op jit(solution)/shard_map/ppermute | solution.py:372
  25.0 4.1 %copy-start = (bf16[4,96,512]{2,1,0:T(8,128)(2,1)}, bf16[4,96,512]{2,1,0:T(8,128)(2,1)S(1)}, u32[]{:S(2)}) copy-start(bf16[4,96,512]{2,1,0:T(8,128)(2,1)S(1)} %get-tuple-element.50.delta_ref.delta_in) | copy-start | bytes 1179652
  25.0 3.2 %collective-permute-start.6 = (f32[1024,128]{1,0:T(8,128)S(1)}, f32[1024,128]{1,0:T(8,128)S(1)}, u32[]{:S(2)}, u32[]{:S(2)}) collective-permute-start(f32[1024,128]{1,0:T(8,128)S(1)} %get-tuple-element.49), channel_id=1, source_target_pairs={{0,16},{16,0},{1,17},{17,1},{2,18},{18,2},{3,19},{19,3},{4,20},{20... | collective-permute-start | bytes 1572872 | tf_op jit(solution)/shard_map/ppermute | solution.py:424
  29.1 17.9 %all-to-all-start = ((f32[16,64,128]{2,1,0:T(8,128)}), f32[16,64,128]{2,1,0:T(8,128)S(1)}, u32[]{:S(2)}, u32[]{:S(2)}) async-start(f32[16,64,128]{2,1,0:T(8,128)} %bitcast.1), calls=%async_computation | async-start | bytes 1048576 | tf_op jit(solution)/shard_map/all_to_all | solution.py:380
  36.3 8.5 %collective-permute-start.7 = (bf16[224,128]{1,0:T(8,128)(2,1)S(1)}, bf16[224,128]{1,0:T(8,128)(2,1)S(1)}, u32[]{:S(2)}, u32[]{:S(2)}) collective-permute-start(bf16[224,128]{1,0:T(8,128)(2,1)S(1)} %get-tuple-element.58), channel_id=1, source_target_pairs={{0,32},{32,0},{1,33},{33,1},{2,34},{34,2},{3,35},{35,3},{4,36},{36... | collective-permute-start | bytes 172040 | tf_op jit(solution)/shard_map/ppermute | solution.py:371
  36.4 8.3 %collective-permute-start.9 = (bf16[2,96,128]{2,1,0:T(8,128)(2,1)S(1)}, bf16[2,96,128]{2,1,0:T(8,128)(2,1)S(1)}, u32[]{:S(2)}, u32[]{:S(2)}) collective-permute-start(bf16[2,96,128]{2,1,0:T(8,128)(2,1)S(1)} %get-tuple-element.60), channel_id=1, source_target_pairs={{0,1},{1,0},{2,3},{3,2},{4,5},{5,4},{6,7},{7,6},{8,9},{9,8},{10,11... | collective-permute-start | bytes 147464 | tf_op jit(solution)/shard_map/ppermute | solution.py:374
  37.8 3.3 %collective-permute-start.8 = (bf16[96,128]{1,0:T(8,128)(2,1)S(1)}, bf16[96,128]{1,0:T(8,128)(2,1)S(1)}, u32[]{:S(2)}, u32[]{:S(2)}) collective-permute-start(bf16[96,128]{1,0:T(8,128)(2,1)S(1)} %get-tuple-element.59), channel_id=1, source_target_pairs={{0,64},{64,0},{128,192},{192,128},{1,65},{65,1},{129,193},{193,129... | collective-permute-start | bytes 73736 | tf_op jit(solution)/shard_map/ppermute | solution.py:372
  41.1 24.7 %copy-start.5 = (bf16[96,128]{1,0:T(8,128)(2,1)}, bf16[96,128]{1,0:T(8,128)(2,1)S(1)}, u32[]{:S(2)}) copy-start(bf16[96,128]{1,0:T(8,128)(2,1)S(1)} %collective-permute-done.8.recv2) | copy-start | bytes 73732
  44.8 21.0 %copy-start.2 = (bf16[2,96,128]{2,1,0:T(8,128)(2,1)}, bf16[2,96,128]{2,1,0:T(8,128)(2,1)S(1)}, u32[]{:S(2)}) copy-start(bf16[2,96,128]{2,1,0:T(8,128)(2,1)S(1)} %collective-permute-done.9.recv4) | copy-start | bytes 147460
  44.8 21.0 %copy-start.1 = (bf16[224,128]{1,0:T(8,128)(2,1)}, bf16[224,128]{1,0:T(8,128)(2,1)S(1)}, u32[]{:S(2)}) copy-start(bf16[224,128]{1,0:T(8,128)(2,1)S(1)} %collective-permute-done.7.recv1) | copy-start | bytes 172036
  47.8 12.8 %all-to-all-start.1 = ((f32[8,64,128]{2,1,0:T(8,128)}), f32[8,64,128]{2,1,0:T(8,128)S(1)}, u32[]{:S(2)}, u32[]{:S(2)}) async-start(f32[8,64,128]{2,1,0:T(8,128)} %shard_map.107), calls=%async_computation.1 | async-start | bytes 524288 | tf_op jit(solution)/shard_map/all_to_all | solution.py:380
  51.2 5.1 %collective-permute-start.12 = (bf16[2,96,128]{2,1,0:T(8,128)(2,1)S(1)}, bf16[2,96,128]{2,1,0:T(8,128)(2,1)S(1)}, u32[]{:S(2)}, u32[]{:S(2)}) collective-permute-start(bf16[2,96,128]{2,1,0:T(8,128)(2,1)S(1)} %get-tuple-element.64), channel_id=1, source_target_pairs={{1,2},{2,1},{3,4},{4,3},{5,6},{6,5},{7,8},{8,7},{9,10},{10,9},{11,... | collective-permute-start | bytes 147464 | tf_op jit(solution)/shard_map/ppermute | solution.py:375
  51.9 4.4 %collective-permute-start.11 = (bf16[160,128]{1,0:T(8,128)(2,1)S(1)}, bf16[160,128]{1,0:T(8,128)(2,1)S(1)}, u32[]{:S(2)}, u32[]{:S(2)}) collective-permute-start(bf16[160,128]{1,0:T(8,128)(2,1)S(1)} %get-tuple-element.63), channel_id=1, source_target_pairs={{0,128},{64,192},{128,0},{192,64},{1,129},{65,193},{129,1},{193,65... | collective-permute-start | bytes 122888 | tf_op jit(solution)/shard_map/ppermute | solution.py:373
  52.8 3.1 %collective-permute-start.10 = (bf16[96,128]{1,0:T(8,128)(2,1)S(1)}, bf16[96,128]{1,0:T(8,128)(2,1)S(1)}, u32[]{:S(2)}, u32[]{:S(2)}) collective-permute-start(bf16[96,128]{1,0:T(8,128)(2,1)S(1)} %get-tuple-element.62), channel_id=1, source_target_pairs={{0,16},{16,0},{1,17},{17,1},{2,18},{18,2},{3,19},{19,3},{4,20},{20... | collective-permute-start | bytes 73736 | tf_op jit(solution)/shard_map/ppermute | solution.py:370
  55.9 9.9 %copy-start.6 = (bf16[96,128]{1,0:T(8,128)(2,1)}, bf16[96,128]{1,0:T(8,128)(2,1)S(1)}, u32[]{:S(2)}) copy-start(bf16[96,128]{1,0:T(8,128)(2,1)S(1)} %collective-permute-done.10.recv0) | copy-start | bytes 73732
  56.3 9.5 %copy-start.4 = (bf16[160,128]{1,0:T(8,128)(2,1)}, bf16[160,128]{1,0:T(8,128)(2,1)S(1)}, u32[]{:S(2)}) copy-start(bf16[160,128]{1,0:T(8,128)(2,1)S(1)} %collective-permute-done.11.recv3) | copy-start | bytes 122884
  56.3 9.5 %copy-start.3 = (bf16[2,96,128]{2,1,0:T(8,128)(2,1)}, bf16[2,96,128]{2,1,0:T(8,128)(2,1)S(1)}, u32[]{:S(2)}) copy-start(bf16[2,96,128]{2,1,0:T(8,128)(2,1)S(1)} %collective-permute-done.12.recv5) | copy-start | bytes 147460
  61.3 12.1 %all-to-all-start.2 = ((bf16[16,64,128]{2,1,0:T(8,128)(2,1)}), bf16[16,64,128]{2,1,0:T(8,128)(2,1)S(1)}, u32[]{:S(2)}, u32[]{:S(2)}) async-start(bf16[16,64,128]{2,1,0:T(8,128)(2,1)} %shard_map.108), calls=%async_computation.2 | async-start | bytes 524288 | tf_op jit(solution)/shard_map/all_to_all | solution.py:380
  73.4 5.3 %collective-permute-start.13 = (bf16[1024,128]{1,0:T(8,128)(2,1)S(1)}, bf16[1024,128]{1,0:T(8,128)(2,1)S(1)}, u32[]{:S(2)}, u32[]{:S(2)}) collective-permute-start(bf16[1024,128]{1,0:T(8,128)(2,1)S(1)} %bitcast.4), channel_id=1, source_target_pairs={{0,16},{16,0},{1,17},{17,1},{2,18},{18,2},{3,19},{19,3},{4,20},{20... | collective-permute-start | bytes 786440 | tf_op jit(solution)/shard_map/ppermute | solution.py:448

commit v6 on v5

--- a/solution.py
+++ b/solution.py
@@ -426,12 +426,12 @@
     halos = exchange(*out)
     part = keep + other
     part = exchanged(part.reshape(16, HALF // 16, 128), PLANE)
-    part, delta_own, halos[1], halos[2], halos[4] = lax.optimization_barrier(
-        (part, delta_own, halos[1], halos[2], halos[4])
+    part, halos[1], halos[2] = lax.optimization_barrier(
+        (part, halos[1], halos[2])
     )
     part = exchanged(summed(part, 8, F32), COLUMN)
-    part, halos[0], halos[3], halos[5] = lax.optimization_barrier(
-        (part, halos[0], halos[3], halos[5])
+    part, delta_own, halos[0], halos[3], halos[4], halos[5] = lax.optimization_barrier(
+        (part, delta_own, halos[0], halos[3], halos[4], halos[5])
     )
     part = exchanged(summed(part, 16, BF16), PLANE)
     (input_grad,) = call(

time: 80.8 us -> 80.8 us (level)
    ppermute x2, waiting for transfers between devices: 0.01 us -> 3.92 us  [exchange(): lax.ppermute(lat1, 'zh', flip2)]
    ppermute x2, waiting for transfers between devices: 3.67 us -> 0.01 us  [exchange(): lax.ppermute(zf0, BAND, [p for i, j in pairs[0:15:2] for p in ((i, j), (j...]
    ppermute x2, waiting for transfers between devices: 2.39 us -> 4.41 us  [exchange(): lax.ppermute(lat2, 'y', [(i, i ^ 1) for i in range(4)])]
    ppermute x1, starting transfers between devices: 4.16 us -> 2.73 us  [on_device(): other = lax.ppermute(mine, 'c', [(0, 1), (1, 0)])]
    all_to_all x3, starting transfers between devices: 15.1 us -> 16.4 us  [exchanged(): return lax.all_to_all(pieces, axes, 0, 0, tiled=True)]
    ppermute x2, waiting for transfers between devices: 0.85 us -> 0.01 us  [exchange(): lax.ppermute(lat0, 'c', flip2)]
  transfers between devices with their start and end apart: 17 -> 17, of which waited for: 9 -> 8; matrix products, arithmetic and copies ran while one was open for 0% -> 0% of each run, Pallas kernels for 11% -> 11%
where the time goes in v6:
time: 80.8 us; the launch traced here: 80.3 us
  starting transfers between devices  40.8 us (50%)
  Pallas kernels  19.3 us (24%)
  waiting for transfers between devices  18.2 us (23%)
  between operations  1.01 us (1%)
  other arithmetic  0.87 us (1%)
    all_to_all x3, starting transfers between devices, exchanged(): return lax.all_to_all(pieces, axes, 0, 0, tiled=True)  16.4 us
    all_to_all x3, waiting for transfers between devices, exchanged(): return lax.all_to_all(pieces, axes, 0, 0, tiled=True)  8.41 us
    ppermute x2, starting transfers between devices, exchange(): lax.ppermute(lat1, 'zh', flip2)  7.92 us
    pallas_call x1, Pallas kernels, on_device(): call(forward_kernel, [HB] * 7 + [VM] * 8, [(HB, BLOCKS, BF16), (VM, BLOCK...  6.28 us
    pallas_call x1, Pallas kernels, on_device(): call(backward_kernel, [HB] * 14, [(HB, BLOCKS, BF16)], SCRATCH + [FEAT, p...  5.27 us
    ppermute x2, waiting for transfers between devices, exchange(): lax.ppermute(lat2, 'y', [(i, i ^ 1) for i in range(4)])  4.41 us
    ppermute x2, waiting for transfers between devices, exchange(): lax.ppermute(lat1, 'zh', flip2)  3.92 us
    ppermute x2, starting transfers between devices, exchange(): lax.ppermute(lat3, 'y', [(i, i ^ 2) for i in range(4)])  3.77 us
  transfers between devices with their start and end apart: 17, of which 8 were waited for; matrix products, arithmetic and copies ran while one was open for 0% of the time, Pallas kernels for 11%

profile of v6, /device:TPU:1, one launch (start us, length us, event | category | flops | bytes accessed | tf_op | source)
XLA Modules:
  0.0 80.3 jit_solution(149641003582997285)
XLA Ops:
  0.6 1.6 %shard_map.103 = (bf16[4,96,512]{2,1,0:T(8,128)(2,1)S(1)}, bf16[16,96,128]{2,1,0:T(8,128)(2,1)S(1)}, bf16[96,128]{1,0:T(8,128)(2,1)S(1)}, bf16[224,128]{1,0:T(8,...) custom-call(bf16[4,96,512]{2,1,0:T(8,128)(2,1)} %feat_in.3, ...), custom_call_target="tpu_custom_call" | custom-call | tf_op jit(solution)/shard_map/pallas_call | solution.py:396
  2.2 7.8 %collective-permute-start.1 = (bf16[224,128]{1,0:T(8,128)(2,1)S(1)}, bf16[224,128]{1,0:T(8,128)(2,1)S(1)}, u32[]{:S(2)}, u32[]{:S(2)}) collective-permute-start(bf16[224,128]{1,0:T(8,128)(2,1)S(1)} %get-tuple-element.42), channel_id=1, source_target_pairs={{0,32},{32,0},{1,33},{33,1},{2,34},{34,2},{3,35},{35,3},{4,36},{36... | collective-permute-start | bytes 172040 | tf_op jit(solution)/shard_map/ppermute | solution.py:371
  10.0 1.0 %collective-permute-start = (bf16[96,128]{1,0:T(8,128)(2,1)S(1)}, bf16[96,128]{1,0:T(8,128)(2,1)S(1)}, u32[]{:S(2)}, u32[]{:S(2)}) collective-permute-start(bf16[96,128]{1,0:T(8,128)(2,1)S(1)} %get-tuple-element.41), channel_id=1, source_target_pairs={{0,16},{16,0},{1,17},{17,1},{2,18},{18,2},{3,19},{19,3},{4,20},{20... | collective-permute-start | bytes 73736 | tf_op jit(solution)/shard_map/ppermute | solution.py:370
  11.0 1.2 %collective-permute-start.4 = (bf16[2,96,128]{2,1,0:T(8,128)(2,1)S(1)}, bf16[2,96,128]{2,1,0:T(8,128)(2,1)S(1)}, u32[]{:S(2)}, u32[]{:S(2)}) collective-permute-start(bf16[2,96,128]{2,1,0:T(8,128)(2,1)S(1)} %get-tuple-element.45), channel_id=1, source_target_pairs={{0,1},{1,0},{2,3},{3,2},{4,5},{5,4},{6,7},{7,6},{8,9},{9,8},{10,11... | collective-permute-start | bytes 147464 | tf_op jit(solution)/shard_map/ppermute | solution.py:374
  12.2 0.7 collective-permute-start.5
  12.9 3.0 %collective-permute-start.3 = (bf16[160,128]{1,0:T(8,128)(2,1)S(1)}, bf16[160,128]{1,0:T(8,128)(2,1)S(1)}, u32[]{:S(2)}, u32[]{:S(2)}) collective-permute-start(bf16[160,128]{1,0:T(8,128)(2,1)S(1)} %get-tuple-element.44), channel_id=1, source_target_pairs={{0,128},{64,192},{128,0},{192,64},{1,129},{65,193},{129,1},{193,65... | collective-permute-start | bytes 122888 | tf_op jit(solution)/shard_map/ppermute | solution.py:373
  15.9 0.0 collective-permute-done.recv0
  15.9 0.4 collective-permute-start.2
  16.3 2.4 %collective-permute-done.2.recv2 = bf16[96,128]{1,0:T(8,128)(2,1)S(1)} collective-permute-done((bf16[96,128]{1,0:T(8,128)(2,1)S(1)}, bf16[96,128]{1,0:T(8,128)(2,1)S(1)}, u32[]{:S(2)}, u32[]{:S(2)}) %collective-permute-start.2) | collective-permute-done | bytes 24608 | tf_op jit(solution)/shard_map/ppermute | solution.py:372
  18.7 0.0 collective-permute-done.3.recv3
  18.7 0.0 collective-permute-done.4.recv4
  18.7 0.0 collective-permute-done.5.recv5
  18.7 0.0 collective-permute-done.1.recv1
  18.7 6.3 %shard_map.104 = (bf16[4,96,512]{2,1,0:T(8,128)(2,1)}, bf16[4,96,512]{2,1,0:T(8,128)(2,1)S(1)}, f32[1024,128]{1,0:T(8,128)S(1)}, f32[1024,128]{1,0:T(8,128)S(1)}) custom-call(bf16[4,96,512]{2,1,0:T(8,128)(2,1)} %feat_in.3, s32[4,512]{1,0:T(4,128)} %occ_in.5, bf16[4,96,512]{2,1,0:T(8,128)(2,1)} %grad_in.3, bf16[27,96,96]{2,1,0:T(8,128)(2,1)} %w_in.3, ...), custom_call_target="tpu_custom_call" | custom-call | tf_op jit(solution)/shard_map/pallas_call | solution.py:401
  25.0 0.0 copy-start
  25.0 1.7 %collective-permute-start.6 = (f32[1024,128]{1,0:T(8,128)S(1)}, f32[1024,128]{1,0:T(8,128)S(1)}, u32[]{:S(2)}, u32[]{:S(2)}) collective-permute-start(f32[1024,128]{1,0:T(8,128)S(1)} %get-tuple-element.49), channel_id=1, source_target_pairs={{0,16},{16,0},{1,17},{17,1},{2,18},{18,2},{3,19},{19,3},{4,20},{20... | collective-permute-start | bytes 1572872 | tf_op jit(solution)/shard_map/ppermute | solution.py:424
  26.7 1.2 %shard_map.105 = (bf16[96,128]{1,0:T(8,128)(2,1)S(1)}, bf16[224,128]{1,0:T(8,128)(2,1)S(1)}, bf16[96,128]{1,0:T(8,128)(2,1)S(1)}, bf16[160,128]{1,0:T(8,128)(2,1...) custom-call(bf16[4,96,512]{2,1,0:T(8,128)(2,1)S(1)} %get-tuple-element.50.delta_ref.delta_in, ...), custom_call_target="tpu_custom_call" | custom-call | flops 301989888 | bytes 2000000 | tf_op jit(solution)/shard_map/pallas_call | solution.py:414
  27.9 0.3 collective-permute-done.6
  28.2 0.9 %add.3 = f32[1024,128]{1,0:T(8,128)} add(f32[1024,128]{1,0:T(8,128)S(1)} %get-tuple-element.48, f32[1024,128]{1,0:T(8,128)S(1)} %collective-permute-done.6) | non-fusion elementwise | flops 131072 | bytes 1572864 | tf_op jit(solution)/shard_map/add | solution.py:427
  29.1 0.0 copy-done
  29.1 7.2 %all-to-all-start = ((f32[16,64,128]{2,1,0:T(8,128)}), f32[16,64,128]{2,1,0:T(8,128)S(1)}, u32[]{:S(2)}, u32[]{:S(2)}) async-start(f32[16,64,128]{2,1,0:T(8,128)} %bitcast.1), calls=%async_computation | async-start | bytes 1048576 | tf_op jit(solution)/shard_map/all_to_all | solution.py:380
  36.3 0.1 collective-permute-start.7
  36.4 1.4 %collective-permute-start.8 = (bf16[96,128]{1,0:T(8,128)(2,1)S(1)}, bf16[96,128]{1,0:T(8,128)(2,1)S(1)}, u32[]{:S(2)}, u32[]{:S(2)}) collective-permute-start(bf16[96,128]{1,0:T(8,128)(2,1)S(1)} %get-tuple-element.59), channel_id=1, source_target_pairs={{0,64},{64,0},{128,192},{192,128},{1,65},{65,1},{129,193},{193,129... | collective-permute-start | bytes 73736 | tf_op jit(solution)/shard_map/ppermute | solution.py:372
  37.8 2.0 %collective-permute-done.8.recv2 = bf16[96,128]{1,0:T(8,128)(2,1)S(1)} collective-permute-done((bf16[96,128]{1,0:T(8,128)(2,1)S(1)}, bf16[96,128]{1,0:T(8,128)(2,1)S(1)}, u32[]{:S(2)}, u32[]{:S(2)}) %collective-permute-start.8) | collective-permute-done | bytes 24608 | tf_op jit(solution)/shard_map/ppermute | solution.py:372
  39.8 0.0 copy-start.5
  39.8 3.9 %collective-permute-done.7.recv1 = bf16[224,128]{1,0:T(8,128)(2,1)S(1)} collective-permute-done((bf16[224,128]{1,0:T(8,128)(2,1)S(1)}, bf16[224,128]{1,0:T(8,128)(2,1)S(1)}, u32[]{:S(2)}, u32[]{:S(2)}) %collective-permute-start.7) | collective-permute-done | bytes 57376 | tf_op jit(solution)/shard_map/ppermute | solution.py:371
  43.7 0.0 copy-start.1
  43.7 3.3 %all-to-all-done.pieces_ref = f32[16,64,128]{2,1,0:T(8,128)S(1)} async-done(((f32[16,64,128]{2,1,0:T(8,128)}), f32[16,64,128]{2,1,0:T(8,128)S(1)}, u32[]{:S(2)}, u32[]{:S(2)}) %all-to-all-start) | async-done | bytes 524320 | tf_op jit(solution)/shard_map/all_to_all | solution.py:380
  47.0 0.7 shard_map.106
  47.8 3.4 %all-to-all-start.1 = ((f32[8,64,128]{2,1,0:T(8,128)}), f32[8,64,128]{2,1,0:T(8,128)S(1)}, u32[]{:S(2)}, u32[]{:S(2)}) async-start(f32[8,64,128]{2,1,0:T(8,128)} %shard_map.106), calls=%async_computation.1 | async-start | bytes 524288 | tf_op jit(solution)/shard_map/all_to_all | solution.py:380
  51.2 0.6 collective-permute-start.11
  51.7 0.7 collective-permute-start.12
  52.4 0.8 collective-permute-start.10
  53.2 2.6 %collective-permute-start.9 = (bf16[96,128]{1,0:T(8,128)(2,1)S(1)}, bf16[96,128]{1,0:T(8,128)(2,1)S(1)}, u32[]{:S(2)}, u32[]{:S(2)}) collective-permute-start(bf16[96,128]{1,0:T(8,128)(2,1)S(1)} %get-tuple-element.61), channel_id=1, source_target_pairs={{0,16},{16,0},{1,17},{17,1},{2,18},{18,2},{3,19},{19,3},{4,20},{20... | collective-permute-start | bytes 73736 | tf_op jit(solution)/shard_map/ppermute | solution.py:370
  55.7 2.1 %shard_map.107.own_in = bf16[16,96,128]{2,1,0:T(8,128)(2,1)} custom-call(bf16[4,96,512]{2,1,0:T(8,128)(2,1)} %copy-done), custom_call_target="tpu_custom_call" | custom-call | flops 201326592 | bytes 2000000 | tf_op jit(solution)/shard_map/pallas_call | solution.py:419
  57.9 0.0 collective-permute-done.9.recv0
  57.9 0.0 copy-start.6
  57.9 0.0 collective-permute-done.10.recv3
  57.9 0.0 copy-start.4
  57.9 0.0 collective-permute-done.11.recv4
  57.9 0.0 copy-start.2
  57.9 0.0 collective-permute-done.12.recv5
  57.9 0.0 copy-start.3
  57.9 2.7 %all-to-all-done.1.pieces_ref = f32[8,64,128]{2,1,0:T(8,128)S(1)} async-done(((f32[8,64,128]{2,1,0:T(8,128)}), f32[8,64,128]{2,1,0:T(8,128)S(1)}, u32[]{:S(2)}, u32[]{:S(2)}) %all-to-all-start.1) | async-done | bytes 262176 | tf_op jit(solution)/shard_map/all_to_all | solution.py:380
  60.7 0.7 shard_map.108
  61.4 0.0 copy-done.5
  61.4 0.0 copy-done.1
  61.4 5.7 %all-to-all-start.2 = ((bf16[16,64,128]{2,1,0:T(8,128)(2,1)}), bf16[16,64,128]{2,1,0:T(8,128)(2,1)S(1)}, u32[]{:S(2)}, u32[]{:S(2)}) async-start(bf16[16,64,128]{2,1,0:T(8,128)(2,1)} %shard_map.108), calls=%async_computation.2 | async-start | bytes 524288 | tf_op jit(solution)/shard_map/all_to_all | solution.py:380
  67.1 0.0 copy-done.6
  67.1 0.0 copy-done.4
  67.2 0.0 copy-done.2
  67.2 0.0 copy-done.3
  67.2 5.3 %shard_map.109 = bf16[4,96,512]{2,1,0:T(8,128)(2,1)} custom-call(s32[4,512]{1,0:T(4,128)} %occ_in.5, bf16[4,96,512]{2,1,0:T(8,128)(2,1)} %grad_in.3, bf16[27,96,96]{2,1,0:T(8,128)(2,1)} %w_in.3, s32[4,4]{1,0:T(4,128)} %src_in.3, s32[4]{0:T(128)} %down_in.3, s32[4]{0:T(128)} %up_in.3, bf16[4,96,512]{2,1,0:T(8,128)(2,1)} %copy-done, ...), custom_call_target="tpu_custom_call" | custom-call | flops 5000000000 | bytes 4000000 | tf_op jit(solution)/shard_map/pallas_call | solution.py:437
  72.5 2.4 %all-to-all-done.2 = bf16[16,64,128]{2,1,0:T(8,128)(2,1)S(1)} async-done(((bf16[16,64,128]{2,1,0:T(8,128)(2,1)}), bf16[16,64,128]{2,1,0:T(8,128)(2,1)S(1)}, u32[]{:S(2)}, u32[]{:S(2)}) %all-to-all-start.2) | async-done | bytes 262176 | tf_op jit(solution)/shard_map/all_to_all | solution.py:380
  74.8 2.7 %collective-permute-start.13 = (bf16[1024,128]{1,0:T(8,128)(2,1)S(1)}, bf16[1024,128]{1,0:T(8,128)(2,1)S(1)}, u32[]{:S(2)}, u32[]{:S(2)}) collective-permute-start(bf16[1024,128]{1,0:T(8,128)(2,1)S(1)} %bitcast.4), channel_id=1, source_target_pairs={{0,16},{16,0},{1,17},{17,1},{2,18},{18,2},{3,19},{19,3},{4,20},{20... | collective-permute-start | bytes 786440 | tf_op jit(solution)/shard_map/ppermute | solution.py:448
  77.6 1.2 %collective-permute-done.13.other_ref = bf16[1024,128]{1,0:T(8,128)(2,1)S(1)} collective-permute-done((bf16[1024,128]{1,0:T(8,128)(2,1)S(1)}, bf16[1024,128]{1,0:T(8,128)(2,1)S(1)}, u32[]{:S(2)}, u32[]{:S(2)}) %collective-permute-start.13) | collective-permute-done | bytes 262176 | tf_op jit(solution)/shard_map/ppermute | solution.py:448
  78.7 1.4 %shard_map.110 = f32[2592,96]{1,0:T(8,128)} custom-call(bf16[1024,128]{1,0:T(8,128)(2,1)S(1)} %bitcast.5, bf16[1024,128]{1,0:T(8,128)(2,1)S(1)} %collective-permute-done.13.other_ref), custom_call_target="tpu_custom_call" | custom-call | tf_op jit(solution)/shard_map/pallas_call | solution.py:449
Async XLA Ops:
  2.2 16.5 %collective-permute-start.1 = (bf16[224,128]{1,0:T(8,128)(2,1)S(1)}, bf16[224,128]{1,0:T(8,128)(2,1)S(1)}, u32[]{:S(2)}, u32[]{:S(2)}) collective-permute-start(bf16[224,128]{1,0:T(8,128)(2,1)S(1)} %get-tuple-element.42), channel_id=1, source_target_pairs={{0,32},{32,0},{1,33},{33,1},{2,34},{34,2},{3,35},{35,3},{4,36},{36... | collective-permute-start | bytes 172040 | tf_op jit(solution)/shard_map/ppermute | solution.py:371
  10.0 5.8 %collective-permute-start = (bf16[96,128]{1,0:T(8,128)(2,1)S(1)}, bf16[96,128]{1,0:T(8,128)(2,1)S(1)}, u32[]{:S(2)}, u32[]{:S(2)}) collective-permute-start(bf16[96,128]{1,0:T(8,128)(2,1)S(1)} %get-tuple-element.41), channel_id=1, source_target_pairs={{0,16},{16,0},{1,17},{17,1},{2,18},{18,2},{3,19},{19,3},{4,20},{20... | collective-permute-start | bytes 73736 | tf_op jit(solution)/shard_map/ppermute | solution.py:370
  11.0 7.7 %collective-permute-start.4 = (bf16[2,96,128]{2,1,0:T(8,128)(2,1)S(1)}, bf16[2,96,128]{2,1,0:T(8,128)(2,1)S(1)}, u32[]{:S(2)}, u32[]{:S(2)}) collective-permute-start(bf16[2,96,128]{2,1,0:T(8,128)(2,1)S(1)} %get-tuple-element.45), channel_id=1, source_target_pairs={{0,1},{1,0},{2,3},{3,2},{4,5},{5,4},{6,7},{7,6},{8,9},{9,8},{10,11... | collective-permute-start | bytes 147464 | tf_op jit(solution)/shard_map/ppermute | solution.py:374
  12.2 6.5 %collective-permute-start.5 = (bf16[2,96,128]{2,1,0:T(8,128)(2,1)S(1)}, bf16[2,96,128]{2,1,0:T(8,128)(2,1)S(1)}, u32[]{:S(2)}, u32[]{:S(2)}) collective-permute-start(bf16[2,96,128]{2,1,0:T(8,128)(2,1)S(1)} %get-tuple-element.46), channel_id=1, source_target_pairs={{1,2},{2,1},{3,4},{4,3},{5,6},{6,5},{7,8},{8,7},{9,10},{10,9},{11,... | collective-permute-start | bytes 147464 | tf_op jit(solution)/shard_map/ppermute | solution.py:375
  12.9 5.8 %collective-permute-start.3 = (bf16[160,128]{1,0:T(8,128)(2,1)S(1)}, bf16[160,128]{1,0:T(8,128)(2,1)S(1)}, u32[]{:S(2)}, u32[]{:S(2)}) collective-permute-start(bf16[160,128]{1,0:T(8,128)(2,1)S(1)} %get-tuple-element.44), channel_id=1, source_target_pairs={{0,128},{64,192},{128,0},{192,64},{1,129},{65,193},{129,1},{193,65... | collective-permute-start | bytes 122888 | tf_op jit(solution)/shard_map/ppermute | solution.py:373
  15.9 2.8 %collective-permute-start.2 = (bf16[96,128]{1,0:T(8,128)(2,1)S(1)}, bf16[96,128]{1,0:T(8,128)(2,1)S(1)}, u32[]{:S(2)}, u32[]{:S(2)}) collective-permute-start(bf16[96,128]{1,0:T(8,128)(2,1)S(1)} %get-tuple-element.43), channel_id=1, source_target_pairs={{0,64},{64,0},{128,192},{192,128},{1,65},{65,1},{129,193},{193,129... | collective-permute-start | bytes 73736 | tf_op jit(solution)/shard_map/ppermute | solution.py:372
  25.0 4.1 %copy-start = (bf16[4,96,512]{2,1,0:T(8,128)(2,1)}, bf16[4,96,512]{2,1,0:T(8,128)(2,1)S(1)}, u32[]{:S(2)}) copy-start(bf16[4,96,512]{2,1,0:T(8,128)(2,1)S(1)} %get-tuple-element.50.delta_ref.delta_in) | copy-start | bytes 1179652
  25.0 3.2 %collective-permute-start.6 = (f32[1024,128]{1,0:T(8,128)S(1)}, f32[1024,128]{1,0:T(8,128)S(1)}, u32[]{:S(2)}, u32[]{:S(2)}) collective-permute-start(f32[1024,128]{1,0:T(8,128)S(1)} %get-tuple-element.49), channel_id=1, source_target_pairs={{0,16},{16,0},{1,17},{17,1},{2,18},{18,2},{3,19},{19,3},{4,20},{20... | collective-permute-start | bytes 1572872 | tf_op jit(solution)/shard_map/ppermute | solution.py:424
  29.1 17.9 %all-to-all-start = ((f32[16,64,128]{2,1,0:T(8,128)}), f32[16,64,128]{2,1,0:T(8,128)S(1)}, u32[]{:S(2)}, u32[]{:S(2)}) async-start(f32[16,64,128]{2,1,0:T(8,128)} %bitcast.1), calls=%async_computation | async-start | bytes 1048576 | tf_op jit(solution)/shard_map/all_to_all | solution.py:380
  36.3 7.4 %collective-permute-start.7 = (bf16[224,128]{1,0:T(8,128)(2,1)S(1)}, bf16[224,128]{1,0:T(8,128)(2,1)S(1)}, u32[]{:S(2)}, u32[]{:S(2)}) collective-permute-start(bf16[224,128]{1,0:T(8,128)(2,1)S(1)} %get-tuple-element.58), channel_id=1, source_target_pairs={{0,32},{32,0},{1,33},{33,1},{2,34},{34,2},{3,35},{35,3},{4,36},{36... | collective-permute-start | bytes 172040 | tf_op jit(solution)/shard_map/ppermute | solution.py:371
  36.4 3.4 %collective-permute-start.8 = (bf16[96,128]{1,0:T(8,128)(2,1)S(1)}, bf16[96,128]{1,0:T(8,128)(2,1)S(1)}, u32[]{:S(2)}, u32[]{:S(2)}) collective-permute-start(bf16[96,128]{1,0:T(8,128)(2,1)S(1)} %get-tuple-element.59), channel_id=1, source_target_pairs={{0,64},{64,0},{128,192},{192,128},{1,65},{65,1},{129,193},{193,129... | collective-permute-start | bytes 73736 | tf_op jit(solution)/shard_map/ppermute | solution.py:372
  39.8 21.6 %copy-start.5 = (bf16[96,128]{1,0:T(8,128)(2,1)}, bf16[96,128]{1,0:T(8,128)(2,1)S(1)}, u32[]{:S(2)}) copy-start(bf16[96,128]{1,0:T(8,128)(2,1)S(1)} %collective-permute-done.8.recv2) | copy-start | bytes 73732
  43.7 17.7 %copy-start.1 = (bf16[224,128]{1,0:T(8,128)(2,1)}, bf16[224,128]{1,0:T(8,128)(2,1)S(1)}, u32[]{:S(2)}) copy-start(bf16[224,128]{1,0:T(8,128)(2,1)S(1)} %collective-permute-done.7.recv1) | copy-start | bytes 172036
  47.8 12.9 %all-to-all-start.1 = ((f32[8,64,128]{2,1,0:T(8,128)}), f32[8,64,128]{2,1,0:T(8,128)S(1)}, u32[]{:S(2)}, u32[]{:S(2)}) async-start(f32[8,64,128]{2,1,0:T(8,128)} %shard_map.106), calls=%async_computation.1 | async-start | bytes 524288 | tf_op jit(solution)/shard_map/all_to_all | solution.py:380
  51.2 6.7 %collective-permute-start.11 = (bf16[2,96,128]{2,1,0:T(8,128)(2,1)S(1)}, bf16[2,96,128]{2,1,0:T(8,128)(2,1)S(1)}, u32[]{:S(2)}, u32[]{:S(2)}) collective-permute-start(bf16[2,96,128]{2,1,0:T(8,128)(2,1)S(1)} %get-tuple-element.63), channel_id=1, source_target_pairs={{0,1},{1,0},{2,3},{3,2},{4,5},{5,4},{6,7},{7,6},{8,9},{9,8},{10,11... | collective-permute-start | bytes 147464 | tf_op jit(solution)/shard_map/ppermute | solution.py:374
  51.7 6.2 %collective-permute-start.12 = (bf16[2,96,128]{2,1,0:T(8,128)(2,1)S(1)}, bf16[2,96,128]{2,1,0:T(8,128)(2,1)S(1)}, u32[]{:S(2)}, u32[]{:S(2)}) collective-permute-start(bf16[2,96,128]{2,1,0:T(8,128)(2,1)S(1)} %get-tuple-element.64), channel_id=1, source_target_pairs={{1,2},{2,1},{3,4},{4,3},{5,6},{6,5},{7,8},{8,7},{9,10},{10,9},{11,... | collective-permute-start | bytes 147464 | tf_op jit(solution)/shard_map/ppermute | solution.py:375
  52.4 5.5 %collective-permute-start.10 = (bf16[160,128]{1,0:T(8,128)(2,1)S(1)}, bf16[160,128]{1,0:T(8,128)(2,1)S(1)}, u32[]{:S(2)}, u32[]{:S(2)}) collective-permute-start(bf16[160,128]{1,0:T(8,128)(2,1)S(1)} %get-tuple-element.62), channel_id=1, source_target_pairs={{0,128},{64,192},{128,0},{192,64},{1,129},{65,193},{129,1},{193,65... | collective-permute-start | bytes 122888 | tf_op jit(solution)/shard_map/ppermute | solution.py:373
  53.2 4.7 %collective-permute-start.9 = (bf16[96,128]{1,0:T(8,128)(2,1)S(1)}, bf16[96,128]{1,0:T(8,128)(2,1)S(1)}, u32[]{:S(2)}, u32[]{:S(2)}) collective-permute-start(bf16[96,128]{1,0:T(8,128)(2,1)S(1)} %get-tuple-element.61), channel_id=1, source_target_pairs={{0,16},{16,0},{1,17},{17,1},{2,18},{18,2},{3,19},{19,3},{4,20},{20... | collective-permute-start | bytes 73736 | tf_op jit(solution)/shard_map/ppermute | solution.py:370
  57.9 9.3 %copy-start.6 = (bf16[96,128]{1,0:T(8,128)(2,1)}, bf16[96,128]{1,0:T(8,128)(2,1)S(1)}, u32[]{:S(2)}) copy-start(bf16[96,128]{1,0:T(8,128)(2,1)S(1)} %collective-permute-done.9.recv0) | copy-start | bytes 73732
  57.9 9.3 %copy-start.4 = (bf16[160,128]{1,0:T(8,128)(2,1)}, bf16[160,128]{1,0:T(8,128)(2,1)S(1)}, u32[]{:S(2)}) copy-start(bf16[160,128]{1,0:T(8,128)(2,1)S(1)} %collective-permute-done.10.recv3) | copy-start | bytes 122884
  57.9 9.3 %copy-start.2 = (bf16[2,96,128]{2,1,0:T(8,128)(2,1)}, bf16[2,96,128]{2,1,0:T(8,128)(2,1)S(1)}, u32[]{:S(2)}) copy-start(bf16[2,96,128]{2,1,0:T(8,128)(2,1)S(1)} %collective-permute-done.11.recv4) | copy-start | bytes 147460
  57.9 9.2 %copy-start.3 = (bf16[2,96,128]{2,1,0:T(8,128)(2,1)}, bf16[2,96,128]{2,1,0:T(8,128)(2,1)S(1)}, u32[]{:S(2)}) copy-start(bf16[2,96,128]{2,1,0:T(8,128)(2,1)S(1)} %collective-permute-done.12.recv5) | copy-start | bytes 147460
  61.4 13.4 %all-to-all-start.2 = ((bf16[16,64,128]{2,1,0:T(8,128)(2,1)}), bf16[16,64,128]{2,1,0:T(8,128)(2,1)S(1)}, u32[]{:S(2)}, u32[]{:S(2)}) async-start(bf16[16,64,128]{2,1,0:T(8,128)(2,1)} %shard_map.108), calls=%async_computation.2 | async-start | bytes 524288 | tf_op jit(solution)/shard_map/all_to_all | solution.py:380
  74.8 3.9 %collective-permute-start.13 = (bf16[1024,128]{1,0:T(8,128)(2,1)S(1)}, bf16[1024,128]{1,0:T(8,128)(2,1)S(1)}, u32[]{:S(2)}, u32[]{:S(2)}) collective-permute-start(bf16[1024,128]{1,0:T(8,128)(2,1)S(1)} %bitcast.4), channel_id=1, source_target_pairs={{0,16},{16,0},{1,17},{17,1},{2,18},{18,2},{3,19},{19,3},{4,20},{20... | collective-permute-start | bytes 786440 | tf_op jit(solution)/shard_map/ppermute | solution.py:448
